TPU v7x, 128 devices: a whole 4x4x4 slice. The times are simulated.
128 devices in a mesh: req: 32 (over x, z, core), head: 4 (over y).
Axes of the slice: x: 4, y: 4, z: 4, core: 2. Of those that a mesh axis runs over, the one named last changes fastest.
Arguments:
- prompt_query_latents: bfloat16 [16384, 1536], P(('req', 'head')), may hold values from -6 to 6
- prompt_latents: bfloat16 [16384, 512], P(('req', 'head')), may hold values from -320 to 320
- prompt_rotary_keys: bfloat16 [64, 16384], P(None, ('req', 'head')), may hold values from -6 to 6
- positions: int32 [16384], P(('req', 'head')), may hold values from 0 to 511, as said below
- query_up_weight: bfloat16 [1536, 12288], P(None, 'head'), may hold values from -0.15625 to 0.15625
- key_up_weight: bfloat16 [512, 8192], P(None, 'head'), may hold values from -0.25 to 0.25
- value_up_weight: bfloat16 [512, 8192], P(None, 'head'), may hold values from -0.25 to 0.25
- decode_queries: bfloat16 [2048, 12288], P('req', 'head'), may hold values from -6 to 6
- decode_owner_index: int32 [2048], P('req'), may hold values from 0 to 31, as said below
- decode_cache_slot: int32 [2048], P('req'), may hold values from 0 to 63, as said below
- latent_cache_rows: bfloat16 [2048, 256, 512], P('req'), may hold values from -320 to 320
- rotated_cache_keys: bfloat16 [2048, 64, 256], P('req'), may hold values from -6 to 6
- cache_live_lengths: int32 [2048], P('req'), may hold values from 1 to 256
Outputs:
- prompt_attention_output: bfloat16 [16384, 8192], P('req', 'head')
- decode_out: bfloat16 [2048, 8192], P('req', 'head')
Inputs may be any that keep to these rules, and one draw needn't show every extreme that they name: `positions`: a position is 0 where a prompt begins, always at the first token of a block and, from the second block on, at other tokens too, and otherwise one more than the previous token's; the first block holds one whole prompt. `decode_owner_index`: each entry device's 64 requests name 16 owners, each exactly 4 times; every pair of owner and slot is named by exactly one request. `decode_cache_slot`: see decode_owner_index.
All inputs are finite; a program needn't handle non-finite values.
Results may differ from a plain program's by a relative error of at most 0.012.
The roundings to bfloat16 on the way count: a program that leaves them out, or rounds other values in their place, can miss the bound.
Values may be sent and summed in bfloat16 or wider, within the bound.
No kernel may reach another device: no remote copies, remote signals or barrier semaphores. Data moves between devices by JAX's collectives and lax.ppermute only.
A program may use at most 192 MiB of HBM per device.

v0:
```python
import jax
import jax.numpy as jnp
from jax import lax
from jax.sharding import PartitionSpec as P

D_C = 512
D_NOPE = 128
D_ROPE = 64
D_V = 128


ROPE_BASE = 10000.0


def rotate(values, position):
    half_width = values.shape[-1] // 2
    frequency = ROPE_BASE ** (-jnp.arange(half_width, dtype=jnp.float32) / half_width)
    angles = position.astype(jnp.float32)[..., None] * frequency
    cosines = jnp.cos(angles)
    sine_term = jnp.sin(angles)
    first_half = values[..., :half_width]
    second_half = values[..., half_width:]
    return jnp.concatenate(
        [
            first_half * cosines - second_half * sine_term,
            first_half * sine_term + second_half * cosines,
        ],
        axis=-1,
    )


def prompt_prefill(
    prompt_query_latents,
    prompt_latents,
    prompt_rotary_keys,
    positions,
    query_up_weight,
    key_up_weight,
    value_up_weight,
):
    score_scale = (D_NOPE + D_ROPE) ** (-0.5)
    rows_query, rows_latent, rows_rope, rows_place = (
        lax.all_gather(prompt_query_latents, "head", axis=0, tiled=True),
        lax.all_gather(prompt_latents, "head", axis=0, tiled=True),
        lax.all_gather(prompt_rotary_keys, "head", axis=1, tiled=True),
        lax.all_gather(positions, "head", axis=0, tiled=True),
    )
    token_count = rows_query.shape[0]
    head_count = key_up_weight.shape[1] // D_NOPE
    queries = jnp.dot(rows_query, query_up_weight, preferred_element_type=jnp.float32).reshape(
        token_count, head_count, D_NOPE + D_ROPE
    )
    query_rope = rotate(queries[..., D_NOPE:], rows_place[:, None])
    queries = jnp.concatenate([queries[..., :D_NOPE], query_rope], axis=-1).astype(jnp.bfloat16)
    key_nope = (
        jnp.dot(rows_latent, key_up_weight, preferred_element_type=jnp.float32)
        .astype(jnp.bfloat16)
        .reshape(token_count, head_count, D_NOPE)
    )
    value_rows = (
        jnp.dot(rows_latent, value_up_weight, preferred_element_type=jnp.float32)
        .astype(jnp.bfloat16)
        .reshape(token_count, head_count, D_V)
    )
    key_rope = rotate(rows_rope.T.astype(jnp.float32), rows_place).astype(jnp.bfloat16)
    scores = (
        jnp.einsum(
            "shd,thd->hst", queries[..., :D_NOPE], key_nope, preferred_element_type=jnp.float32
        )
        + jnp.einsum(
            "shd,td->hst", queries[..., D_NOPE:], key_rope, preferred_element_type=jnp.float32
        )
    ) * score_scale
    token_index = jnp.arange(token_count, dtype=jnp.int32)
    visible = (token_index[None, :] <= token_index[:, None]) & (
        token_index[None, :] >= token_index[:, None] - rows_place[:, None]
    )
    scores = jnp.where(visible[None], scores, -jnp.inf)
    weights = jax.nn.softmax(scores, axis=-1).astype(jnp.bfloat16)
    attended = jnp.einsum(
        "hst,thd->shd", weights, value_rows, preferred_element_type=jnp.float32
    ).astype(jnp.bfloat16)
    return attended.reshape(token_count, head_count * D_V)


def attend(
    latent_query, query_rope, slot_ids, latent_cache_rows, rotated_cache_keys, cache_live_lengths
):
    score_scale = (D_NOPE + D_ROPE) ** (-0.5)
    safe_slots = jnp.clip(slot_ids, 0, latent_cache_rows.shape[0] - 1)
    latent = jnp.take(latent_cache_rows, safe_slots, axis=0)
    rope_rows = jnp.take(rotated_cache_keys, safe_slots, axis=0)
    length = jnp.take(cache_live_lengths, safe_slots, axis=0)
    scores = (
        jnp.einsum("nhc,ntc->nht", latent_query, latent, preferred_element_type=jnp.float32)
        + jnp.einsum("nhd,ndt->nht", query_rope, rope_rows, preferred_element_type=jnp.float32)
    ) * score_scale
    visible = jnp.arange(latent.shape[1], dtype=jnp.int32)[None, None, :] < length[:, None, None]
    scores = jnp.where(visible, scores, -jnp.inf)
    weights = jax.nn.softmax(scores, axis=-1).astype(jnp.bfloat16)
    return jnp.einsum("nht,ntc->nhc", weights, latent, preferred_element_type=jnp.float32).astype(
        jnp.bfloat16
    )


def absorb(query_nope, key_map):
    return jnp.einsum(
        "rhd,chd->rhc", query_nope, key_map, preferred_element_type=jnp.float32
    ).astype(jnp.bfloat16)


def decode(
    decode_queries,
    decode_owner_index,
    decode_cache_slot,
    latent_cache_rows,
    rotated_cache_keys,
    cache_live_lengths,
    key_up_weight,
    value_up_weight,
):
    row_count = decode_queries.shape[0]
    peer_count = lax.axis_size("req")
    slot_most = max(2, row_count * 2 // peer_count)
    head_count = key_up_weight.shape[1] // D_NOPE
    key_map = key_up_weight.reshape(D_C, head_count, D_NOPE)
    value_map = value_up_weight.reshape(D_C, head_count, D_V)
    row_index = jnp.arange(row_count, dtype=jnp.int32)
    earlier = (decode_owner_index[:, None] == decode_owner_index[None, :]) & (
        row_index[None, :] < row_index[:, None]
    )
    target = decode_owner_index * slot_most + jnp.sum(earlier.astype(jnp.int32), axis=1)
    placing = target[None, :] == jnp.arange(peer_count * slot_most, dtype=jnp.int32)[:, None]
    scatter_rows = placing.astype(jnp.bfloat16)
    slot_send = (
        jnp.sum(jnp.where(placing, decode_cache_slot[None, :] + 1, 0), axis=1) - 1
    ).reshape(peer_count, slot_most)
    queries = decode_queries.reshape(row_count, head_count, D_NOPE + D_ROPE)
    latent_query = absorb(queries[..., :D_NOPE], key_map)
    packed = jnp.concatenate([latent_query, queries[..., D_NOPE:]], axis=-1).reshape(
        row_count, head_count * (D_C + D_ROPE)
    )
    sending = (
        jnp.dot(scatter_rows, packed, preferred_element_type=jnp.float32)
        .astype(jnp.bfloat16)
        .reshape(peer_count, slot_most, head_count * (D_C + D_ROPE))
    )
    query_slots = lax.all_to_all(sending, "req", split_axis=0, concat_axis=0, tiled=True)
    slot_ids = lax.all_to_all(slot_send, "req", split_axis=0, concat_axis=0, tiled=True)
    item_count = slot_ids.shape[1]
    flattened = query_slots.reshape(peer_count * item_count, head_count, D_C + D_ROPE)
    latent_out = attend(
        flattened[..., :D_C],
        flattened[..., D_C:],
        slot_ids.reshape(-1),
        latent_cache_rows,
        rotated_cache_keys,
        cache_live_lengths,
    )
    returned = lax.all_to_all(
        latent_out.reshape(peer_count, item_count, head_count * D_C),
        "req",
        split_axis=0,
        concat_axis=0,
        tiled=True,
    )
    gathered = jnp.dot(
        scatter_rows.T,
        returned.reshape(peer_count * slot_most, head_count * D_C),
        preferred_element_type=jnp.float32,
    ).astype(jnp.bfloat16)
    result = jnp.einsum(
        "rhc,chd->rhd",
        gathered.reshape(row_count, head_count, D_C),
        value_map,
        preferred_element_type=jnp.float32,
    ).astype(jnp.bfloat16)
    result = result.reshape(row_count, head_count * D_V)
    return result


def on_device(
    prompt_query_latents,
    prompt_latents,
    prompt_rotary_keys,
    positions,
    query_up_weight,
    key_up_weight,
    value_up_weight,
    decode_queries,
    decode_owner_index,
    decode_cache_slot,
    latent_cache_rows,
    rotated_cache_keys,
    cache_live_lengths,
):
    prompt_attention_output = prompt_prefill(
        prompt_query_latents,
        prompt_latents,
        prompt_rotary_keys,
        positions,
        query_up_weight,
        key_up_weight,
        value_up_weight,
    )
    decode_out = decode(
        decode_queries,
        decode_owner_index,
        decode_cache_slot,
        latent_cache_rows,
        rotated_cache_keys,
        cache_live_lengths,
        key_up_weight,
        value_up_weight,
    )
    return (prompt_attention_output, decode_out)


def solution(mesh):
    placed = (
        P(("req", "head"), None),
        P(("req", "head"), None),
        P(None, ("req", "head")),
        P(("req", "head")),
        P(None, "head"),
        P(None, "head"),
        P(None, "head"),
        P("req", "head"),
        P("req"),
        P("req"),
        P("req", None, None),
        P("req", None, None),
        P("req"),
    )
    return jax.shard_map(
        on_device,
        mesh=mesh,
        in_specs=placed,
        out_specs=(P("req", "head"), P("req", "head")),
        check_vma=False,
    )
```

profile of v0, /device:TPU:1, one launch (start us, length us, event | category | flops | bytes accessed | tf_op | source)
XLA Modules:
  0.0 234.2 jit_solution(17933435202271265834)
XLA Ops:
  7.2 1.0 convert_reduce_fusion
  8.2 0.7 multiply_add_fusion
  8.9 0.5 copy-done.6
  9.4 0.1 select_reduce_fusion
  9.5 0.7 sub.38
  10.2 9.4 %all-to-all-start = ((s32[32,1,4]{2,1,0:T(1,128)}), s32[32,1,4]{2,1,0:T(1,128)S(1)}, u32[]{:S(2)}, u32[]{:S(2)}) async-start(s32[32,1,4]{2,1,0:T(1,128)} %bitcast.9), calls=%async_computation | async-start | bytes 32768 | tf_op jit(solution)/shard_map/all_to_all | solution.py:149
  19.7 0.7 all-gather.3.cloned.1.call-update
  20.4 1.6 reshape.249
  22.1 0.1 copy.85
  22.2 2.4 %fusion.28 = bf16[64,16,512]{2,0,1:T(8,128)(2,1)S(1)} fusion(bf16[64,16,128]{2,1,0:T(8,128)(2,1)S(1)} %slice.54, bf16[512,2048]{1,0:T(8,128)(2,1)} %param.18), kind=kOutput, calls=%fused_computation.39 | convolution fusion | flops 134742016 | bytes 3407872 | tf_op jit(solution)/shard_map/rhd,chd->rhc/dot_general | solution.py:107
  24.7 0.1 pad_maximum_fusion
  24.8 0.7 copy.75
  25.6 2.0 reshape.250
  27.5 12.7 %all_gather.12 = bf16[512,512]{1,0:T(8,128)(2,1)S(1)} all-gather(bf16[128,512]{1,0:T(8,128)(2,1)S(1)} %copy-done.4), channel_id=1, replica_groups=mesh['req'=32,'head'=4] {'head'}, dimensions={0}, use_global_device_ids=true | all-gather | bytes 655360 | tf_op jit(solution)/shard_map/all_gather | solution.py:44
  40.2 4.3 %convolution_convert_fusion.3 = bf16[512,2048]{1,0:T(8,128)(2,1)} fusion(bf16[512,512]{1,0:T(8,128)(2,1)S(1)} %all_gather.12, bf16[512,2048]{1,0:T(8,128)(2,1)} %param.19), kind=kOutput, calls=%fused_computation.21 | convolution fusion | flops 1074790400 | bytes 4718592 | tf_op jit(solution)/shard_map/dot_general | solution.py:61
  44.5 2.3 convolution_convert_fusion
  46.8 4.3 %reshape.251 = bf16[32,4,9216]{2,1,0:T(4,128)(2,1)} reshape(bf16[128,9216]{1,0:T(8,128)(2,1)} %convolution_convert_fusion) | data formatting | bytes 4718592 | tf_op jit(solution)/shard_map/reshape | solution.py:146
  51.1 9.6 %all-to-all-start.1 = ((bf16[32,4,9216]{2,1,0:T(4,128)(2,1)}), bf16[32,4,9216]{2,1,0:T(4,128)(2,1)}, u32[]{:S(2)}, u32[]{:S(2)}) async-start(bf16[32,4,9216]{2,1,0:T(4,128)(2,1)} %reshape.251), calls=%async_computation.1 | async-start | bytes 4718592 | tf_op jit(solution)/shard_map/all_to_all | solution.py:148
  60.7 8.6 %all-gather = s32[4,1,128]{2,1,0:T(1,128)S(1)} all-gather(s32[1,1,128]{2,1,0:T(1,128)S(1)} %bitcast.81), channel_id=1, replica_groups=mesh['req'=32,'head'=4] {'head'}, dimensions={0}, use_global_device_ids=true | all-gather | bytes 2560 | tf_op jit(solution)/shard_map/all_gather | solution.py:46
  69.3 3.9 %copy.83 = bf16[512,2048]{0,1:T(8,128)(2,1)} copy(bf16[512,2048]{1,0:T(8,128)(2,1)} %convolution_convert_fusion.3) | data formatting | bytes 4194304 | tf_op jit(solution)/shard_map/reshape | solution.py:63
  73.3 9.5 %all_gather.15 = bf16[64,512]{1,0:T(8,128)(2,1)S(1)} all-gather(bf16[64,128]{1,0:T(8,128)(2,1)S(1)} %copy-done.5), channel_id=1, replica_groups=mesh['req'=32,'head'=4] {'head'}, dimensions={1}, use_global_device_ids=true | all-gather | bytes 81920 | tf_op jit(solution)/shard_map/all_gather | solution.py:45
  82.8 0.1 fusion.44
  83.0 0.3 subtract_convert_fusion.1
  83.3 4.2 %fusion.24 = bf16[64,16,8,128]{3,2,1,0:T(8,128)(2,1)} fusion(bf16[512,512]{1,0:T(8,128)(2,1)S(1)} %all_gather.12, bf16[512,2048]{1,0:T(8,128)(2,1)} %param.18), kind=kOutput, calls=%fused_computation.37 | convolution fusion | flops 1074790400 | bytes 4718592 | tf_op jit(solution)/shard_map/dot_general | solution.py:56
  87.6 0.1 min.18
  87.7 0.1 min.16
  87.8 1.2 gather_fusion
  89.1 2.8 %gather_fusion.2 = bf16[128,64,256]{2,1,0:T(8,128)(2,1)} fusion(bf16[64,64,256]{2,1,0:T(8,128)(2,1)S(1)} %copy-done, s32[1024]{0:T(1024)S(1)} %pad_clamp_fusion), kind=kCustom, calls=%fused_computation.2 | custom fusion | bytes 8389120 | tf_op jit(solution)/shard_map/jit(_take)/gather | solution.py:92
  91.9 18.4 %gather_fusion.1 = bf16[128,256,512]{2,1,0:T(8,128)(2,1)} fusion(bf16[64,256,512]{2,1,0:T(8,128)(2,1)} %param.23, s32[1024]{0:T(1024)S(1)} %pad_clamp_fusion), kind=kCustom, calls=%fused_computation.1 | custom fusion | bytes 67109376 | tf_op jit(solution)/shard_map/jit(_take)/gather | solution.py:91
  110.4 0.1 iota_compare_fusion.2
  110.5 5.7 %reshape.252 = bf16[128,16,576]{2,1,0:T(8,128)(2,1)} reshape(bf16[32,4,9216]{2,1,0:T(4,128)(2,1)} %all-to-all-done.1) | data formatting | bytes 4718592 | tf_op jit(solution)/shard_map/reshape | solution.py:151
  116.2 3.2 %fusion.7 = f32[128,16,256]{2,1,0:T(8,128)S(1)} fusion(bf16[128,64,256]{2,1,0:T(8,128)(2,1)} %gather_fusion.2, pred[128]{0:T(512)(128)(4,1)S(1)} %get-tuple-element.13, bf16[128,16,576]{2,1,0:T(8,128)(2,1)} %reshape.252), kind=kOutput, calls=%fused_computation.17 | convolution fusion | flops 69206016 | bytes 6815872 | tf_op jit(solution)/shard_map/nhd,ndt->nht/dot_general | solution.py:96
  119.4 16.8 %fusion.60 = (f32[128,16]{1,0:T(8,128)S(1)}, f32[128,16,256]{2,1,0:T(8,128)}) fusion(f32[128,16,256]{2,1,0:T(8,128)S(1)} %fusion.7, bf16[128,256,512]{2,1,0:T(8,128)(2,1)} %gather_fusion.1, pred[128]{0:T(512)(128)(4,1)S(1)} %get-tuple-element.13, bf16[128,16,576]{2,1,0:T(8,128)(2,1)} %reshape.252, pred[128,256]{1,0:T(8,128)(4,1)S(1)} %iota_compare_fusion.2), kind=kOutput, calls=%fused_computation.93 | convolution fusion | flops 556269824 | bytes 39886976 | tf_op jit(solution)/shard_map/sub | solution.py:100
  136.2 13.9 %fusion.20 = bf16[128,16,512]{2,1,0:T(8,128)(2,1)S(1)} fusion(bf16[128,256,512]{2,1,0:T(8,128)(2,1)} %gather_fusion.1, pred[128]{0:T(512)(128)(4,1)S(1)} %get-tuple-element.13, f32[128,16,256]{2,1,0:T(8,128)} %get-tuple-element.23, f32[128,16]{1,0:T(8,128)S(1)} %get-tuple-element.22), kind=kOutput, calls=%fused_computation.35 | convolution fusion | flops 555745280 | bytes 37757056 | tf_op jit(solution)/shard_map/nht,ntc->nhc/dot_general | solution.py:101
  150.1 2.8 %reshape.253 = bf16[32,4,8192]{2,1,0:T(4,128)(2,1)} reshape(bf16[128,16,512]{2,1,0:T(8,128)(2,1)S(1)} %fusion.20) | data formatting | bytes 4194304 | tf_op jit(solution)/shard_map/reshape | solution.py:161
  152.8 9.7 %all-to-all-start.2 = ((bf16[32,4,8192]{2,1,0:T(4,128)(2,1)}), bf16[32,4,8192]{2,1,0:T(4,128)(2,1)S(1)}, u32[]{:S(2)}, u32[]{:S(2)}) async-start(bf16[32,4,8192]{2,1,0:T(4,128)(2,1)} %reshape.253), calls=%async_computation.2 | async-start | bytes 4194304 | tf_op jit(solution)/shard_map/all_to_all | solution.py:160
  162.6 8.3 %fusion.63 = f32[512,3072]{0,1:T(8,128)S(1)} fusion(bf16[512,1536]{1,0:T(8,128)(2,1)} %all-gather.3.cloned.1.call-done, bf16[1536,3072]{1,0:T(8,128)(2,1)} %param.17), kind=kOutput, calls=%fused_computation.94 | convolution fusion | flops 4831838208 | bytes 17301504 | tf_op jit(solution)/shard_map/dot_general | solution.py:50
  170.9 0.4 subtract_convert_fusion
  171.3 8.1 %fusion.39 = f32[512,512,16]{1,0,2:T(8,128)} fusion(bf16[512,16,32]{0,2,1:T(8,128)(2,1)S(1)} %get-tuple-element.15, bf16[512,16,32]{0,2,1:T(8,128)(2,1)S(1)} %get-tuple-element.14, bf16[512,32]{0,1:T(8,128)(2,1)S(1)} %get-tuple-element.17, bf16[512,32]{0,1:T(8,128)(2,1)S(1)} %get-tuple-element.16), kind=kOutput, calls=%fused_computation.45 | convolution fusion | flops 539099136 | bytes 17891328 | tf_op jit(solution)/shard_map/shd,td->hst/dot_general | solution.py:70
  179.4 11.5 %fusion.3 = f32[16,512,512]{1,2,0:T(8,128)} fusion(f32[512,512,16]{1,0,2:T(8,128)} %fusion.39, pred[512,512]{0,1:T(8,128)(4,1)S(1)} %fusion.44, f32[512,16,192]{0,2,1:T(8,128)S(1)} %bitcast.73, bf16[64,16,8,128]{3,2,1,0:T(8,128)(2,1)} %fusion.24), kind=kOutput, calls=%fused_computation.8 | convolution fusion | flops 1086324736 | bytes 38010880 | tf_op jit(solution)/shard_map/shd,thd->hst/dot_general | solution.py:67
  190.9 12.0 %fusion.59 = f32[16,512]{1,0:T(8,128)S(1)} fusion(f32[16,512,512]{1,2,0:T(8,128)} %fusion.3), kind=kOutput, calls=%fused_computation.92 | output fusion | flops 8389119 | bytes 16809984 | tf_op jit(solution)/shard_map/sub | solution.py:79
  202.9 14.7 %fusion.21 = bf16[16,128,512]{2,1,0:T(8,128)(2,1)} fusion(bf16[512,16,128]{0,2,1:T(8,128)(2,1)} %bitcast.74, f32[16,512]{1,0:T(8,128)S(1)} %fusion.59, f32[16,512,512]{1,2,0:T(8,128)} %fusion.3), kind=kOutput, calls=%fused_computation.36 | convolution fusion | flops 1087382016 | bytes 21004288 | tf_op jit(solution)/shard_map/hst,thd->shd/dot_general | solution.py:80
  217.6 3.9 %copy.79 = bf16[512,2048]{1,0:T(8,128)(2,1)} copy(bf16[512,2048]{0,1:T(8,128)(2,1)} %bitcast.75) | data formatting | bytes 4194304
  221.5 2.0 reshape.254
  223.6 2.2 convolution_convert_fusion.1
  225.8 0.6 fusion.34
  226.4 0.8 copy.118
  227.1 0.3 copy-done.1
  (34 shorter events, 0.3 us)
Async XLA Ops:
  7.2 81.9 %copy-start = (bf16[64,64,256]{2,1,0:T(8,128)(2,1)S(1)}, bf16[64,64,256]{2,1,0:T(8,128)(2,1)}, u32[]{:S(2)}) copy-start(bf16[64,64,256]{2,1,0:T(8,128)(2,1)} %param.24) | copy-start | bytes 6291460
  8.9 0.5 copy-start.6
  10.2 40.9 %all-to-all-start = ((s32[32,1,4]{2,1,0:T(1,128)}), s32[32,1,4]{2,1,0:T(1,128)S(1)}, u32[]{:S(2)}, u32[]{:S(2)}) async-start(s32[32,1,4]{2,1,0:T(1,128)} %bitcast.9), calls=%async_computation | async-start | bytes 32768 | tf_op jit(solution)/shard_map/all_to_all | solution.py:149
  19.7 142.9 %all-gather.3.cloned.1.call-start = ((), (), s32[]{:S(2)}) async-start(), calls=%async_computation.3 | async-start | bytes 1966080 | tf_op jit(solution)/shard_map/all_gather | solution.py:43
  24.8 2.7 %copy-start.4 = (bf16[128,512]{1,0:T(8,128)(2,1)S(1)}, bf16[128,512]{1,0:T(8,128)(2,1)}, u32[]{:S(2)}) copy-start(bf16[128,512]{1,0:T(8,128)(2,1)} %param.14) | copy-start | bytes 393220
  40.2 4.3 %copy-start.3 = (bf16[64,9216]{1,0:T(8,128)(2,1)S(1)}, bf16[64,9216]{1,0:T(8,128)(2,1)}, u32[]{:S(2)}) copy-start(bf16[64,9216]{1,0:T(8,128)(2,1)} %reshape.250) | copy-start | bytes 3538948
  40.2 4.3 %copy-start.7 = (s32[64]{0:T(128)S(1)}, s32[64]{0:T(128)}, u32[]{:S(2)}) copy-start(s32[64]{0:T(128)} %copy-done.6) | copy-start | bytes 772
  51.1 9.6 %copy-start.8 = (s32[128]{0:T(128)S(1)}, s32[128]{0:T(128)}, u32[]{:S(2)}) copy-start(s32[128]{0:T(128)} %param.16) | copy-start | bytes 1540
  51.1 59.4 %all-to-all-start.1 = ((bf16[32,4,9216]{2,1,0:T(4,128)(2,1)}), bf16[32,4,9216]{2,1,0:T(4,128)(2,1)}, u32[]{:S(2)}, u32[]{:S(2)}) async-start(bf16[32,4,9216]{2,1,0:T(4,128)(2,1)} %reshape.251), calls=%async_computation.1 | async-start | bytes 4718592 | tf_op jit(solution)/shard_map/all_to_all | solution.py:148
  69.3 3.9 %copy-start.5 = (bf16[64,128]{1,0:T(8,128)(2,1)S(1)}, bf16[64,128]{1,0:T(8,128)(2,1)}, u32[]{:S(2)}) copy-start(bf16[64,128]{1,0:T(8,128)(2,1)} %param.15) | copy-start | bytes 49156
  83.3 4.5 %copy-start.2 = (s32[64]{0:T(128)S(1)}, s32[64]{0:T(128)}, u32[]{:S(2)}) copy-start(s32[64]{0:T(128)} %param.25) | copy-start | bytes 772
  152.8 68.7 %all-to-all-start.2 = ((bf16[32,4,8192]{2,1,0:T(4,128)(2,1)}), bf16[32,4,8192]{2,1,0:T(4,128)(2,1)S(1)}, u32[]{:S(2)}, u32[]{:S(2)}) async-start(bf16[32,4,8192]{2,1,0:T(4,128)(2,1)} %reshape.253), calls=%async_computation.2 | async-start | bytes 4194304 | tf_op jit(solution)/shard_map/all_to_all | solution.py:160
  223.6 2.2 copy-start.9
  225.8 1.6 copy-start.1
Sparse Core Ops, SparseCore 0:
  22.2 29.8 all-gather.2
where the time goes:
time: 235 us; the launch traced here: 234 us
  matrix products  92.6 us (39%)
  local copies, waits for them, and re-layouts  52.2 us (22%)
  blocking collectives  30.8 us (13%)
  starting transfers between devices  28.8 us (12%)
  other arithmetic  14.9 us (6%)
  between operations  14.3 us (6%)
    gather x1, local copies, waits for them, and re-layouts, attend(): latent = jnp.take(latent_cache_rows, safe_slots, axis=0)  18.4 us
    sub x1, matrix products, attend(): weights = jax.nn.softmax(scores, axis=-1).astype(jnp.bfloat16)  16.8 us
    dot_general x1, matrix products, prompt_prefill(): jnp.einsum('hst,thd->shd', weights, value_rows, preferred_element_type=jn...  14.7 us
    dot_general x1, matrix products, attend(): jnp.einsum('nht,ntc->nhc', weights, latent, preferred_element_type=jnp.fl...  13.9 us
    all_gather x1, blocking collectives, prompt_prefill(): lax.all_gather(prompt_latents, 'head', axis=0, tiled=True)  12.7 us
    sub x1, other arithmetic, prompt_prefill(): weights = jax.nn.softmax(scores, axis=-1).astype(jnp.bfloat16)  12 us
    dot_general x1, matrix products, prompt_prefill(): jnp.einsum('shd,thd->hst', queries[..., :D_NOPE], key_nope, preferred_ele...  11.5 us
    all_to_all x1, starting transfers between devices, decode(): lax.all_to_all(latent_out.reshape(peer_count, item_count, head_count * D_...  9.7 us
  transfers between devices with their start and end apart: 4, of which 0 were waited for; matrix products, arithmetic and copies ran while one was open for 64% of the time, Pallas kernels for 0%

commit v1 on v0

v1 whole, which is shorter than its diff:
```python
import functools
import math

import jax
import jax.numpy as jnp
import numpy as np
from jax import lax
from jax.experimental import pallas as pl
from jax.experimental.pallas import tpu as pltpu
from jax.sharding import PartitionSpec as P

D_C = 512
D_NOPE = 128
D_ROPE = 64
D_V = 128
D_Q = 1536
HEADS = 16
TOKENS = 512
CHUNK = 128
ROWS = 64
MOST = 4
SLOTS = 64
CMAX = 256
PEERS = 32
PACK = D_Q + D_C + 128
SEND = 1536 + 128
RET = 1024
ROPE_BASE = 10000.0
SCALE = (D_NOPE + D_ROPE) ** -0.5
SCALE_LOG2 = SCALE * math.log2(math.e)
MASKED = -1e30
F32 = jnp.float32
BF16 = jnp.bfloat16
MIB = 1024 * 1024


def iota(shape, dim):
    return lax.broadcasted_iota(jnp.int32, shape, dim)


def dot(a, b, dims=((1,), (0,))):
    return lax.dot_general(a, b, (dims, ((), ())), preferred_element_type=F32)


def column_of(row):
    n = row.shape[1]
    eye = iota((n, n), 0) == iota((n, n), 1)
    return jnp.sum(jnp.where(eye, row, 0), axis=1, keepdims=True)


def pack_kernel(x_ref, l_ref, rk_ref, pos_ref, freq_ref, q_ref, owner_ref, slot_ref, packed_ref, send_ref):
    packed_ref[:, :D_Q] = x_ref[...]
    packed_ref[:, D_Q:D_Q + D_C] = l_ref[...]
    pos = pos_ref[...]
    angle = pos.astype(F32) * freq_ref[...]
    cos, sin = jnp.cos(angle), jnp.sin(angle)
    keys = rk_ref[...].astype(F32)
    first, second = keys[:32], keys[32:]
    high = (pos >> 4).astype(F32)
    low = (pos & 15).astype(F32)
    place = iota((64, CHUNK), 0)
    tail = jnp.where(place == 0, high, jnp.where(place == 1, low, 0.0))
    block = jnp.concatenate([first * cos - second * sin, first * sin + second * cos, tail], axis=0)
    packed_ref[:, D_Q + D_C:] = block.T.astype(BF16)

    owner = owner_ref[...]
    owner_col = column_of(owner)
    same = owner_col == owner
    before = iota((ROWS, ROWS), 0) < iota((ROWS, ROWS), 1)
    rank = jnp.sum(jnp.where(same & before, 1, 0), axis=0, keepdims=True)
    target = owner * (2 * MOST) + rank
    target = jnp.concatenate([target, target + MOST], axis=1)
    placing = iota((PEERS * 2 * MOST, 2 * ROWS), 0) == target
    queries = jnp.concatenate([q_ref[:, :1536], q_ref[:, 1536:]], axis=0)
    send_ref[:, :1536] = dot(placing.astype(BF16), queries).astype(BF16)
    slot = slot_ref[...] + 1
    slot = jnp.concatenate([slot, slot], axis=1)
    slot_col = jnp.sum(jnp.where(placing, slot, 0), axis=1, keepdims=True)
    send_ref[:, 1536:] = jnp.broadcast_to(slot_col.astype(F32), (PEERS * 2 * MOST, 128)).astype(BF16)


def split_pair(three):
    low_lane = iota((three.shape[0], 128), 1) < 64
    second, third = three[:, 128:256], three[:, 256:]
    rotary = jnp.where(low_lane, second, third)
    odd = pltpu.roll(jnp.where(low_lane, third, second), 64, 1)
    return three[:, :128], odd, rotary


SLOTS_PER_STEP = 8


def decode_kernel(recv_ref, kup_ref, vup_ref, lat_ref, rk_ref, len_ref, out_ref, lq_ref, qr_ref, lo_ref):
    step = pl.program_id(0)
    rows = PEERS * 2 * MOST

    def slot_onehot():
        slot_col = recv_ref[:, 1536:].astype(jnp.int32)
        lane = iota((rows, 128), 1)
        hit = slot_col == lane + 1
        half = (iota((rows, 128), 0) & 7) < MOST
        return hit & half, hit & jnp.logical_not(half)

    @pl.when(step == 0)
    def _():
        first, second = slot_onehot()
        for side, hit in enumerate((first, second)):
            spread = jnp.where(hit, 1.0, 0.0).T[:SLOTS].astype(BF16)
            queries = dot(spread, recv_ref[:, :1536])
            for pair in range(4):
                even, odd, rotary = split_pair(queries[:, pair * 384:(pair + 1) * 384])
                for sub, nope in enumerate((even, odd)):
                    head = side * 8 + pair * 2 + sub
                    latent = dot(nope.astype(BF16), kup_ref[:, head * 128:(head + 1) * 128], ((1,), (1,)))
                    latent = latent.astype(BF16).astype(F32)
                    for part in range(4):
                        lq_ref[part, head * SLOTS:(head + 1) * SLOTS, :] = latent[:, part * 128:(part + 1) * 128]
                    qr_ref[head * SLOTS:(head + 1) * SLOTS, :] = rotary if sub == 0 else pltpu.roll(rotary, 64, 1)

    scores = []
    for i in range(SLOTS_PER_STEP):
        slot = step * SLOTS_PER_STEP + i
        latent = jnp.concatenate(
            [lq_ref[part, pl.ds(slot, HEADS, stride=SLOTS), :].astype(BF16) for part in range(4)], axis=1)
        rotary = qr_ref[pl.ds(slot, HEADS, stride=SLOTS), :].astype(BF16)
        score = dot(latent, lat_ref[i], ((1,), (1,))) + dot(rotary[:, :D_ROPE], rk_ref[i])
        score = jnp.where(iota((HEADS, CMAX), 1) < len_ref[slot], score * SCALE, MASKED)
        scores.append(score)
    weights = []
    for i in range(SLOTS_PER_STEP):
        score = scores[i]
        raised = jnp.exp(score - jnp.max(score, axis=1, keepdims=True))
        weights.append((raised / jnp.sum(raised, axis=1, keepdims=True)).astype(BF16))
    for i in range(SLOTS_PER_STEP):
        slot = step * SLOTS_PER_STEP + i
        latent_out = dot(weights[i], lat_ref[i])
        latent_out = latent_out.astype(BF16).astype(F32)
        for part in range(4):
            lo_ref[part, pl.ds(slot, HEADS, stride=SLOTS), :] = latent_out[:, part * 128:(part + 1) * 128]

    @pl.when(step == pl.num_programs(0) - 1)
    def _():
        outs = []
        for head in range(HEADS):
            latent_out = jnp.concatenate(
                [lo_ref[part, head * SLOTS:(head + 1) * SLOTS, :].astype(BF16) for part in range(4)], axis=1)
            outs.append(dot(latent_out, vup_ref[:, head * 128:(head + 1) * 128]).astype(BF16))
        outs = jnp.concatenate([jnp.concatenate(outs[:8], axis=1), jnp.concatenate(outs[8:], axis=1)], axis=0)
        first, second = slot_onehot()
        spread = jnp.concatenate([jnp.where(first, 1.0, 0.0)[:, :SLOTS], jnp.where(second, 1.0, 0.0)[:, :SLOTS]], axis=1)
        out_ref[...] = dot(spread.astype(BF16), outs).astype(BF16)


def unplace_kernel(ret_ref, owner_ref, out_ref):
    owner = owner_ref[...]
    owner_col = column_of(owner)
    before = iota((ROWS, ROWS), 1) < iota((ROWS, ROWS), 0)
    rank = jnp.sum(jnp.where((owner_col == owner) & before, 1, 0), axis=1, keepdims=True)
    target = owner_col * (2 * MOST) + rank
    lane = iota((ROWS, PEERS * 2 * MOST), 1)
    for side in range(2):
        spread = jnp.where(lane == target + side * MOST, 1.0, 0.0).astype(BF16)
        out_ref[:, side * RET:(side + 1) * RET] = dot(spread, ret_ref[...]).astype(BF16)


GROUP = 4


def project_kernel(head_ref, own_ref, left_ref, right_ref, top_ref, bottom_ref, freq_ref, wq_ref, wk_ref, wv_ref,
                   qn_ref, qr_ref, k_ref, v_ref, kr_ref, x_ref, cos_ref, sin_ref):
    @pl.when(pl.program_id(0) == 0)
    def _():
        me = head_ref[0]
        x_ref[me] = own_ref[...]
        x_ref[(me + 3) & 3] = left_ref[...]
        x_ref[(me + 1) & 3] = right_ref[...]
        x_ref[(me + 2) & 3, :64] = top_ref[...]
        x_ref[(me + 2) & 3, 64:] = bottom_ref[...]
        extra = x_ref[:, :, D_Q + D_C:].reshape(TOKENS, 128)
        kr_ref[...] = extra
        turned = extra.astype(F32).T
        pos = turned[64:65] * 16.0 + turned[65:66]
        angle = pos * freq_ref[...]
        cos, sin = jnp.cos(angle), jnp.sin(angle)
        cos_ref[...] = jnp.concatenate([cos, cos, cos, cos], axis=0).T
        sin_ref[...] = jnp.concatenate([-sin, sin, -sin, sin], axis=0).T

    half = TOKENS // 2
    lane = iota((half, 128), 1) & 63
    for part in range(2):
        rows = slice(part * half, (part + 1) * half)
        x = x_ref[2 * part:2 * part + 2, :, :].reshape(half, PACK)
        queries = dot(x[:, :D_Q], wq_ref[...])
        cos, sin = cos_ref[rows, :], sin_ref[rows, :]
        for pair in range(GROUP // 2):
            even, odd, rotary = split_pair(queries[:, pair * 384:(pair + 1) * 384])
            qn_ref[rows, pair * 256:pair * 256 + 128] = even.astype(BF16)
            qn_ref[rows, pair * 256 + 128:pair * 256 + 256] = odd.astype(BF16)
            swapped = jnp.where(lane < 32, pltpu.roll(rotary, 96, 1), pltpu.roll(rotary, 32, 1))
            qr_ref[rows, pair * 128:(pair + 1) * 128] = (rotary * cos + swapped * sin).astype(BF16)
        latents = x[:, D_Q:D_Q + D_C]
        k_ref[rows, :] = dot(latents, wk_ref[...]).astype(BF16)
        v_ref[rows, :] = dot(latents, wv_ref[...]).astype(BF16)


def attention_kernel(qn_ref, qr_ref, k_ref, v_ref, kr_ref, out_ref, bias_ref, key_ref, value_ref):
    half = TOKENS // 2

    @pl.when(pl.program_id(0) == 0)
    def _():
        extra = kr_ref[...].astype(F32)
        pos = (extra[:, 64:65] * 16.0 + extra[:, 65:66]).astype(jnp.int32)
        query, key = iota((TOKENS, TOKENS), 0), iota((TOKENS, TOKENS), 1)
        bias_ref[...] = jnp.where((key <= query) & (key >= query - pos), 0.0, MASKED)
        low_lane = iota((TOKENS, 128), 1) < 64
        keep = jnp.where(low_lane, extra, 0.0)
        key_ref[0, :, 128:] = keep.astype(BF16)
        key_ref[1, :, 128:] = pltpu.roll(keep, 64, 1).astype(BF16)
        value_ref[:, :, 128:] = jnp.ones((2, TOKENS, 128), BF16)

    for sub in range(2):
        lanes = slice(sub * 128, (sub + 1) * 128)
        key_ref[sub, :, :128] = k_ref[:, lanes]
        value_ref[sub, :, :128] = v_ref[:, lanes]
    for sub in range(2):
        lanes = slice(sub * 128, (sub + 1) * 128)
        for part in range(2):
            rows = slice(part * half, (part + 1) * half)
            seen = (part + 1) * half
            query = jnp.concatenate([qn_ref[rows, lanes], qr_ref[rows, :]], axis=1)
            score = dot(query, key_ref[sub, :seen, :], ((1,), (1,))) + bias_ref[rows, :seen]
            top = jnp.max(score, axis=1, keepdims=True)
            raised = jnp.exp2((score - top) * SCALE_LOG2).astype(BF16)
            total = dot(raised, value_ref[sub, :seen, :])
            out_ref[rows, lanes] = (total[:, :128] / total[:, 128:]).astype(BF16)


def whole(shape):
    return pl.BlockSpec(shape, lambda *_: (0,) * len(shape))


def params(mib):
    return pltpu.CompilerParams(vmem_limit_bytes=mib * MIB)


def smem():
    return pl.BlockSpec(memory_space=pltpu.SMEM)


def on_device(x, latents, rotary_keys, positions, wq, wk, wv, queries, owner, slot, cache, cache_rope, lengths):
    me = lax.axis_index("head").astype(jnp.int32).reshape(1)
    freq = jnp.asarray(ROPE_BASE ** (-np.arange(32) / 32.0), F32).reshape(32, 1)
    owner_row, slot_row = owner.reshape(1, ROWS), slot.reshape(1, ROWS)
    packed, send = pl.pallas_call(
        pack_kernel,
        out_shape=(
            jax.ShapeDtypeStruct((CHUNK, PACK), BF16),
            jax.ShapeDtypeStruct((PEERS * 2 * MOST, SEND), BF16),
        ),
        compiler_params=params(24),
        name="pack",
    )(x, latents, rotary_keys, positions.reshape(1, CHUNK), freq, queries, owner_row, slot_row)

    up = [(i, (i + 1) % 4) for i in range(4)]
    down = [(i, (i + 3) % 4) for i in range(4)]
    left = lax.ppermute(packed, "head", up)
    right = lax.ppermute(packed, "head", down)
    recv = lax.all_to_all(send, "req", 0, 0, tiled=True)
    top = lax.ppermute(left[:64], "head", up)
    bottom = lax.ppermute(right[64:], "head", down)

    returned = pl.pallas_call(
        decode_kernel,
        grid=(SLOTS // SLOTS_PER_STEP,),
        in_specs=[
            whole((PEERS * 2 * MOST, SEND)),
            whole((D_C, HEADS * D_NOPE)),
            whole((D_C, HEADS * D_V)),
            pl.BlockSpec((SLOTS_PER_STEP, CMAX, D_C), lambda i: (i, 0, 0)),
            pl.BlockSpec((SLOTS_PER_STEP, D_ROPE, CMAX), lambda i: (i, 0, 0)),
            smem(),
        ],
        out_specs=whole((PEERS * 2 * MOST, RET)),
        out_shape=jax.ShapeDtypeStruct((PEERS * 2 * MOST, RET), BF16),
        scratch_shapes=[
            pltpu.VMEM((4, HEADS * SLOTS, 128), F32),
            pltpu.VMEM((HEADS * SLOTS, 128), F32),
            pltpu.VMEM((4, HEADS * SLOTS, 128), F32),
        ],
        compiler_params=params(40),
        name="decode",
    )(recv, wk, wv, cache, cache_rope, lengths)
    returned = lax.all_to_all(returned, "req", 0, 0, tiled=True)

    steps = HEADS // GROUP
    qn, qr, keys, values, key_rope = pl.pallas_call(
        project_kernel,
        grid=(steps,),
        in_specs=[
            smem(),
            whole((CHUNK, PACK)),
            whole((CHUNK, PACK)),
            whole((CHUNK, PACK)),
            whole((64, PACK)),
            whole((64, PACK)),
            whole((32, 1)),
            pl.BlockSpec((D_Q, GROUP * 192), lambda i: (0, i)),
            pl.BlockSpec((D_C, GROUP * 128), lambda i: (0, i)),
            pl.BlockSpec((D_C, GROUP * 128), lambda i: (0, i)),
        ],
        out_specs=(
            pl.BlockSpec((TOKENS, GROUP * 128), lambda i: (0, i)),
            pl.BlockSpec((TOKENS, GROUP * 64), lambda i: (0, i)),
            pl.BlockSpec((TOKENS, GROUP * 128), lambda i: (0, i)),
            pl.BlockSpec((TOKENS, GROUP * 128), lambda i: (0, i)),
            whole((TOKENS, 128)),
        ),
        out_shape=(
            jax.ShapeDtypeStruct((TOKENS, HEADS * 128), BF16),
            jax.ShapeDtypeStruct((TOKENS, HEADS * 64), BF16),
            jax.ShapeDtypeStruct((TOKENS, HEADS * 128), BF16),
            jax.ShapeDtypeStruct((TOKENS, HEADS * 128), BF16),
            jax.ShapeDtypeStruct((TOKENS, 128), BF16),
        ),
        scratch_shapes=[
            pltpu.VMEM((4, CHUNK, PACK), BF16),
            pltpu.VMEM((TOKENS, 128), F32),
            pltpu.VMEM((TOKENS, 128), F32),
        ],
        compiler_params=params(40),
        name="project",
    )(me, packed, left, right, top, bottom, freq, wq, wk, wv)

    prompt_out = pl.pallas_call(
        attention_kernel,
        grid=(HEADS // 2,),
        in_specs=[
            pl.BlockSpec((TOKENS, 256), lambda i: (0, i)),
            pl.BlockSpec((TOKENS, 128), lambda i: (0, i)),
            pl.BlockSpec((TOKENS, 256), lambda i: (0, i)),
            pl.BlockSpec((TOKENS, 256), lambda i: (0, i)),
            whole((TOKENS, 128)),
        ],
        out_specs=pl.BlockSpec((TOKENS, 256), lambda i: (0, i)),
        out_shape=jax.ShapeDtypeStruct((TOKENS, HEADS * D_V), BF16),
        scratch_shapes=[
            pltpu.VMEM((TOKENS, TOKENS), F32),
            pltpu.VMEM((2, TOKENS, 256), BF16),
            pltpu.VMEM((2, TOKENS, 256), BF16),
        ],
        compiler_params=params(32),
        name="attention",
    )(qn, qr, keys, values, key_rope)

    decode_out = pl.pallas_call(
        unplace_kernel,
        out_shape=jax.ShapeDtypeStruct((ROWS, HEADS * D_V), BF16),
        compiler_params=params(16),
        name="unplace",
    )(returned, owner_row)
    return prompt_out, decode_out


def solution(mesh):
    placed = (
        P(("req", "head"), None),
        P(("req", "head"), None),
        P(None, ("req", "head")),
        P(("req", "head")),
        P(None, "head"),
        P(None, "head"),
        P(None, "head"),
        P("req", "head"),
        P("req"),
        P("req"),
        P("req", None, None),
        P("req", None, None),
        P("req"),
    )
    return jax.shard_map(
        on_device,
        mesh=mesh,
        in_specs=placed,
        out_specs=(P("req", "head"), P("req", "head")),
        check_vma=False,
    )
```

time: 235 us -> 98.2 us (0.42)
  matrix products: 92.6 us -> 0 us
  Pallas kernels: 0 us -> 39.9 us
  local copies, waits for them, and re-layouts: 52.2 us -> 16.4 us
  blocking collectives: 30.8 us -> 0 us
  waiting for transfers between devices: 0.71 us -> 21.3 us
  other arithmetic: 14.9 us -> 0 us
  between operations: 14.3 us -> 0.72 us
  starting transfers between devices: 28.8 us -> 19 us
    dot_general x12 -> x0, matrix products: 75.7 us -> none  [the longest x1 14.7 us: prompt_prefill(): jnp.einsum('hst,thd->shd', weights, value_rows, preferred_element_type=jn...]
    pallas_call x0 -> x5, Pallas kernels: none -> 39.9 us  [the longest x1 15.4 us: on_device(): pl.pallas_call(decode_kernel, grid=(SLOTS // SLOTS_PER_STEP,), in_specs=[...]
    all_gather x3 -> x0, blocking collectives: 30.8 us -> none  [the longest x1 12.7 us: prompt_prefill(): lax.all_gather(prompt_latents, 'head', axis=0, tiled=True)]
    reshape x8 -> x0, local copies, waits for them, and re-layouts: 23.1 us -> none  [the longest x1 5.71 us: decode(): query_slots.reshape(peer_count * item_count, head_count, D_C + D_ROPE)]
    gather x3 -> x0, local copies, waits for them, and re-layouts: 22.5 us -> none  [the longest x1 18.4 us: attend(): latent = jnp.take(latent_cache_rows, safe_slots, axis=0)]
    sub x1 -> x0, matrix products: 16.8 us -> none  [attend(): weights = jax.nn.softmax(scores, axis=-1).astype(jnp.bfloat16)]
    all_to_all x3 -> x2, starting transfers between devices: 28.7 us -> 13.5 us  [the longest x1 9.44 us: on_device(): recv = lax.all_to_all(send, 'req', 0, 0, tiled=True)]
    all_to_all x3 -> x2, waiting for transfers between devices: 0.01 us -> 12.1 us  [the longest x1 12 us: on_device(): recv = lax.all_to_all(send, 'req', 0, 0, tiled=True)]
  transfers between devices with their start and end apart: 4 -> 6, of which waited for: 0 -> 3; matrix products, arithmetic and copies ran while one was open for 64% -> 2% of each run, Pallas kernels for 0% -> 39%
where the time goes in v1:
time: 98.2 us; the launch traced here: 97.4 us
  Pallas kernels  39.9 us (41%)
  waiting for transfers between devices  21.3 us (22%)
  starting transfers between devices  19 us (19%)
  local copies, waits for them, and re-layouts  16.4 us (17%)
    pallas_call x1, Pallas kernels, on_device(): pl.pallas_call(decode_kernel, grid=(SLOTS // SLOTS_PER_STEP,), in_specs=[...  15.4 us
    unnamed x36, local copies, waits for them, and re-layouts  14 us
    all_to_all x1, waiting for transfers between devices, on_device(): recv = lax.all_to_all(send, 'req', 0, 0, tiled=True)  12 us
    pallas_call x1, Pallas kernels, on_device(): pl.pallas_call(attention_kernel, grid=(HEADS // 2,), in_specs=[pl.BlockSp...  11.7 us
    pallas_call x1, Pallas kernels, on_device(): pl.pallas_call(project_kernel, grid=(steps,), in_specs=[smem(), whole((CH...  11.1 us
    all_to_all x1, starting transfers between devices, on_device(): recv = lax.all_to_all(send, 'req', 0, 0, tiled=True)  9.44 us
    ppermute x1, waiting for transfers between devices, on_device(): top = lax.ppermute(left[:64], 'head', up)  4.78 us
    ppermute x1, waiting for transfers between devices, on_device(): bottom = lax.ppermute(right[64:], 'head', down)  4.45 us
  transfers between devices with their start and end apart: 6, of which 3 were waited for; matrix products, arithmetic and copies ran while one was open for 2% of the time, Pallas kernels for 39%

profile of v1, /device:TPU:1, one launch (start us, length us, event | category | flops | bytes accessed | tf_op | source)
XLA Modules:
  0.0 97.4 jit_solution(2301906387007977341)
XLA Ops:
  0.6 0.0 copy-start
  0.6 0.0 copy-start.7
  0.7 1.1 %copy-done.7 = bf16[128,1536]{1,0:T(8,128)(2,1)S(1)} copy-done((bf16[128,1536]{1,0:T(8,128)(2,1)S(1)}, bf16[128,1536]{1,0:T(8,128)(2,1)}, u32[]{:S(2)}) %copy-start.7) | copy-done | bytes 393240
  1.8 0.0 copy-start.8
  1.8 1.0 %copy-done.8 = bf16[64,3072]{1,0:T(8,128)(2,1)S(1)} copy-done((bf16[64,3072]{1,0:T(8,128)(2,1)S(1)}, bf16[64,3072]{1,0:T(8,128)(2,1)}, u32[]{:S(2)}) %copy-start.8) | copy-done | bytes 393240
  2.8 0.0 copy-start.9
  2.8 0.9 copy-done.9
  3.7 0.0 copy-start.10
  3.7 0.7 copy-done.10
  4.4 0.0 copy-start.12
  4.4 0.7 copy-done.12
  5.1 0.0 copy-start.13
  5.1 0.7 copy-done.13
  5.8 0.0 copy-start.15
  5.8 0.7 copy-done.15
  6.4 0.0 copy-start.16
  6.4 0.7 copy-done.16
  7.1 0.5 pack.1
  7.6 0.0 copy-start.5
  7.6 0.8 copy-done.5
  8.5 0.9 copy-done.4
  9.4 9.4 %all-to-all-start = ((bf16[32,8,1664]{2,1,0:T(8,128)(2,1)}), bf16[32,8,1664]{2,1,0:T(8,128)(2,1)S(1)}, u32[]{:S(2)}, u32[]{:S(2)}) async-start(bf16[32,8,1664]{2,1,0:T(8,128)(2,1)} %bitcast.10), calls=%async_computation | async-start | bytes 1703936 | tf_op jit(solution)/shard_map/all_to_all | solution.py:268
  18.8 2.8 %collective-permute-start.1 = (bf16[128,2176]{1,0:T(8,128)(2,1)}, bf16[128,2176]{1,0:T(8,128)(2,1)S(1)}, u32[]{:S(2)}, u32[]{:S(2)}) collective-permute-start(bf16[128,2176]{1,0:T(8,128)(2,1)} %copy-done.5), channel_id=1, source_target_pairs={{0,3},{1,0},{2,1},{3,2},{4,7},{5,4},{6,5},{7,6},{8,11},{9,8},{10,9... | collective-permute-start | bytes 1671176 | tf_op jit(solution)/shard_map/ppermute | solution.py:267
  21.6 0.0 collective-permute-start
  21.6 12.0 %all-to-all-done = bf16[32,8,1664]{2,1,0:T(8,128)(2,1)S(1)} async-done(((bf16[32,8,1664]{2,1,0:T(8,128)(2,1)}), bf16[32,8,1664]{2,1,0:T(8,128)(2,1)S(1)}, u32[]{:S(2)}, u32[]{:S(2)}) %all-to-all-start) | async-done | bytes 852000 | tf_op jit(solution)/shard_map/all_to_all | solution.py:268
  33.7 0.0 copy-done
  33.7 0.0 copy-done.17
  33.7 1.6 %copy-done.1 = bf16[512,2048]{1,0:T(8,128)(2,1)S(1)} copy-done((bf16[512,2048]{1,0:T(8,128)(2,1)S(1)}, bf16[512,2048]{1,0:T(8,128)(2,1)}, u32[]{:S(2)}) %copy-start.1) | copy-done | bytes 2097176
  35.3 1.6 %copy-done.3 = bf16[64,64,256]{2,1,0:T(8,128)(2,1)S(1)} copy-done((bf16[64,64,256]{2,1,0:T(8,128)(2,1)S(1)}, bf16[64,64,256]{2,1,0:T(8,128)(2,1)}, u32[]{:S(2)}) %copy-start.3) | copy-done | bytes 2097176
  36.9 15.4 %decode.1 = bf16[256,1024]{1,0:T(8,128)(2,1)} custom-call(bf16[256,1664]{1,0:T(8,128)(2,1)S(1)} %bitcast.8, bf16[512,2048]{1,0:T(8,128)(2,1)S(1)} %copy-done, bf16[512,2048]{1,0:T(8,128)(2,1)S(1)} %copy-done.1, bf16[64,256,512]{2,1,0:T(8,128)(2,1)} %lat_ref.1, bf16[64,64,256]{2,1,0:T(8,128)(2,1)S(1)} %copy-done.3, s32[64]{0:T(128)S(1)} %copy-done.17), custom_call_target="tpu_custom_call" | custom-call | tf_op jit(solution)/shard_map/decode/pallas_call | solution.py:272
  52.3 4.0 %all-to-all-start.1 = ((bf16[32,8,1024]{2,1,0:T(8,128)(2,1)}), bf16[32,8,1024]{2,1,0:T(8,128)(2,1)S(1)}, u32[]{:S(2)}, u32[]{:S(2)}) async-start(bf16[32,8,1024]{2,1,0:T(8,128)(2,1)} %bitcast.6), calls=%async_computation.1 | async-start | bytes 1048576 | tf_op jit(solution)/shard_map/all_to_all | solution.py:293
  56.3 0.0 collective-permute-done.1.right_ref
  56.4 0.7 slice.9
  57.1 2.7 %collective-permute-start.3 = (bf16[64,2176]{1,0:T(8,128)(2,1)}, bf16[64,2176]{1,0:T(8,128)(2,1)S(1)}, u32[]{:S(2)}, u32[]{:S(2)}) collective-permute-start(bf16[64,2176]{1,0:T(8,128)(2,1)} %slice.9), channel_id=1, source_target_pairs={{0,3},{1,0},{2,1},{3,2},{4,7},{5,4},{6,5},{7,6},{8,11},{9,8},{10,9... | collective-permute-start | bytes 835592 | tf_op jit(solution)/shard_map/ppermute | solution.py:270
  59.8 0.0 collective-permute-done.left_ref
  59.8 1.7 %slice.8 = bf16[64,2176]{1,0:T(8,128)(2,1)} slice(bf16[128,2176]{1,0:T(8,128)(2,1)} %collective-permute-done.left_ref), slice={[0:64], [0:2176]} | slice | bytes 557056 | tf_op jit(solution)/shard_map/slice | solution.py:269
  61.5 0.0 collective-permute-start.2
  61.5 4.4 %collective-permute-done.3.bottom_ref = bf16[64,2176]{1,0:T(8,128)(2,1)S(1)} collective-permute-done((bf16[64,2176]{1,0:T(8,128)(2,1)}, bf16[64,2176]{1,0:T(8,128)(2,1)S(1)}, u32[]{:S(2)}, u32[]{:S(2)}) %collective-permute-start.3) | collective-permute-done | bytes 278560 | tf_op jit(solution)/shard_map/ppermute | solution.py:270
  66.0 4.8 %collective-permute-done.2.top_ref = bf16[64,2176]{1,0:T(8,128)(2,1)} collective-permute-done((bf16[64,2176]{1,0:T(8,128)(2,1)}, bf16[64,2176]{1,0:T(8,128)(2,1)}, u32[]{:S(2)}, u32[]{:S(2)}) %collective-permute-start.2) | collective-permute-done | bytes 278560 | tf_op jit(solution)/shard_map/ppermute | solution.py:269
  70.7 0.0 copy-done.11
  70.8 1.6 %copy-done.2 = bf16[512,2048]{1,0:T(8,128)(2,1)S(1)} copy-done((bf16[512,2048]{1,0:T(8,128)(2,1)S(1)}, bf16[512,2048]{1,0:T(8,128)(2,1)}, u32[]{:S(2)}) %copy-start.2) | copy-done | bytes 2097176
  72.3 1.1 %copy-done.6 = bf16[128,2176]{1,0:T(8,128)(2,1)S(1)} copy-done((bf16[128,2176]{1,0:T(8,128)(2,1)S(1)}, bf16[128,2176]{1,0:T(8,128)(2,1)}, u32[]{:S(2)}) %copy-start.6) | copy-done | bytes 557080
  73.4 11.1 %project.1 = (bf16[512,2048]{1,0:T(8,128)(2,1)S(1)}, bf16[512,1024]{1,0:T(8,128)(2,1)S(1)}, bf16[512,2048]{1,0:T(8,128)(2,1)S(1)}, bf16[512,2048]{1,0:T(8,128)(2,1)S(1)}, bf16[512,128]{1,0:T(8,128)(2,1)S(1)}) custom-call(s32[1]{0:T(128)} %bitcast.head_ref, bf16[128,2176]{1,0:T(8,128)(2,1)S(1)} %copy-done.6, bf16[128,2176]{1,0:T(8,128)(2,1)} %collective-permute-done.left_ref, ...), custom_call_target="tpu_custom_call" | custom-call | tf_op jit(solution)/shard_map/project/pallas_call | solution.py:296
  84.5 0.0 copy-start.14
  84.5 11.7 %attention.1 = bf16[512,2048]{1,0:T(8,128)(2,1)} custom-call(bf16[512,2048]{1,0:T(8,128)(2,1)S(1)} %get-tuple-element.10.qn_ref, bf16[512,1024]{1,0:T(8,128)(2,1)S(1)} %get-tuple-element.11.qr_ref, bf16[512,2048]{1,0:T(8,128)(2,1)S(1)} %get-tuple-element.12.k_ref, bf16[512,2048]{1,0:T(8,128)(2,1)S(1)} %get-tuple-element.13.v_ref, ...), custom_call_target="tpu_custom_call" | custom-call | tf_op jit(solution)/shard_map/attention/pallas_call | solution.py:334
  96.2 0.0 all-to-all-done.1
  96.2 0.0 copy-done.14
  96.2 1.1 %unplace.1 = bf16[64,2048]{1,0:T(8,128)(2,1)} custom-call(bf16[256,1024]{1,0:T(8,128)(2,1)S(1)} %bitcast.9, s32[1,64]{1,0:T(1,128)S(1)} %bitcast.12), custom_call_target="tpu_custom_call" | custom-call | tf_op jit(solution)/shard_map/unplace/pallas_call | solution.py:355
  (7 shorter events, 0.0 us)
Async XLA Ops:
  0.6 33.0 %copy-start = (bf16[512,2048]{1,0:T(8,128)(2,1)S(1)}, bf16[512,2048]{1,0:T(8,128)(2,1)}, u32[]{:S(2)}) copy-start(bf16[512,2048]{1,0:T(8,128)(2,1)} %kup_ref.1) | copy-start | bytes 6291460
  0.6 1.1 %copy-start.7 = (bf16[128,1536]{1,0:T(8,128)(2,1)S(1)}, bf16[128,1536]{1,0:T(8,128)(2,1)}, u32[]{:S(2)}) copy-start(bf16[128,1536]{1,0:T(8,128)(2,1)} %x_ref.1) | copy-start | bytes 1179652
  1.8 1.0 %copy-start.8 = (bf16[64,3072]{1,0:T(8,128)(2,1)S(1)}, bf16[64,3072]{1,0:T(8,128)(2,1)}, u32[]{:S(2)}) copy-start(bf16[64,3072]{1,0:T(8,128)(2,1)} %q_ref.1) | copy-start | bytes 1179652
  2.8 0.9 copy-start.9
  3.7 0.7 copy-start.10
  4.4 0.7 copy-start.12
  5.1 0.7 copy-start.13
  5.8 0.7 copy-start.15
  6.4 0.7 copy-start.16
  7.1 26.6 %copy-start.17 = (s32[64]{0:T(128)S(1)}, s32[64]{0:T(128)}, u32[]{:S(2)}) copy-start(s32[64]{0:T(128)} %len_ref.1) | copy-start | bytes 772
  7.6 0.8 copy-start.5
  8.5 0.9 copy-start.4
  9.4 24.3 %all-to-all-start = ((bf16[32,8,1664]{2,1,0:T(8,128)(2,1)}), bf16[32,8,1664]{2,1,0:T(8,128)(2,1)S(1)}, u32[]{:S(2)}, u32[]{:S(2)}) async-start(bf16[32,8,1664]{2,1,0:T(8,128)(2,1)} %bitcast.10), calls=%async_computation | async-start | bytes 1703936 | tf_op jit(solution)/shard_map/all_to_all | solution.py:268
  18.8 37.5 %collective-permute-start.1 = (bf16[128,2176]{1,0:T(8,128)(2,1)}, bf16[128,2176]{1,0:T(8,128)(2,1)S(1)}, u32[]{:S(2)}, u32[]{:S(2)}) collective-permute-start(bf16[128,2176]{1,0:T(8,128)(2,1)} %copy-done.5), channel_id=1, source_target_pairs={{0,3},{1,0},{2,1},{3,2},{4,7},{5,4},{6,5},{7,6},{8,11},{9,8},{10,9... | collective-permute-start | bytes 1671176 | tf_op jit(solution)/shard_map/ppermute | solution.py:267
  21.6 38.2 %collective-permute-start = (bf16[128,2176]{1,0:T(8,128)(2,1)}, bf16[128,2176]{1,0:T(8,128)(2,1)}, u32[]{:S(2)}, u32[]{:S(2)}) collective-permute-start(bf16[128,2176]{1,0:T(8,128)(2,1)} %copy-done.5), channel_id=1, source_target_pairs={{0,1},{1,2},{2,3},{3,0},{4,5},{5,6},{6,7},{7,4},{8,9},{9,10},{10,1... | collective-permute-start | bytes 1671176 | tf_op jit(solution)/shard_map/ppermute | solution.py:266
  33.7 1.6 %copy-start.1 = (bf16[512,2048]{1,0:T(8,128)(2,1)S(1)}, bf16[512,2048]{1,0:T(8,128)(2,1)}, u32[]{:S(2)}) copy-start(bf16[512,2048]{1,0:T(8,128)(2,1)} %vup_ref.1) | copy-start | bytes 6291460
  35.3 1.6 %copy-start.3 = (bf16[64,64,256]{2,1,0:T(8,128)(2,1)S(1)}, bf16[64,64,256]{2,1,0:T(8,128)(2,1)}, u32[]{:S(2)}) copy-start(bf16[64,64,256]{2,1,0:T(8,128)(2,1)} %rk_ref.3) | copy-start | bytes 6291460
  52.3 18.4 %copy-start.11 = (f32[32,1]{1,0:T(8,128)S(1)}, f32[32,1]{1,0:T(8,128)}, u32[]{:S(2)}) copy-start(f32[32,1]{1,0:T(8,128)} %constant.7.freq_ref) | copy-start | bytes 388
  52.3 43.9 %all-to-all-start.1 = ((bf16[32,8,1024]{2,1,0:T(8,128)(2,1)}), bf16[32,8,1024]{2,1,0:T(8,128)(2,1)S(1)}, u32[]{:S(2)}, u32[]{:S(2)}) async-start(bf16[32,8,1024]{2,1,0:T(8,128)(2,1)} %bitcast.6), calls=%async_computation.1 | async-start | bytes 1048576 | tf_op jit(solution)/shard_map/all_to_all | solution.py:293
  57.1 8.9 %collective-permute-start.3 = (bf16[64,2176]{1,0:T(8,128)(2,1)}, bf16[64,2176]{1,0:T(8,128)(2,1)S(1)}, u32[]{:S(2)}, u32[]{:S(2)}) collective-permute-start(bf16[64,2176]{1,0:T(8,128)(2,1)} %slice.9), channel_id=1, source_target_pairs={{0,3},{1,0},{2,1},{3,2},{4,7},{5,4},{6,5},{7,6},{8,11},{9,8},{10,9... | collective-permute-start | bytes 835592 | tf_op jit(solution)/shard_map/ppermute | solution.py:270
  61.5 9.2 %collective-permute-start.2 = (bf16[64,2176]{1,0:T(8,128)(2,1)}, bf16[64,2176]{1,0:T(8,128)(2,1)}, u32[]{:S(2)}, u32[]{:S(2)}) collective-permute-start(bf16[64,2176]{1,0:T(8,128)(2,1)} %slice.8), channel_id=1, source_target_pairs={{0,1},{1,2},{2,3},{3,0},{4,5},{5,6},{6,7},{7,4},{8,9},{9,10},{10,1... | collective-permute-start | bytes 835592 | tf_op jit(solution)/shard_map/ppermute | solution.py:269
  70.8 1.6 %copy-start.2 = (bf16[512,2048]{1,0:T(8,128)(2,1)S(1)}, bf16[512,2048]{1,0:T(8,128)(2,1)}, u32[]{:S(2)}) copy-start(bf16[512,2048]{1,0:T(8,128)(2,1)} %vup_ref.1) | copy-start | bytes 6291460
  72.3 1.1 %copy-start.6 = (bf16[128,2176]{1,0:T(8,128)(2,1)S(1)}, bf16[128,2176]{1,0:T(8,128)(2,1)}, u32[]{:S(2)}) copy-start(bf16[128,2176]{1,0:T(8,128)(2,1)} %copy-done.5) | copy-start | bytes 1671172
  84.5 11.7 %copy-start.14 = (s32[64]{0:T(128)S(1)}, s32[64]{0:T(128)}, u32[]{:S(2)}) copy-start(s32[64]{0:T(128)} %param.22) | copy-start | bytes 772

commit v2 on v1

--- a/solution.py
+++ b/solution.py
@@ -1,4 +1,3 @@
-import functools
 import math
 
 import jax
@@ -48,7 +47,7 @@
     return jnp.sum(jnp.where(eye, row, 0), axis=1, keepdims=True)
 
 
-def pack_kernel(x_ref, l_ref, rk_ref, pos_ref, freq_ref, q_ref, owner_ref, slot_ref, packed_ref, send_ref):
+def pack_kernel(x_ref, l_ref, rk_ref, pos_ref, freq_ref, after_ref, packed_ref):
     packed_ref[:, :D_Q] = x_ref[...]
     packed_ref[:, D_Q:D_Q + D_C] = l_ref[...]
     pos = pos_ref[...]
@@ -63,6 +62,8 @@
     block = jnp.concatenate([first * cos - second * sin, first * sin + second * cos, tail], axis=0)
     packed_ref[:, D_Q + D_C:] = block.T.astype(BF16)
 
+
+def place_kernel(q_ref, owner_ref, slot_ref, send_ref):
     owner = owner_ref[...]
     owner_col = column_of(owner)
     same = owner_col == owner
@@ -90,7 +91,7 @@
 SLOTS_PER_STEP = 8
 
 
-def decode_kernel(recv_ref, kup_ref, vup_ref, lat_ref, rk_ref, len_ref, out_ref, lq_ref, qr_ref, lo_ref):
+def decode_kernel(recv_ref, kup_ref, vup_ref, lat_ref, rk_ref, len_ref, after_ref, out_ref, lq_ref, qr_ref, lo_ref):
     step = pl.program_id(0)
     rows = PEERS * 2 * MOST
 
@@ -166,18 +167,16 @@
 GROUP = 4
 
 
-def project_kernel(head_ref, own_ref, left_ref, right_ref, top_ref, bottom_ref, freq_ref, wq_ref, wk_ref, wv_ref,
-                   qn_ref, qr_ref, k_ref, v_ref, kr_ref, x_ref, cos_ref, sin_ref):
+def project_kernel(count, chunks, freq_ref, wq_ref, wk_ref, wv_ref, qn_ref, qr_ref, k_ref, v_ref, kr_ref,
+                   x_ref, cos_ref, sin_ref):
+    rows = count * CHUNK
+
     @pl.when(pl.program_id(0) == 0)
     def _():
-        me = head_ref[0]
-        x_ref[me] = own_ref[...]
-        x_ref[(me + 3) & 3] = left_ref[...]
-        x_ref[(me + 1) & 3] = right_ref[...]
-        x_ref[(me + 2) & 3, :64] = top_ref[...]
-        x_ref[(me + 2) & 3, 64:] = bottom_ref[...]
-        extra = x_ref[:, :, D_Q + D_C:].reshape(TOKENS, 128)
-        kr_ref[...] = extra
+        for i, chunk in enumerate(chunks):
+            x_ref[i * CHUNK:(i + 1) * CHUNK, :] = chunk[...]
+        extra = x_ref[:, D_Q + D_C:]
+        kr_ref[...] = extra.reshape(count, CHUNK, 128)
         turned = extra.astype(F32).T
         pos = turned[64:65] * 16.0 + turned[65:66]
         angle = pos * freq_ref[...]
@@ -185,53 +184,66 @@
         cos_ref[...] = jnp.concatenate([cos, cos, cos, cos], axis=0).T
         sin_ref[...] = jnp.concatenate([-sin, sin, -sin, sin], axis=0).T
 
-    half = TOKENS // 2
-    lane = iota((half, 128), 1) & 63
-    for part in range(2):
-        rows = slice(part * half, (part + 1) * half)
-        x = x_ref[2 * part:2 * part + 2, :, :].reshape(half, PACK)
-        queries = dot(x[:, :D_Q], wq_ref[...])
-        cos, sin = cos_ref[rows, :], sin_ref[rows, :]
-        for pair in range(GROUP // 2):
-            even, odd, rotary = split_pair(queries[:, pair * 384:(pair + 1) * 384])
-            qn_ref[rows, pair * 256:pair * 256 + 128] = even.astype(BF16)
-            qn_ref[rows, pair * 256 + 128:pair * 256 + 256] = odd.astype(BF16)
-            swapped = jnp.where(lane < 32, pltpu.roll(rotary, 96, 1), pltpu.roll(rotary, 32, 1))
-            qr_ref[rows, pair * 128:(pair + 1) * 128] = (rotary * cos + swapped * sin).astype(BF16)
-        latents = x[:, D_Q:D_Q + D_C]
-        k_ref[rows, :] = dot(latents, wk_ref[...]).astype(BF16)
-        v_ref[rows, :] = dot(latents, wv_ref[...]).astype(BF16)
-
-
-def attention_kernel(qn_ref, qr_ref, k_ref, v_ref, kr_ref, out_ref, bias_ref, key_ref, value_ref):
-    half = TOKENS // 2
+    lane = iota((rows, 128), 1) & 63
+    shape = (count, CHUNK, 128)
+    queries = dot(x_ref[:, :D_Q], wq_ref[...])
+    for pair in range(GROUP // 2):
+        even, odd, rotary = split_pair(queries[:, pair * 384:(pair + 1) * 384])
+        qn_ref[:, :, pair * 256:pair * 256 + 128] = even.astype(BF16).reshape(shape)
+        qn_ref[:, :, pair * 256 + 128:pair * 256 + 256] = odd.astype(BF16).reshape(shape)
+        swapped = jnp.where(lane < 32, pltpu.roll(rotary, 96, 1), pltpu.roll(rotary, 32, 1))
+        turned = (rotary * cos_ref[...] + swapped * sin_ref[...]).astype(BF16)
+        qr_ref[:, :, pair * 128:(pair + 1) * 128] = turned.reshape(shape)
+    latents = x_ref[:, D_Q:D_Q + D_C]
+    k_ref[...] = dot(latents, wk_ref[...]).astype(BF16).reshape(count, CHUNK, GROUP * 128)
+    v_ref[...] = dot(latents, wv_ref[...]).astype(BF16).reshape(count, CHUNK, GROUP * 128)
+
+
+def project_own_kernel(own_ref, freq_ref, wq_ref, wk_ref, wv_ref, *rest):
+    project_kernel(1, (own_ref,), freq_ref, wq_ref, wk_ref, wv_ref, *rest)
+
+
+def project_rest_kernel(right_ref, far_ref, left_ref, freq_ref, wq_ref, wk_ref, wv_ref, a, b, c, d, e, after, *rest):
+    project_kernel(3, (right_ref, far_ref, left_ref), freq_ref, wq_ref, wk_ref, wv_ref, *rest)
+
+
+TILE = 256
+
+
+def attention_kernel(head_ref, qn_ref, qr_ref, k_ref, v_ref, kr_ref, out_ref, bias_ref, pair_ref):
+    me = head_ref[0]
+    place = [(c - me + 3) & 3 for c in range(4)]
+    per_tile = TILE // CHUNK
 
     @pl.when(pl.program_id(0) == 0)
     def _():
-        extra = kr_ref[...].astype(F32)
-        pos = (extra[:, 64:65] * 16.0 + extra[:, 65:66]).astype(jnp.int32)
-        query, key = iota((TOKENS, TOKENS), 0), iota((TOKENS, TOKENS), 1)
-        bias_ref[...] = jnp.where((key <= query) & (key >= query - pos), 0.0, MASKED)
-        low_lane = iota((TOKENS, 128), 1) < 64
-        keep = jnp.where(low_lane, extra, 0.0)
-        key_ref[0, :, 128:] = keep.astype(BF16)
-        key_ref[1, :, 128:] = pltpu.roll(keep, 64, 1).astype(BF16)
-        value_ref[:, :, 128:] = jnp.ones((2, TOKENS, 128), BF16)
-
-    for sub in range(2):
-        lanes = slice(sub * 128, (sub + 1) * 128)
-        key_ref[sub, :, :128] = k_ref[:, lanes]
-        value_ref[sub, :, :128] = v_ref[:, lanes]
-    for sub in range(2):
-        lanes = slice(sub * 128, (sub + 1) * 128)
-        for part in range(2):
-            rows = slice(part * half, (part + 1) * half)
-            seen = (part + 1) * half
-            query = jnp.concatenate([qn_ref[rows, lanes], qr_ref[rows, :]], axis=1)
-            score = dot(query, key_ref[sub, :seen, :], ((1,), (1,))) + bias_ref[rows, :seen]
+        low_lane = iota((CHUNK, 128), 1) < 64
+        for c in range(4):
+            extra = kr_ref[place[c]].astype(F32)
+            pos = (extra[:, 64:65] * 16.0 + extra[:, 65:66]).astype(jnp.int32)
+            query, key = iota((CHUNK, TOKENS), 0) + c * CHUNK, iota((CHUNK, TOKENS), 1)
+            bias_ref[c * CHUNK:(c + 1) * CHUNK, :] = jnp.where((key <= query) & (key >= query - pos), 0.0, MASKED)
+            keep = jnp.where(low_lane, extra, 0.0)
+            pair_ref[0, c] = keep.astype(BF16)
+            pair_ref[1, c] = pltpu.roll(keep, 64, 1).astype(BF16)
+
+    ones = jnp.ones((CHUNK, 128), BF16)
+    for tile in range(TOKENS // TILE):
+        for sub in range(2):
+            lanes = slice(sub * 128, (sub + 1) * 128)
+            mine = range(tile * per_tile, (tile + 1) * per_tile)
+            seen = range((tile + 1) * per_tile)
+            query = jnp.concatenate(
+                [jnp.concatenate([qn_ref[place[c], :, lanes], qr_ref[place[c]]], axis=1) for c in mine], axis=0)
+            keys = jnp.concatenate(
+                [jnp.concatenate([k_ref[place[c], :, lanes], pair_ref[sub, c]], axis=1) for c in seen], axis=0)
+            values = jnp.concatenate(
+                [jnp.concatenate([v_ref[place[c], :, lanes], ones], axis=1) for c in seen], axis=0)
+            rows = slice(tile * TILE, (tile + 1) * TILE)
+            score = dot(query, keys, ((1,), (1,))) + bias_ref[rows, :len(seen) * CHUNK]
             top = jnp.max(score, axis=1, keepdims=True)
             raised = jnp.exp2((score - top) * SCALE_LOG2).astype(BF16)
-            total = dot(raised, value_ref[sub, :seen, :])
+            total = dot(raised, values)
             out_ref[rows, lanes] = (total[:, :128] / total[:, 128:]).astype(BF16)
 
 
@@ -245,29 +257,65 @@
 
 def smem():
     return pl.BlockSpec(memory_space=pltpu.SMEM)
+
+
+def anywhere():
+    return pl.BlockSpec(memory_space=pl.ANY)
+
+
+def project(count, kernel, chunks, freq, wq, wk, wv, into, after):
+    first = 0 if into else 3
+    shapes = [(HEADS * 128, GROUP * 128), (HEADS * 64, GROUP * 64), (HEADS * 128, GROUP * 128), (HEADS * 128, GROUP * 128)]
+    inputs = list(chunks) + [freq, wq, wk, wv] + list(into) + list(after)
+    n = len(chunks) + 4
+    return pl.pallas_call(
+        kernel,
+        grid=(HEADS // GROUP,),
+        in_specs=[whole((CHUNK, PACK))] * len(chunks) + [
+            whole((32, 1)),
+            pl.BlockSpec((D_Q, GROUP * 192), lambda i: (0, i)),
+            pl.BlockSpec((D_C, GROUP * 128), lambda i: (0, i)),
+            pl.BlockSpec((D_C, GROUP * 128), lambda i: (0, i)),
+        ] + [anywhere()] * (len(into) + len(after)),
+        out_specs=[pl.BlockSpec((count, CHUNK, block), lambda i: (first, 0, i)) for _, block in shapes]
+        + [pl.BlockSpec((count, CHUNK, 128), lambda i: (first, 0, 0))],
+        out_shape=[jax.ShapeDtypeStruct((4, CHUNK, width), BF16) for width, _ in shapes]
+        + [jax.ShapeDtypeStruct((4, CHUNK, 128), BF16)],
+        input_output_aliases={n + i: i for i in range(len(into))},
+        scratch_shapes=[
+            pltpu.VMEM((count * CHUNK, PACK), BF16),
+            pltpu.VMEM((count * CHUNK, 128), F32),
+            pltpu.VMEM((count * CHUNK, 128), F32),
+        ],
+        compiler_params=params(60),
+        name="project_rest" if count == 3 else "project_own",
+    )(*inputs)
 
 
 def on_device(x, latents, rotary_keys, positions, wq, wk, wv, queries, owner, slot, cache, cache_rope, lengths):
     me = lax.axis_index("head").astype(jnp.int32).reshape(1)
     freq = jnp.asarray(ROPE_BASE ** (-np.arange(32) / 32.0), F32).reshape(32, 1)
     owner_row, slot_row = owner.reshape(1, ROWS), slot.reshape(1, ROWS)
-    packed, send = pl.pallas_call(
+    send = pl.pallas_call(
+        place_kernel,
+        out_shape=jax.ShapeDtypeStruct((PEERS * 2 * MOST, SEND), BF16),
+        compiler_params=params(60),
+        name="place",
+    )(queries, owner_row, slot_row)
+    recv = lax.all_to_all(send, "req", 0, 0, tiled=True)
+
+    packed = pl.pallas_call(
         pack_kernel,
-        out_shape=(
-            jax.ShapeDtypeStruct((CHUNK, PACK), BF16),
-            jax.ShapeDtypeStruct((PEERS * 2 * MOST, SEND), BF16),
-        ),
-        compiler_params=params(24),
+        in_specs=[whole((CHUNK, D_Q)), whole((CHUNK, D_C)), whole((64, CHUNK)), whole((1, CHUNK)), whole((32, 1)), anywhere()],
+        out_specs=whole((CHUNK, PACK)),
+        out_shape=jax.ShapeDtypeStruct((CHUNK, PACK), BF16),
+        compiler_params=params(60),
         name="pack",
-    )(x, latents, rotary_keys, positions.reshape(1, CHUNK), freq, queries, owner_row, slot_row)
-
-    up = [(i, (i + 1) % 4) for i in range(4)]
-    down = [(i, (i + 3) % 4) for i in range(4)]
-    left = lax.ppermute(packed, "head", up)
-    right = lax.ppermute(packed, "head", down)
-    recv = lax.all_to_all(send, "req", 0, 0, tiled=True)
-    top = lax.ppermute(left[:64], "head", up)
-    bottom = lax.ppermute(right[64:], "head", down)
+    )(x, latents, rotary_keys, positions.reshape(1, CHUNK), freq, send)
+    right = lax.ppermute(packed, "head", [(i, (i + 3) % 4) for i in range(4)])
+    left = lax.ppermute(packed, "head", [(i, (i + 1) % 4) for i in range(4)])
+    far = lax.ppermute(packed, "head", [(i, (i + 2) % 4) for i in range(4)])
+    own = project(1, project_own_kernel, (packed,), freq, wq, wk, wv, (), ())
 
     returned = pl.pallas_call(
         decode_kernel,
@@ -279,6 +327,7 @@
             pl.BlockSpec((SLOTS_PER_STEP, CMAX, D_C), lambda i: (i, 0, 0)),
             pl.BlockSpec((SLOTS_PER_STEP, D_ROPE, CMAX), lambda i: (i, 0, 0)),
             smem(),
+            anywhere(),
         ],
         out_specs=whole((PEERS * 2 * MOST, RET)),
         out_shape=jax.ShapeDtypeStruct((PEERS * 2 * MOST, RET), BF16),
@@ -287,75 +336,39 @@
             pltpu.VMEM((HEADS * SLOTS, 128), F32),
             pltpu.VMEM((4, HEADS * SLOTS, 128), F32),
         ],
-        compiler_params=params(40),
+        compiler_params=params(60),
         name="decode",
-    )(recv, wk, wv, cache, cache_rope, lengths)
+    )(recv, wk, wv, cache, cache_rope, lengths, own[4])
+
+    qn, qr, keys, values, key_rope = project(
+        3, project_rest_kernel, (right, far, left), freq, wq, wk, wv, own, (returned,))
     returned = lax.all_to_all(returned, "req", 0, 0, tiled=True)
-
-    steps = HEADS // GROUP
-    qn, qr, keys, values, key_rope = pl.pallas_call(
-        project_kernel,
-        grid=(steps,),
-        in_specs=[
-            smem(),
-            whole((CHUNK, PACK)),
-            whole((CHUNK, PACK)),
-            whole((CHUNK, PACK)),
-            whole((64, PACK)),
-            whole((64, PACK)),
-            whole((32, 1)),
-            pl.BlockSpec((D_Q, GROUP * 192), lambda i: (0, i)),
-            pl.BlockSpec((D_C, GROUP * 128), lambda i: (0, i)),
-            pl.BlockSpec((D_C, GROUP * 128), lambda i: (0, i)),
-        ],
-        out_specs=(
-            pl.BlockSpec((TOKENS, GROUP * 128), lambda i: (0, i)),
-            pl.BlockSpec((TOKENS, GROUP * 64), lambda i: (0, i)),
-            pl.BlockSpec((TOKENS, GROUP * 128), lambda i: (0, i)),
-            pl.BlockSpec((TOKENS, GROUP * 128), lambda i: (0, i)),
-            whole((TOKENS, 128)),
-        ),
-        out_shape=(
-            jax.ShapeDtypeStruct((TOKENS, HEADS * 128), BF16),
-            jax.ShapeDtypeStruct((TOKENS, HEADS * 64), BF16),
-            jax.ShapeDtypeStruct((TOKENS, HEADS * 128), BF16),
-            jax.ShapeDtypeStruct((TOKENS, HEADS * 128), BF16),
-            jax.ShapeDtypeStruct((TOKENS, 128), BF16),
-        ),
-        scratch_shapes=[
-            pltpu.VMEM((4, CHUNK, PACK), BF16),
-            pltpu.VMEM((TOKENS, 128), F32),
-            pltpu.VMEM((TOKENS, 128), F32),
-        ],
-        compiler_params=params(40),
-        name="project",
-    )(me, packed, left, right, top, bottom, freq, wq, wk, wv)
 
     prompt_out = pl.pallas_call(
         attention_kernel,
         grid=(HEADS // 2,),
         in_specs=[
-            pl.BlockSpec((TOKENS, 256), lambda i: (0, i)),
-            pl.BlockSpec((TOKENS, 128), lambda i: (0, i)),
-            pl.BlockSpec((TOKENS, 256), lambda i: (0, i)),
-            pl.BlockSpec((TOKENS, 256), lambda i: (0, i)),
-            whole((TOKENS, 128)),
+            smem(),
+            pl.BlockSpec((4, CHUNK, 256), lambda i: (0, 0, i)),
+            pl.BlockSpec((4, CHUNK, 128), lambda i: (0, 0, i)),
+            pl.BlockSpec((4, CHUNK, 256), lambda i: (0, 0, i)),
+            pl.BlockSpec((4, CHUNK, 256), lambda i: (0, 0, i)),
+            whole((4, CHUNK, 128)),
         ],
         out_specs=pl.BlockSpec((TOKENS, 256), lambda i: (0, i)),
         out_shape=jax.ShapeDtypeStruct((TOKENS, HEADS * D_V), BF16),
         scratch_shapes=[
             pltpu.VMEM((TOKENS, TOKENS), F32),
-            pltpu.VMEM((2, TOKENS, 256), BF16),
-            pltpu.VMEM((2, TOKENS, 256), BF16),
-        ],
-        compiler_params=params(32),
+            pltpu.VMEM((2, 4, CHUNK, 128), BF16),
+        ],
+        compiler_params=params(60),
         name="attention",
-    )(qn, qr, keys, values, key_rope)
+    )(me, qn, qr, keys, values, key_rope)
 
     decode_out = pl.pallas_call(
         unplace_kernel,
         out_shape=jax.ShapeDtypeStruct((ROWS, HEADS * D_V), BF16),
-        compiler_params=params(16),
+        compiler_params=params(60),
         name="unplace",
     )(returned, owner_row)
     return prompt_out, decode_out

time: 98.2 us -> 81 us (0.82)
  waiting for transfers between devices: 21.3 us -> 0.96 us
  Pallas kernels: 39.9 us -> 55.3 us
  local copies, waits for them, and re-layouts: 16.4 us -> 2.87 us
  starting transfers between devices: 19 us -> 20.5 us
    pallas_call x3 -> x5, Pallas kernels: 23.3 us -> 36 us  [the longest x2 19.1 us: project(): pl.pallas_call(kernel, grid=(HEADS // GROUP,), in_specs=[whole((CHUNK, PA...]
    unnamed x36 -> x10, local copies, waits for them, and re-layouts: 14 us -> 2.87 us
    all_to_all x1, waiting for transfers between devices: 12 us -> 0.95 us  [on_device(): recv = lax.all_to_all(send, 'req', 0, 0, tiled=True)]
    ppermute x4 -> x3, waiting for transfers between devices: 9.23 us -> 0.01 us  [the longest x1 0.01 us: on_device(): right = lax.ppermute(packed, 'head', [(i, (i + 3) % 4) for i in range(4)])]
    all_to_all x1, starting transfers between devices: 4.03 us -> 7.25 us  [on_device(): returned = lax.all_to_all(returned, 'req', 0, 0, tiled=True)]
    slice x2 -> x0, local copies, waits for them, and re-layouts: 2.42 us -> none  [the longest x1 1.68 us: on_device(): top = lax.ppermute(left[:64], 'head', up)]
    ppermute x4 -> x3, starting transfers between devices: 5.55 us -> 3.78 us  [the longest x1 2.74 us: on_device(): right = lax.ppermute(packed, 'head', [(i, (i + 3) % 4) for i in range(4)])]
    pallas_call x1, Pallas kernels: 15.4 us -> 17.2 us  [on_device(): pl.pallas_call(decode_kernel, grid=(SLOTS // SLOTS_PER_STEP,), in_specs=[...]
  transfers between devices with their start and end apart: 6 -> 5, of which waited for: 3 -> 1; matrix products, arithmetic and copies ran while one was open for 2% -> 0% of each run, Pallas kernels for 39% -> 63%
where the time goes in v2:
time: 81 us; the launch traced here: 80.3 us
  Pallas kernels  55.3 us (68%)
  starting transfers between devices  20.5 us (25%)
  local copies, waits for them, and re-layouts  2.87 us (4%)
  waiting for transfers between devices  0.96 us (1%)
    pallas_call x2, Pallas kernels, project(): pl.pallas_call(kernel, grid=(HEADS // GROUP,), in_specs=[whole((CHUNK, PA...  19.1 us
    pallas_call x1, Pallas kernels, on_device(): pl.pallas_call(decode_kernel, grid=(SLOTS // SLOTS_PER_STEP,), in_specs=[...  17.2 us
    pallas_call x1, Pallas kernels, on_device(): pl.pallas_call(attention_kernel, grid=(HEADS // 2,), in_specs=[smem(), pl...  12.2 us
    all_to_all x1, starting transfers between devices, on_device(): recv = lax.all_to_all(send, 'req', 0, 0, tiled=True)  9.42 us
    all_to_all x1, starting transfers between devices, on_device(): returned = lax.all_to_all(returned, 'req', 0, 0, tiled=True)  7.25 us
    unnamed x10, local copies, waits for them, and re-layouts  2.87 us
    ppermute x1, starting transfers between devices, on_device(): right = lax.ppermute(packed, 'head', [(i, (i + 3) % 4) for i in range(4)])  2.74 us
    pallas_call x1, Pallas kernels, on_device(): pl.pallas_call(place_kernel, out_shape=jax.ShapeDtypeStruct((PEERS * 2 *...  2.44 us
  transfers between devices with their start and end apart: 5, of which 1 were waited for; matrix products, arithmetic and copies ran while one was open for 0% of the time, Pallas kernels for 63%

profile of v2, /device:TPU:1, one launch (start us, length us, event | category | flops | bytes accessed | tf_op | source)
XLA Modules:
  0.0 80.3 jit_solution(5914397143915509581)
XLA Ops:
  0.6 2.4 %place.1.after_ref = bf16[256,1664]{1,0:T(8,128)(2,1)} custom-call(bf16[64,3072]{1,0:T(8,128)(2,1)} %q_ref.1, s32[1,64]{1,0:T(1,128)} %bitcast.12, s32[1,64]{1,0:T(1,128)} %bitcast.14), custom_call_target="tpu_custom_call" | custom-call | tf_op jit(solution)/shard_map/place/pallas_call | solution.py:299
  3.1 9.4 %all-to-all-start = ((bf16[32,8,1664]{2,1,0:T(8,128)(2,1)}), bf16[32,8,1664]{2,1,0:T(8,128)(2,1)S(1)}, u32[]{:S(2)}, u32[]{:S(2)}) async-start(bf16[32,8,1664]{2,1,0:T(8,128)(2,1)} %bitcast.8), calls=%async_computation | async-start | bytes 1703936 | tf_op jit(solution)/shard_map/all_to_all | solution.py:305
  12.5 2.2 %pack.1.own_ref = bf16[128,2176]{1,0:T(8,128)(2,1)} custom-call(bf16[128,1536]{1,0:T(8,128)(2,1)} %x_ref.1, bf16[128,512]{1,0:T(8,128)(2,1)} %l_ref.1, bf16[64,128]{1,0:T(8,128)(2,1)} %rk_ref.2, s32[1,128]{1,0:T(1,128)} %bitcast.15, f32[32,1]{1,0:T(8,128)} %constant.7.freq_ref, bf16[256,1664]{1,0:T(8,128)(2,1)} %place.1.after_ref), custom_call_target="tpu_custom_call" | custom-call | tf_op jit(solution)/shard_map/pack/pallas_call | solution.py:307
  14.7 2.7 %collective-permute-start = (bf16[128,2176]{1,0:T(8,128)(2,1)}, bf16[128,2176]{1,0:T(8,128)(2,1)S(1)}, u32[]{:S(2)}, u32[]{:S(2)}) collective-permute-start(bf16[128,2176]{1,0:T(8,128)(2,1)} %pack.1.own_ref), channel_id=1, source_target_pairs={{0,3},{1,0},{2,1},{3,2},{4,7},{5,4},{6,5},{7,6},{8,11},{9,8},{10,9... | collective-permute-start | bytes 1671176 | tf_op jit(solution)/shard_map/ppermute | solution.py:315
  17.4 0.3 collective-permute-start.1
  17.8 0.7 collective-permute-start.2
  18.5 7.9 %project_own.1 = (bf16[4,128,2048]{2,1,0:T(8,128)(2,1)}, bf16[4,128,1024]{2,1,0:T(8,128)(2,1)}, bf16[4,128,2048]{2,1,0:T(8,128)(2,1)}, bf16[4,128,2048]{2,1,0:T(8,128)(2,1)}, bf16[4,128,128]{2,1,0:T(8,128)(2,1)}) custom-call(bf16[128,2176]{1,0:T(8,128)(2,1)} %pack.1.own_ref, f32[32,1]{1,0:T(8,128)} %constant.7.freq_ref, bf16[1536,3072]{1,0:T(8,128)(2,1)} %wq_ref.3, ...), custom_call_target="tpu_custom_call" | custom-call | tf_op jit(solution)/shard_map/project_own/pallas_call | solution.py:271
  26.4 1.0 %all-to-all-done = bf16[32,8,1664]{2,1,0:T(8,128)(2,1)S(1)} async-done(((bf16[32,8,1664]{2,1,0:T(8,128)(2,1)}), bf16[32,8,1664]{2,1,0:T(8,128)(2,1)S(1)}, u32[]{:S(2)}, u32[]{:S(2)}) %all-to-all-start) | async-done | bytes 852000 | tf_op jit(solution)/shard_map/all_to_all | solution.py:305
  27.4 0.0 copy-start
  27.4 0.9 %copy-done = bf16[32,8,1664]{2,1,0:T(8,128)(2,1)} copy-done((bf16[32,8,1664]{2,1,0:T(8,128)(2,1)}, bf16[32,8,1664]{2,1,0:T(8,128)(2,1)S(1)}, u32[]{:S(2)}) %copy-start) | copy-done | bytes 851992
  28.3 17.2 %decode.1.after = bf16[256,1024]{1,0:T(8,128)(2,1)} custom-call(bf16[256,1664]{1,0:T(8,128)(2,1)} %bitcast.10, bf16[512,2048]{1,0:T(8,128)(2,1)} %wk_ref.3, bf16[512,2048]{1,0:T(8,128)(2,1)} %wv_ref.3, bf16[64,256,512]{2,1,0:T(8,128)(2,1)} %lat_ref.1, bf16[64,64,256]{2,1,0:T(8,128)(2,1)} %rk_ref.3, s32[64]{0:T(128)} %len_ref.1, ...), custom_call_target="tpu_custom_call" | custom-call | tf_op jit(solution)/shard_map/decode/pallas_call | solution.py:320
  45.4 7.3 %all-to-all-start.1 = ((bf16[32,8,1024]{2,1,0:T(8,128)(2,1)}), bf16[32,8,1024]{2,1,0:T(8,128)(2,1)S(1)}, u32[]{:S(2)}, u32[]{:S(2)}) async-start(bf16[32,8,1024]{2,1,0:T(8,128)(2,1)} %bitcast.9), calls=%async_computation.1 | async-start | bytes 1048576 | tf_op jit(solution)/shard_map/all_to_all | solution.py:345
  52.7 0.0 collective-permute-done.right_ref
  52.7 0.0 copy-start.2
  52.7 0.0 collective-permute-done.1.far_ref
  52.7 0.0 copy-start.3
  52.7 0.0 collective-permute-done.2.left_ref
  52.7 0.0 copy-start.4
  52.7 0.8 copy-done.2
  53.5 0.2 copy-done.3
  53.7 0.2 copy-done.4
  53.9 11.1 %project_rest.1 = (bf16[4,128,2048]{2,1,0:T(8,128)(2,1)}, bf16[4,128,1024]{2,1,0:T(8,128)(2,1)}, bf16[4,128,2048]{2,1,0:T(8,128)(2,1)}, bf16[4,128,2048]{2,1,0:T(8,128)(2,1)}, bf16[4,128,128]{2,1,0:T(8,128)(2,1)}) custom-call(bf16[128,2176]{1,0:T(8,128)(2,1)} %copy-done.2, ...), custom_call_target="tpu_custom_call", output_to_operand_aliasing={{0}: (7, {}), {1}: (8, {}), {2}: (9, {}), {3}: (10, {}), {4... | custom-call | tf_op jit(solution)/shard_map/project_rest/pallas_call | solution.py:271
  65.1 12.2 %attention.1 = bf16[512,2048]{1,0:T(8,128)(2,1)} custom-call(s32[1]{0:T(128)} %bitcast.head_ref, bf16[4,128,2048]{2,1,0:T(8,128)(2,1)} %get-tuple-element.17.qn_ref, bf16[4,128,1024]{2,1,0:T(8,128)(2,1)} %get-tuple-element.18.qr_ref, bf16[4,128,2048]{2,1,0:T(8,128)(2,1)} %get-tuple-element.19.k_ref, bf16[4,128,2048]{2,1,0:T(8,128)(2,1)} %get-tuple-element.20.v_ref, ...), custom_call_target="tpu_custom_call" | custom-call | tf_op jit(solution)/shard_map/attention/pallas_call | solution.py:347
  77.3 0.0 all-to-all-done.1
  77.3 0.0 copy-start.1
  77.3 0.8 copy-done.1
  78.1 2.2 %unplace.1 = bf16[64,2048]{1,0:T(8,128)(2,1)} custom-call(bf16[256,1024]{1,0:T(8,128)(2,1)} %bitcast.11, s32[1,64]{1,0:T(1,128)} %bitcast.13), custom_call_target="tpu_custom_call" | custom-call | tf_op jit(solution)/shard_map/unplace/pallas_call | solution.py:368
Async XLA Ops:
  3.1 24.3 %all-to-all-start = ((bf16[32,8,1664]{2,1,0:T(8,128)(2,1)}), bf16[32,8,1664]{2,1,0:T(8,128)(2,1)S(1)}, u32[]{:S(2)}, u32[]{:S(2)}) async-start(bf16[32,8,1664]{2,1,0:T(8,128)(2,1)} %bitcast.8), calls=%async_computation | async-start | bytes 1703936 | tf_op jit(solution)/shard_map/all_to_all | solution.py:305
  14.7 38.0 %collective-permute-start = (bf16[128,2176]{1,0:T(8,128)(2,1)}, bf16[128,2176]{1,0:T(8,128)(2,1)S(1)}, u32[]{:S(2)}, u32[]{:S(2)}) collective-permute-start(bf16[128,2176]{1,0:T(8,128)(2,1)} %pack.1.own_ref), channel_id=1, source_target_pairs={{0,3},{1,0},{2,1},{3,2},{4,7},{5,4},{6,5},{7,6},{8,11},{9,8},{10,9... | collective-permute-start | bytes 1671176 | tf_op jit(solution)/shard_map/ppermute | solution.py:315
  17.4 35.3 %collective-permute-start.1 = (bf16[128,2176]{1,0:T(8,128)(2,1)}, bf16[128,2176]{1,0:T(8,128)(2,1)S(1)}, u32[]{:S(2)}, u32[]{:S(2)}) collective-permute-start(bf16[128,2176]{1,0:T(8,128)(2,1)} %pack.1.own_ref), channel_id=1, source_target_pairs={{0,2},{1,3},{2,0},{3,1},{4,6},{5,7},{6,4},{7,5},{8,10},{9,11},{10,... | collective-permute-start | bytes 1671176 | tf_op jit(solution)/shard_map/ppermute | solution.py:317
  17.8 35.0 %collective-permute-start.2 = (bf16[128,2176]{1,0:T(8,128)(2,1)}, bf16[128,2176]{1,0:T(8,128)(2,1)S(1)}, u32[]{:S(2)}, u32[]{:S(2)}) collective-permute-start(bf16[128,2176]{1,0:T(8,128)(2,1)} %pack.1.own_ref), channel_id=1, source_target_pairs={{0,1},{1,2},{2,3},{3,0},{4,5},{5,6},{6,7},{7,4},{8,9},{9,10},{10,1... | collective-permute-start | bytes 1671176 | tf_op jit(solution)/shard_map/ppermute | solution.py:316
  27.4 0.9 %copy-start = (bf16[32,8,1664]{2,1,0:T(8,128)(2,1)}, bf16[32,8,1664]{2,1,0:T(8,128)(2,1)S(1)}, u32[]{:S(2)}) copy-start(bf16[32,8,1664]{2,1,0:T(8,128)(2,1)S(1)} %all-to-all-done) | copy-start | bytes 2555908
  45.4 31.9 %all-to-all-start.1 = ((bf16[32,8,1024]{2,1,0:T(8,128)(2,1)}), bf16[32,8,1024]{2,1,0:T(8,128)(2,1)S(1)}, u32[]{:S(2)}, u32[]{:S(2)}) async-start(bf16[32,8,1024]{2,1,0:T(8,128)(2,1)} %bitcast.9), calls=%async_computation.1 | async-start | bytes 1048576 | tf_op jit(solution)/shard_map/all_to_all | solution.py:345
  52.7 0.8 %copy-start.2 = (bf16[128,2176]{1,0:T(8,128)(2,1)}, bf16[128,2176]{1,0:T(8,128)(2,1)S(1)}, u32[]{:S(2)}) copy-start(bf16[128,2176]{1,0:T(8,128)(2,1)S(1)} %collective-permute-done.right_ref) | copy-start | bytes 1671172
  52.7 1.0 %copy-start.3 = (bf16[128,2176]{1,0:T(8,128)(2,1)}, bf16[128,2176]{1,0:T(8,128)(2,1)S(1)}, u32[]{:S(2)}) copy-start(bf16[128,2176]{1,0:T(8,128)(2,1)S(1)} %collective-permute-done.1.far_ref) | copy-start | bytes 1671172
  52.7 1.2 %copy-start.4 = (bf16[128,2176]{1,0:T(8,128)(2,1)}, bf16[128,2176]{1,0:T(8,128)(2,1)S(1)}, u32[]{:S(2)}) copy-start(bf16[128,2176]{1,0:T(8,128)(2,1)S(1)} %collective-permute-done.2.left_ref) | copy-start | bytes 1671172
  77.3 0.8 copy-start.1

commit v3 on v2

--- a/solution.py
+++ b/solution.py
@@ -47,7 +47,7 @@
     return jnp.sum(jnp.where(eye, row, 0), axis=1, keepdims=True)
 
 
-def pack_kernel(x_ref, l_ref, rk_ref, pos_ref, freq_ref, after_ref, packed_ref):
+def pack_kernel(x_ref, l_ref, rk_ref, pos_ref, freq_ref, len_ref, after_ref, packed_ref, order_ref, sorted_ref):
     packed_ref[:, :D_Q] = x_ref[...]
     packed_ref[:, D_Q:D_Q + D_C] = l_ref[...]
     pos = pos_ref[...]
@@ -61,6 +61,14 @@
     tail = jnp.where(place == 0, high, jnp.where(place == 1, low, 0.0))
     block = jnp.concatenate([first * cos - second * sin, first * sin + second * cos, tail], axis=0)
     packed_ref[:, D_Q + D_C:] = block.T.astype(BF16)
+
+    length = len_ref[...]
+    length_col = column_of(length)
+    this, other = iota((SLOTS, SLOTS), 0), iota((SLOTS, SLOTS), 1)
+    ahead = (length < length_col) | ((length == length_col) & (other < this))
+    rank = jnp.sum(jnp.where(ahead, 1, 0), axis=1, keepdims=True)
+    order_ref[...] = jnp.sum(jnp.where(rank == other, this, 0), axis=0, keepdims=True)
+    sorted_ref[...] = jnp.sum(jnp.where(rank == other, length_col, 0), axis=0, keepdims=True)
 
 
 def place_kernel(q_ref, owner_ref, slot_ref, send_ref):
@@ -88,68 +96,118 @@
     return three[:, :128], odd, rotary
 
 
-SLOTS_PER_STEP = 8
-
-
-def decode_kernel(recv_ref, kup_ref, vup_ref, lat_ref, rk_ref, len_ref, after_ref, out_ref, lq_ref, qr_ref, lo_ref):
-    step = pl.program_id(0)
+TOGETHER = 8
+WIDE = TOGETHER * HEADS
+SECTION = 16
+SECTIONS = SLOTS // SECTION
+WIDTHS = (64, 128, 192, 256)
+
+
+def decode_kernel(recv_hbm, kup_hbm, lat_hbm, rk_hbm, vup_hbm, order_ref, len_ref, order_row_ref, after_ref, out_ref,
+                  recv_ref, kup_ref, lat_ref, rk_ref, vup_ref, lq_ref, qr_ref, lo_ref, sems, lat_sems):
     rows = PEERS * 2 * MOST
-
-    def slot_onehot():
+    copies = [pltpu.make_async_copy(src, dst, sems.at[i]) for i, (src, dst) in enumerate(
+        ((recv_hbm, recv_ref), (kup_hbm, kup_ref), (rk_hbm, rk_ref), (vup_hbm, vup_ref)))]
+    copies[0].start()
+    copies[1].start()
+
+    def of_width(section, width):
+        longest = len_ref[section * SECTION + SECTION - 1]
+        return (longest <= width) & (longest > width - 64)
+
+    def fetch(section, width, place):
+        return pltpu.make_async_copy(
+            lat_hbm.at[order_ref[place], pl.ds(0, width)], lat_ref.at[place, pl.ds(0, width)], lat_sems.at[section])
+
+    for section in range(SECTIONS):
+        for width in WIDTHS:
+            @pl.when(of_width(section, width))
+            def _():
+                @pl.loop(0, SECTION)
+                def _(i):
+                    fetch(section, width, section * SECTION + i).start()
+        if section == 0:
+            copies[2].start()
+    copies[3].start()
+
+    def place_onehot():
         slot_col = recv_ref[:, 1536:].astype(jnp.int32)
-        lane = iota((rows, 128), 1)
-        hit = slot_col == lane + 1
-        half = (iota((rows, 128), 0) & 7) < MOST
+        hit = slot_col[:, :SLOTS] == order_row_ref[...] + 1
+        half = (iota((rows, SLOTS), 0) & 7) < MOST
         return hit & half, hit & jnp.logical_not(half)
 
-    @pl.when(step == 0)
-    def _():
-        first, second = slot_onehot()
-        for side, hit in enumerate((first, second)):
-            spread = jnp.where(hit, 1.0, 0.0).T[:SLOTS].astype(BF16)
-            queries = dot(spread, recv_ref[:, :1536])
-            for pair in range(4):
-                even, odd, rotary = split_pair(queries[:, pair * 384:(pair + 1) * 384])
-                for sub, nope in enumerate((even, odd)):
-                    head = side * 8 + pair * 2 + sub
-                    latent = dot(nope.astype(BF16), kup_ref[:, head * 128:(head + 1) * 128], ((1,), (1,)))
-                    latent = latent.astype(BF16).astype(F32)
-                    for part in range(4):
-                        lq_ref[part, head * SLOTS:(head + 1) * SLOTS, :] = latent[:, part * 128:(part + 1) * 128]
-                    qr_ref[head * SLOTS:(head + 1) * SLOTS, :] = rotary if sub == 0 else pltpu.roll(rotary, 64, 1)
-
-    scores = []
-    for i in range(SLOTS_PER_STEP):
-        slot = step * SLOTS_PER_STEP + i
-        latent = jnp.concatenate(
-            [lq_ref[part, pl.ds(slot, HEADS, stride=SLOTS), :].astype(BF16) for part in range(4)], axis=1)
-        rotary = qr_ref[pl.ds(slot, HEADS, stride=SLOTS), :].astype(BF16)
-        score = dot(latent, lat_ref[i], ((1,), (1,))) + dot(rotary[:, :D_ROPE], rk_ref[i])
-        score = jnp.where(iota((HEADS, CMAX), 1) < len_ref[slot], score * SCALE, MASKED)
-        scores.append(score)
-    weights = []
-    for i in range(SLOTS_PER_STEP):
-        score = scores[i]
-        raised = jnp.exp(score - jnp.max(score, axis=1, keepdims=True))
-        weights.append((raised / jnp.sum(raised, axis=1, keepdims=True)).astype(BF16))
-    for i in range(SLOTS_PER_STEP):
-        slot = step * SLOTS_PER_STEP + i
-        latent_out = dot(weights[i], lat_ref[i])
-        latent_out = latent_out.astype(BF16).astype(F32)
-        for part in range(4):
-            lo_ref[part, pl.ds(slot, HEADS, stride=SLOTS), :] = latent_out[:, part * 128:(part + 1) * 128]
-
-    @pl.when(step == pl.num_programs(0) - 1)
-    def _():
-        outs = []
-        for head in range(HEADS):
-            latent_out = jnp.concatenate(
-                [lo_ref[part, head * SLOTS:(head + 1) * SLOTS, :].astype(BF16) for part in range(4)], axis=1)
-            outs.append(dot(latent_out, vup_ref[:, head * 128:(head + 1) * 128]).astype(BF16))
-        outs = jnp.concatenate([jnp.concatenate(outs[:8], axis=1), jnp.concatenate(outs[8:], axis=1)], axis=0)
-        first, second = slot_onehot()
-        spread = jnp.concatenate([jnp.where(first, 1.0, 0.0)[:, :SLOTS], jnp.where(second, 1.0, 0.0)[:, :SLOTS]], axis=1)
-        out_ref[...] = dot(spread.astype(BF16), outs).astype(BF16)
+    copies[0].wait()
+    first, second = place_onehot()
+    blank = jnp.zeros((SLOTS, 128), BF16)
+    low_lane = iota((SLOTS, 128), 1) < 64
+    spreads = [jnp.concatenate([jnp.where(hit, 1.0, 0.0), jnp.zeros((rows, 64), F32)], axis=1).T[:SLOTS].astype(BF16)
+               for hit in (first, second)]
+    queries = [dot(spread, recv_ref[:, :1536]) for spread in spreads]
+    copies[1].wait()
+    for side in range(2):
+        for pair in range(4):
+            head = side * 8 + pair * 2
+            even, odd, rotary = split_pair(queries[side][:, pair * 384:(pair + 1) * 384])
+            both = jnp.concatenate([jnp.concatenate([even.astype(BF16), blank], axis=1),
+                                    jnp.concatenate([blank, odd.astype(BF16)], axis=1)], axis=0)
+            latent = dot(both, kup_ref[:, head * 128:(head + 2) * 128], ((1,), (1,)))
+            lq_ref[head:head + 2] = latent.astype(BF16).astype(F32).reshape(2, SLOTS, D_C)
+            turned = pltpu.roll(rotary, 64, 1)
+            qr_ref[head] = jnp.where(low_lane, rotary, turned)
+            qr_ref[head + 1] = jnp.where(low_lane, turned, rotary)
+    copies[2].wait()
+
+    def attend(section, width):
+        @pl.loop(0, SECTION)
+        def _(i):
+            fetch(section, width, section * SECTION + i).wait()
+
+        row, lane = iota((WIDE, WIDE), 0), iota((WIDE, WIDE), 1)
+        by_place = jnp.where(lane == (row & 15) * TOGETHER + (row >> 4), 1.0, 0.0).astype(BF16)
+        by_head = jnp.where(row == (lane & 15) * TOGETHER + (lane >> 4), 1.0, 0.0).astype(BF16)
+        row_place = iota((WIDE, 1), 0) >> 4
+        starts = [pl.multiple_of(section * SECTION + group * TOGETHER, TOGETHER) for group in range(SECTION // TOGETHER)]
+        queries = []
+        for start in starts:
+            latent = lq_ref[:, pl.ds(start, TOGETHER), :].reshape(WIDE, D_C).astype(BF16)
+            rotary = qr_ref[:, pl.ds(start, TOGETHER), :].reshape(WIDE, 128).astype(BF16)
+            queries.append((dot(by_place, latent).astype(BF16), dot(by_place, rotary).astype(BF16)))
+        scores = []
+        for start, (latent, rotary) in zip(starts, queries):
+            score = []
+            length = jnp.full((WIDE, 1), len_ref[start], jnp.int32)
+            for i in range(TOGETHER):
+                mine = slice(i * HEADS, (i + 1) * HEADS)
+                score.append(dot(latent[mine], lat_ref[start + i, :width], ((1,), (1,)))
+                             + dot(rotary[mine, :D_ROPE], rk_ref[order_ref[start + i], :, :width]))
+                length = jnp.where(row_place == i, len_ref[start + i], length)
+            score = jnp.concatenate(score, axis=0)
+            scores.append(jnp.where(iota((WIDE, width), 1) < length, score * SCALE, MASKED))
+        for start, score in zip(starts, scores):
+            raised = jnp.exp(score - jnp.max(score, axis=1, keepdims=True))
+            weights = (raised * (1.0 / jnp.sum(raised, axis=1, keepdims=True))).astype(BF16)
+            total = jnp.concatenate(
+                [dot(weights[i * HEADS:(i + 1) * HEADS], lat_ref[start + i, :width]).astype(BF16)
+                 for i in range(TOGETHER)], axis=0)
+            lo_ref[:, pl.ds(start, TOGETHER), :] = dot(by_head, total).reshape(HEADS, TOGETHER, D_C)
+
+    @pl.loop(0, SECTIONS)
+    def _(section):
+        for width in WIDTHS:
+            @pl.when(of_width(section, width))
+            def _():
+                attend(section, width)
+
+    copies[3].wait()
+    outs = []
+    for head in range(0, HEADS, 2):
+        latent_out = lo_ref[head:head + 2].reshape(2 * SLOTS, D_C).astype(BF16)
+        both = dot(latent_out, vup_ref[:, head * 128:(head + 2) * 128])
+        outs += [both[:SLOTS, :128].astype(BF16), both[SLOTS:, 128:].astype(BF16)]
+    outs = jnp.concatenate([jnp.concatenate(outs[:8], axis=1), jnp.concatenate(outs[8:], axis=1)], axis=0)
+    first, second = place_onehot()
+    spread = jnp.concatenate([jnp.where(first, 1.0, 0.0), jnp.where(second, 1.0, 0.0)], axis=1)
+    out_ref[...] = dot(spread.astype(BF16), outs).astype(BF16)
 
 
 def unplace_kernel(ret_ref, owner_ref, out_ref):
@@ -207,13 +265,9 @@
     project_kernel(3, (right_ref, far_ref, left_ref), freq_ref, wq_ref, wk_ref, wv_ref, *rest)
 
 
-TILE = 256
-
-
 def attention_kernel(head_ref, qn_ref, qr_ref, k_ref, v_ref, kr_ref, out_ref, bias_ref, pair_ref):
     me = head_ref[0]
     place = [(c - me + 3) & 3 for c in range(4)]
-    per_tile = TILE // CHUNK
 
     @pl.when(pl.program_id(0) == 0)
     def _():
@@ -228,23 +282,27 @@
             pair_ref[1, c] = pltpu.roll(keep, 64, 1).astype(BF16)
 
     ones = jnp.ones((CHUNK, 128), BF16)
-    for tile in range(TOKENS // TILE):
-        for sub in range(2):
-            lanes = slice(sub * 128, (sub + 1) * 128)
-            mine = range(tile * per_tile, (tile + 1) * per_tile)
-            seen = range((tile + 1) * per_tile)
-            query = jnp.concatenate(
-                [jnp.concatenate([qn_ref[place[c], :, lanes], qr_ref[place[c]]], axis=1) for c in mine], axis=0)
-            keys = jnp.concatenate(
-                [jnp.concatenate([k_ref[place[c], :, lanes], pair_ref[sub, c]], axis=1) for c in seen], axis=0)
-            values = jnp.concatenate(
-                [jnp.concatenate([v_ref[place[c], :, lanes], ones], axis=1) for c in seen], axis=0)
-            rows = slice(tile * TILE, (tile + 1) * TILE)
-            score = dot(query, keys, ((1,), (1,))) + bias_ref[rows, :len(seen) * CHUNK]
-            top = jnp.max(score, axis=1, keepdims=True)
-            raised = jnp.exp2((score - top) * SCALE_LOG2).astype(BF16)
-            total = dot(raised, values)
-            out_ref[rows, lanes] = (total[:, :128] / total[:, 128:]).astype(BF16)
+    half = TOKENS // 2
+    scores = []
+    for sub in range(2):
+        lanes = slice(sub * 128, (sub + 1) * 128)
+        query = [jnp.concatenate([qn_ref[place[c], :, lanes], qr_ref[place[c]]], axis=1) for c in range(4)]
+        keys = [jnp.concatenate([k_ref[place[c], :, lanes], pair_ref[sub, c]], axis=1) for c in range(4)]
+        early = dot(jnp.concatenate(query, axis=0), jnp.concatenate(keys[:2], axis=0), ((1,), (1,))) + bias_ref[:, :half]
+        late = dot(jnp.concatenate(query[2:], axis=0), jnp.concatenate(keys[2:], axis=0), ((1,), (1,)))
+        scores.append((early, late + bias_ref[half:, half:]))
+    for sub in range(2):
+        lanes = slice(sub * 128, (sub + 1) * 128)
+        early, late = scores[sub]
+        values = [jnp.concatenate([v_ref[place[c], :, lanes], ones], axis=1) for c in range(4)]
+        top = jnp.max(early[:half], axis=1, keepdims=True)
+        raised = jnp.exp2((early[:half] - top) * SCALE_LOG2).astype(BF16)
+        top_late = jnp.max(jnp.maximum(early[half:], late), axis=1, keepdims=True)
+        raised_late = [jnp.exp2((part - top_late) * SCALE_LOG2).astype(BF16) for part in (early[half:], late)]
+        total = dot(jnp.concatenate([raised, raised_late[0]], axis=0), jnp.concatenate(values[:2], axis=0))
+        total_late = total[half:] + dot(raised_late[1], jnp.concatenate(values[2:], axis=0))
+        out_ref[:half, lanes] = (total[:half, :128] / total[:half, 128:]).astype(BF16)
+        out_ref[half:, lanes] = (total_late[:, :128] / total_late[:, 128:]).astype(BF16)
 
 
 def whole(shape):
@@ -304,14 +362,16 @@
     )(queries, owner_row, slot_row)
     recv = lax.all_to_all(send, "req", 0, 0, tiled=True)
 
-    packed = pl.pallas_call(
+    row = jax.ShapeDtypeStruct((1, SLOTS), jnp.int32)
+    packed, order, ordered_lengths = pl.pallas_call(
         pack_kernel,
-        in_specs=[whole((CHUNK, D_Q)), whole((CHUNK, D_C)), whole((64, CHUNK)), whole((1, CHUNK)), whole((32, 1)), anywhere()],
-        out_specs=whole((CHUNK, PACK)),
-        out_shape=jax.ShapeDtypeStruct((CHUNK, PACK), BF16),
+        in_specs=[whole((CHUNK, D_Q)), whole((CHUNK, D_C)), whole((64, CHUNK)), whole((1, CHUNK)), whole((32, 1)),
+                  whole((1, SLOTS)), anywhere()],
+        out_specs=[whole((CHUNK, PACK)), whole((1, SLOTS)), whole((1, SLOTS))],
+        out_shape=[jax.ShapeDtypeStruct((CHUNK, PACK), BF16), row, row],
         compiler_params=params(60),
         name="pack",
-    )(x, latents, rotary_keys, positions.reshape(1, CHUNK), freq, send)
+    )(x, latents, rotary_keys, positions.reshape(1, CHUNK), freq, lengths.reshape(1, SLOTS), send)
     right = lax.ppermute(packed, "head", [(i, (i + 3) % 4) for i in range(4)])
     left = lax.ppermute(packed, "head", [(i, (i + 1) % 4) for i in range(4)])
     far = lax.ppermute(packed, "head", [(i, (i + 2) % 4) for i in range(4)])
@@ -319,26 +379,24 @@
 
     returned = pl.pallas_call(
         decode_kernel,
-        grid=(SLOTS // SLOTS_PER_STEP,),
-        in_specs=[
-            whole((PEERS * 2 * MOST, SEND)),
-            whole((D_C, HEADS * D_NOPE)),
-            whole((D_C, HEADS * D_V)),
-            pl.BlockSpec((SLOTS_PER_STEP, CMAX, D_C), lambda i: (i, 0, 0)),
-            pl.BlockSpec((SLOTS_PER_STEP, D_ROPE, CMAX), lambda i: (i, 0, 0)),
-            smem(),
-            anywhere(),
-        ],
+        in_specs=[anywhere()] * 5 + [smem(), smem(), whole((1, SLOTS)), anywhere()],
         out_specs=whole((PEERS * 2 * MOST, RET)),
         out_shape=jax.ShapeDtypeStruct((PEERS * 2 * MOST, RET), BF16),
         scratch_shapes=[
-            pltpu.VMEM((4, HEADS * SLOTS, 128), F32),
-            pltpu.VMEM((HEADS * SLOTS, 128), F32),
-            pltpu.VMEM((4, HEADS * SLOTS, 128), F32),
+            pltpu.VMEM((PEERS * 2 * MOST, SEND), BF16),
+            pltpu.VMEM((D_C, HEADS * D_NOPE), BF16),
+            pltpu.VMEM((SLOTS, CMAX, D_C), BF16),
+            pltpu.VMEM((SLOTS, D_ROPE, CMAX), BF16),
+            pltpu.VMEM((D_C, HEADS * D_V), BF16),
+            pltpu.VMEM((HEADS, SLOTS, D_C), F32),
+            pltpu.VMEM((HEADS, SLOTS, 128), F32),
+            pltpu.VMEM((HEADS, SLOTS, D_C), F32),
+            pltpu.SemaphoreType.DMA((4,)),
+            pltpu.SemaphoreType.DMA((SECTIONS,)),
         ],
         compiler_params=params(60),
         name="decode",
-    )(recv, wk, wv, cache, cache_rope, lengths, own[4])
+    )(recv, wk, cache, cache_rope, wv, order.reshape(SLOTS), ordered_lengths.reshape(SLOTS), order, own[4])
 
     qn, qr, keys, values, key_rope = project(
         3, project_rest_kernel, (right, far, left), freq, wq, wk, wv, own, (returned,))

time: 81 us -> 75.6 us (0.933)
  Pallas kernels: 55.3 us -> 49.2 us
    pallas_call x1, Pallas kernels: 17.2 us -> 12.6 us  [on_device(): pl.pallas_call(decode_kernel, in_specs=[anywhere()] * 5 + [smem(), smem()...]
    pallas_call x1, Pallas kernels: 12.2 us -> 10.6 us  [on_device(): pl.pallas_call(attention_kernel, grid=(HEADS // 2,), in_specs=[smem(), pl...]
  transfers between devices with their start and end apart: 5 -> 5, of which waited for: 1 -> 1; matrix products, arithmetic and copies ran while one was open for 0% -> 0% of each run, Pallas kernels for 63% -> 60%
where the time goes in v3:
time: 75.6 us; the launch traced here: 74.4 us
  Pallas kernels  49.2 us (65%)
  starting transfers between devices  20.7 us (27%)
  local copies, waits for them, and re-layouts  2.86 us (4%)
  waiting for transfers between devices  0.93 us (1%)
    pallas_call x2, Pallas kernels, project(): pl.pallas_call(kernel, grid=(HEADS // GROUP,), in_specs=[whole((CHUNK, PA...  19.1 us
    pallas_call x1, Pallas kernels, on_device(): pl.pallas_call(decode_kernel, in_specs=[anywhere()] * 5 + [smem(), smem()...  12.6 us
    pallas_call x1, Pallas kernels, on_device(): pl.pallas_call(attention_kernel, grid=(HEADS // 2,), in_specs=[smem(), pl...  10.6 us
    all_to_all x1, starting transfers between devices, on_device(): recv = lax.all_to_all(send, 'req', 0, 0, tiled=True)  9.43 us
    all_to_all x1, starting transfers between devices, on_device(): returned = lax.all_to_all(returned, 'req', 0, 0, tiled=True)  7.47 us
    unnamed x10, local copies, waits for them, and re-layouts  2.86 us
    ppermute x1, starting transfers between devices, on_device(): right = lax.ppermute(packed, 'head', [(i, (i + 3) % 4) for i in range(4)])  2.73 us
    pallas_call x1, Pallas kernels, on_device(): pl.pallas_call(place_kernel, out_shape=jax.ShapeDtypeStruct((PEERS * 2 *...  2.44 us
  transfers between devices with their start and end apart: 5, of which 1 were waited for; matrix products, arithmetic and copies ran while one was open for 0% of the time, Pallas kernels for 60%

profile of v3, /device:TPU:1, one launch (start us, length us, event | category | flops | bytes accessed | tf_op | source)
XLA Modules:
  0.0 74.4 jit_solution(16908355309132566488)
XLA Ops:
  0.6 2.4 %place.1.after_ref = bf16[256,1664]{1,0:T(8,128)(2,1)} custom-call(bf16[64,3072]{1,0:T(8,128)(2,1)} %q_ref.1, s32[1,64]{1,0:T(1,128)} %bitcast.16, s32[1,64]{1,0:T(1,128)} %bitcast.18), custom_call_target="tpu_custom_call" | custom-call | tf_op jit(solution)/shard_map/place/pallas_call | solution.py:357
  3.1 9.4 %all-to-all-start = ((bf16[32,8,1664]{2,1,0:T(8,128)(2,1)}), bf16[32,8,1664]{2,1,0:T(8,128)(2,1)S(1)}, u32[]{:S(2)}, u32[]{:S(2)}) async-start(bf16[32,8,1664]{2,1,0:T(8,128)(2,1)} %bitcast.11), calls=%async_computation | async-start | bytes 1703936 | tf_op jit(solution)/shard_map/all_to_all | solution.py:363
  12.5 2.2 %pack.1 = (bf16[128,2176]{1,0:T(8,128)(2,1)}, s32[1,64]{1,0:T(1,128)}, s32[1,64]{1,0:T(1,128)}) custom-call(bf16[128,1536]{1,0:T(8,128)(2,1)} %x_ref.1, bf16[128,512]{1,0:T(8,128)(2,1)} %l_ref.1, bf16[64,128]{1,0:T(8,128)(2,1)} %rk_ref.1, s32[1,128]{1,0:T(1,128)} %bitcast.19, f32[32,1]{1,0:T(8,128)} %constant.7.freq_ref, s32[1,64]{1,0:T(1,128)} %bitcast.20, ...), custom_call_target="tpu_custom_call" | custom-call | tf_op jit(solution)/shard_map/pack/pallas_call | solution.py:366
  14.7 2.7 %collective-permute-start = (bf16[128,2176]{1,0:T(8,128)(2,1)}, bf16[128,2176]{1,0:T(8,128)(2,1)S(1)}, u32[]{:S(2)}, u32[]{:S(2)}) collective-permute-start(bf16[128,2176]{1,0:T(8,128)(2,1)} %get-tuple-element.15.own_ref), channel_id=1, source_target_pairs={{0,3},{1,0},{2,1},{3,2},{4,7},{5,4},{6,5},{7,6},{8,11},{9,8},{10,9... | collective-permute-start | bytes 1671176 | tf_op jit(solution)/shard_map/ppermute | solution.py:375
  17.4 0.4 collective-permute-start.1
  17.8 0.7 collective-permute-start.2
  18.5 8.0 %project_own.1 = (bf16[4,128,2048]{2,1,0:T(8,128)(2,1)}, bf16[4,128,1024]{2,1,0:T(8,128)(2,1)}, bf16[4,128,2048]{2,1,0:T(8,128)(2,1)}, bf16[4,128,2048]{2,1,0:T(8,128)(2,1)}, bf16[4,128,128]{2,1,0:T(8,128)(2,1)}) custom-call(bf16[128,2176]{1,0:T(8,128)(2,1)} %get-tuple-element.15.own_ref, f32[32,1]{1,0:T(8,128)} %constant.7.freq_ref, ...), custom_call_target="tpu_custom_call" | custom-call | tf_op jit(solution)/shard_map/project_own/pallas_call | solution.py:329
  26.4 0.9 %all-to-all-done = bf16[32,8,1664]{2,1,0:T(8,128)(2,1)S(1)} async-done(((bf16[32,8,1664]{2,1,0:T(8,128)(2,1)}), bf16[32,8,1664]{2,1,0:T(8,128)(2,1)S(1)}, u32[]{:S(2)}, u32[]{:S(2)}) %all-to-all-start) | async-done | bytes 852000 | tf_op jit(solution)/shard_map/all_to_all | solution.py:363
  27.4 0.0 copy-start
  27.4 0.9 %copy-done = bf16[32,8,1664]{2,1,0:T(8,128)(2,1)} copy-done((bf16[32,8,1664]{2,1,0:T(8,128)(2,1)}, bf16[32,8,1664]{2,1,0:T(8,128)(2,1)S(1)}, u32[]{:S(2)}) %copy-start) | copy-done | bytes 851992
  28.3 12.6 %decode.1.after = bf16[256,1024]{1,0:T(8,128)(2,1)} custom-call(bf16[256,1664]{1,0:T(8,128)(2,1)} %bitcast.13, bf16[512,2048]{1,0:T(8,128)(2,1)} %wk_ref.3, bf16[64,256,512]{2,1,0:T(8,128)(2,1)} %lat_hbm.1, bf16[64,64,256]{2,1,0:T(8,128)(2,1)} %rk_hbm.1, bf16[512,2048]{1,0:T(8,128)(2,1)} %wv_ref.3, s32[64]{0:T(128)} %bitcast.15, s32[64]{0:T(128)} %bitcast.21, ...), custom_call_target="tpu_custom_call" | custom-call | tf_op jit(solution)/shard_map/decode/pallas_call | solution.py:380
  40.9 7.5 %all-to-all-start.1 = ((bf16[32,8,1024]{2,1,0:T(8,128)(2,1)}), bf16[32,8,1024]{2,1,0:T(8,128)(2,1)S(1)}, u32[]{:S(2)}, u32[]{:S(2)}) async-start(bf16[32,8,1024]{2,1,0:T(8,128)(2,1)} %bitcast.12), calls=%async_computation.1 | async-start | bytes 1048576 | tf_op jit(solution)/shard_map/all_to_all | solution.py:403
  48.4 0.0 collective-permute-done.right_ref
  48.4 0.0 copy-start.2
  48.4 0.0 collective-permute-done.1.far_ref
  48.4 0.0 copy-start.3
  48.4 0.0 collective-permute-done.2.left_ref
  48.4 0.0 copy-start.4
  48.4 0.8 %copy-done.2 = bf16[128,2176]{1,0:T(8,128)(2,1)} copy-done((bf16[128,2176]{1,0:T(8,128)(2,1)}, bf16[128,2176]{1,0:T(8,128)(2,1)S(1)}, u32[]{:S(2)}) %copy-start.2) | copy-done | bytes 557080
  49.2 0.2 copy-done.3
  49.4 0.2 copy-done.4
  49.6 11.2 %project_rest.1 = (bf16[4,128,2048]{2,1,0:T(8,128)(2,1)}, bf16[4,128,1024]{2,1,0:T(8,128)(2,1)}, bf16[4,128,2048]{2,1,0:T(8,128)(2,1)}, bf16[4,128,2048]{2,1,0:T(8,128)(2,1)}, bf16[4,128,128]{2,1,0:T(8,128)(2,1)}) custom-call(bf16[128,2176]{1,0:T(8,128)(2,1)} %copy-done.2, ...), custom_call_target="tpu_custom_call", output_to_operand_aliasing={{0}: (7, {}), {1}: (8, {}), {2}: (9, {}), {3}: (10, {}), {4... | custom-call | tf_op jit(solution)/shard_map/project_rest/pallas_call | solution.py:329
  60.8 10.6 %attention.1 = bf16[512,2048]{1,0:T(8,128)(2,1)} custom-call(s32[1]{0:T(128)} %bitcast.head_ref, bf16[4,128,2048]{2,1,0:T(8,128)(2,1)} %get-tuple-element.23.qn_ref, bf16[4,128,1024]{2,1,0:T(8,128)(2,1)} %get-tuple-element.24.qr_ref, bf16[4,128,2048]{2,1,0:T(8,128)(2,1)} %get-tuple-element.25.k_ref, bf16[4,128,2048]{2,1,0:T(8,128)(2,1)} %get-tuple-element.26.v_ref, ...), custom_call_target="tpu_custom_call" | custom-call | tf_op jit(solution)/shard_map/attention/pallas_call | solution.py:405
  71.4 0.0 all-to-all-done.1
  71.4 0.0 copy-start.1
  71.4 0.8 %copy-done.1 = bf16[32,8,1024]{2,1,0:T(8,128)(2,1)} copy-done((bf16[32,8,1024]{2,1,0:T(8,128)(2,1)}, bf16[32,8,1024]{2,1,0:T(8,128)(2,1)S(1)}, u32[]{:S(2)}) %copy-start.1) | copy-done | bytes 524312
  72.2 2.2 %unplace.1 = bf16[64,2048]{1,0:T(8,128)(2,1)} custom-call(bf16[256,1024]{1,0:T(8,128)(2,1)} %bitcast.14, s32[1,64]{1,0:T(1,128)} %bitcast.17), custom_call_target="tpu_custom_call" | custom-call | tf_op jit(solution)/shard_map/unplace/pallas_call | solution.py:426
Async XLA Ops:
  3.1 24.3 %all-to-all-start = ((bf16[32,8,1664]{2,1,0:T(8,128)(2,1)}), bf16[32,8,1664]{2,1,0:T(8,128)(2,1)S(1)}, u32[]{:S(2)}, u32[]{:S(2)}) async-start(bf16[32,8,1664]{2,1,0:T(8,128)(2,1)} %bitcast.11), calls=%async_computation | async-start | bytes 1703936 | tf_op jit(solution)/shard_map/all_to_all | solution.py:363
  14.7 33.7 %collective-permute-start = (bf16[128,2176]{1,0:T(8,128)(2,1)}, bf16[128,2176]{1,0:T(8,128)(2,1)S(1)}, u32[]{:S(2)}, u32[]{:S(2)}) collective-permute-start(bf16[128,2176]{1,0:T(8,128)(2,1)} %get-tuple-element.15.own_ref), channel_id=1, source_target_pairs={{0,3},{1,0},{2,1},{3,2},{4,7},{5,4},{6,5},{7,6},{8,11},{9,8},{10,9... | collective-permute-start | bytes 1671176 | tf_op jit(solution)/shard_map/ppermute | solution.py:375
  17.4 30.9 %collective-permute-start.1 = (bf16[128,2176]{1,0:T(8,128)(2,1)}, bf16[128,2176]{1,0:T(8,128)(2,1)S(1)}, u32[]{:S(2)}, u32[]{:S(2)}) collective-permute-start(bf16[128,2176]{1,0:T(8,128)(2,1)} %get-tuple-element.15.own_ref), channel_id=1, source_target_pairs={{0,2},{1,3},{2,0},{3,1},{4,6},{5,7},{6,4},{7,5},{8,10},{9,11},{10,... | collective-permute-start | bytes 1671176 | tf_op jit(solution)/shard_map/ppermute | solution.py:377
  17.8 30.6 %collective-permute-start.2 = (bf16[128,2176]{1,0:T(8,128)(2,1)}, bf16[128,2176]{1,0:T(8,128)(2,1)S(1)}, u32[]{:S(2)}, u32[]{:S(2)}) collective-permute-start(bf16[128,2176]{1,0:T(8,128)(2,1)} %get-tuple-element.15.own_ref), channel_id=1, source_target_pairs={{0,1},{1,2},{2,3},{3,0},{4,5},{5,6},{6,7},{7,4},{8,9},{9,10},{10,1... | collective-permute-start | bytes 1671176 | tf_op jit(solution)/shard_map/ppermute | solution.py:376
  27.4 0.9 %copy-start = (bf16[32,8,1664]{2,1,0:T(8,128)(2,1)}, bf16[32,8,1664]{2,1,0:T(8,128)(2,1)S(1)}, u32[]{:S(2)}) copy-start(bf16[32,8,1664]{2,1,0:T(8,128)(2,1)S(1)} %all-to-all-done) | copy-start | bytes 2555908
  40.9 30.5 %all-to-all-start.1 = ((bf16[32,8,1024]{2,1,0:T(8,128)(2,1)}), bf16[32,8,1024]{2,1,0:T(8,128)(2,1)S(1)}, u32[]{:S(2)}, u32[]{:S(2)}) async-start(bf16[32,8,1024]{2,1,0:T(8,128)(2,1)} %bitcast.12), calls=%async_computation.1 | async-start | bytes 1048576 | tf_op jit(solution)/shard_map/all_to_all | solution.py:403
  48.4 0.8 %copy-start.2 = (bf16[128,2176]{1,0:T(8,128)(2,1)}, bf16[128,2176]{1,0:T(8,128)(2,1)S(1)}, u32[]{:S(2)}) copy-start(bf16[128,2176]{1,0:T(8,128)(2,1)S(1)} %collective-permute-done.right_ref) | copy-start | bytes 1671172
  48.4 1.0 %copy-start.3 = (bf16[128,2176]{1,0:T(8,128)(2,1)}, bf16[128,2176]{1,0:T(8,128)(2,1)S(1)}, u32[]{:S(2)}) copy-start(bf16[128,2176]{1,0:T(8,128)(2,1)S(1)} %collective-permute-done.1.far_ref) | copy-start | bytes 1671172
  48.4 1.2 %copy-start.4 = (bf16[128,2176]{1,0:T(8,128)(2,1)}, bf16[128,2176]{1,0:T(8,128)(2,1)S(1)}, u32[]{:S(2)}) copy-start(bf16[128,2176]{1,0:T(8,128)(2,1)S(1)} %collective-permute-done.2.left_ref) | copy-start | bytes 1671172
  71.4 0.8 %copy-start.1 = (bf16[32,8,1024]{2,1,0:T(8,128)(2,1)}, bf16[32,8,1024]{2,1,0:T(8,128)(2,1)S(1)}, u32[]{:S(2)}) copy-start(bf16[32,8,1024]{2,1,0:T(8,128)(2,1)S(1)} %all-to-all-done.1) | copy-start | bytes 1572868

commit v4 on v3

v4 whole, which is shorter than its diff:
```python
import math

import jax
import jax.numpy as jnp
from jax import lax
from jax.experimental import pallas as pl
from jax.experimental.pallas import tpu as pltpu
from jax.sharding import PartitionSpec as P

D_C = 512
D_NOPE = 128
D_ROPE = 64
D_V = 128
D_Q = 1536
HEADS = 16
TOKENS = 512
CHUNK = 128
ROWS = 64
MOST = 4
SLOTS = 64
CMAX = 256
PEERS = 32
PACK = D_Q + D_C + 128
SEND = 1536 + 128
RET = 1024
ROPE_BASE = 10000.0
SCALE = (D_NOPE + D_ROPE) ** -0.5
SCALE_LOG2 = SCALE * math.log2(math.e)
MASKED = -1e30
F32 = jnp.float32
BF16 = jnp.bfloat16
MIB = 1024 * 1024


def iota(shape, dim):
    return lax.broadcasted_iota(jnp.int32, shape, dim)


def dot(a, b, dims=((1,), (0,))):
    return lax.dot_general(a, b, (dims, ((), ())), preferred_element_type=F32)


def frequencies():
    return jnp.exp(iota((32, 128), 0).astype(F32) * (-math.log(ROPE_BASE) / 32.0))[:, :1]


def column_of(row):
    n = row.shape[1]
    eye = iota((n, n), 0) == iota((n, n), 1)
    return jnp.sum(jnp.where(eye, row, 0), axis=1, keepdims=True)


def pack_kernel(x_ref, l_ref, rk_ref, pos_ref, len_ref, after_ref, packed_ref, order_ref, sorted_ref):
    packed_ref[:, :D_Q] = x_ref[...]
    packed_ref[:, D_Q:D_Q + D_C] = l_ref[...]
    pos = pos_ref[...]
    angle = pos.astype(F32) * frequencies()
    cos, sin = jnp.cos(angle), jnp.sin(angle)
    keys = rk_ref[...].astype(F32)
    first, second = keys[:32], keys[32:]
    high = (pos >> 4).astype(F32)
    low = (pos & 15).astype(F32)
    place = iota((64, CHUNK), 0)
    tail = jnp.where(place == 0, high, jnp.where(place == 1, low, 0.0))
    block = jnp.concatenate([first * cos - second * sin, first * sin + second * cos, tail], axis=0)
    packed_ref[:, D_Q + D_C:] = block.T.astype(BF16)

    length = len_ref[...]
    length_col = column_of(length)
    this, other = iota((SLOTS, SLOTS), 0), iota((SLOTS, SLOTS), 1)
    ahead = (length < length_col) | ((length == length_col) & (other < this))
    rank = jnp.sum(jnp.where(ahead, 1, 0), axis=1, keepdims=True)
    order_ref[...] = jnp.sum(jnp.where(rank == other, this, 0), axis=0, keepdims=True)
    sorted_ref[...] = jnp.sum(jnp.where(rank == other, length_col, 0), axis=0, keepdims=True)


def place_kernel(q_ref, owner_ref, slot_ref, send_ref):
    owner = owner_ref[...]
    owner_col = column_of(owner)
    same = owner_col == owner
    before = iota((ROWS, ROWS), 0) < iota((ROWS, ROWS), 1)
    rank = jnp.sum(jnp.where(same & before, 1, 0), axis=0, keepdims=True)
    target = owner * (2 * MOST) + rank
    target = jnp.concatenate([target, target + MOST], axis=1)
    placing = iota((PEERS * 2 * MOST, 2 * ROWS), 0) == target
    queries = jnp.concatenate([q_ref[:, :1536], q_ref[:, 1536:]], axis=0)
    send_ref[:, :1536] = dot(placing.astype(BF16), queries).astype(BF16)
    slot = slot_ref[...] + 1
    slot = jnp.concatenate([slot, slot], axis=1)
    slot_col = jnp.sum(jnp.where(placing, slot, 0), axis=1, keepdims=True)
    send_ref[:, 1536:] = jnp.broadcast_to(slot_col.astype(F32), (PEERS * 2 * MOST, 128)).astype(BF16)


def split_pair(three):
    low_lane = iota((three.shape[0], 128), 1) < 64
    second, third = three[:, 128:256], three[:, 256:]
    rotary = jnp.where(low_lane, second, third)
    odd = pltpu.roll(jnp.where(low_lane, third, second), 64, 1)
    return three[:, :128], odd, rotary


TOGETHER = 8
WIDE = TOGETHER * HEADS
SECTION = 16
SECTIONS = SLOTS // SECTION
WIDTHS = (64, 128, 192, 256)


def decode_kernel(recv_ref, kup_hbm, lat_hbm, rk_hbm, vup_hbm, order_hbm, order_ref, len_ref, after_ref, out_ref,
                  kup_ref, rk_ref, vup_ref, order_row_ref, lat_ref, lq_ref, qr_ref, lo_ref, sems, lat_sems):
    rows = PEERS * 2 * MOST
    order_copy, kup_copy, rk_copy, vup_copy = [
        pltpu.make_async_copy(src, dst, sems.at[i]) for i, (src, dst) in enumerate(
            ((order_hbm, order_row_ref), (kup_hbm, kup_ref), (rk_hbm, rk_ref), (vup_hbm, vup_ref)))]

    def of_width(section, width):
        longest = len_ref[section * SECTION + SECTION - 1]
        return (longest <= width) & (longest > width - 64)

    def fetch(section, width, i):
        place = section * SECTION + i
        return pltpu.make_async_copy(
            lat_hbm.at[order_ref[place], pl.ds(0, width)], lat_ref.at[place, pl.ds(0, width)], lat_sems.at[section])

    def start(section):
        for width in WIDTHS:
            @pl.when(of_width(section, width))
            def _():
                for i in range(SECTION):
                    fetch(section, width, i).start()

    order_copy.start()
    kup_copy.start()
    start(0)
    rk_copy.start()

    def place_onehot():
        slot_col = recv_ref[:, 1536:].astype(jnp.int32)
        hit = slot_col[:, :SLOTS] == order_row_ref[...] + 1
        half = (iota((rows, SLOTS), 0) & 7) < MOST
        return hit & half, hit & jnp.logical_not(half)

    order_copy.wait()
    first, second = place_onehot()
    blank = jnp.zeros((SLOTS, 128), BF16)
    low_lane = iota((SLOTS, 128), 1) < 64
    spreads = [jnp.concatenate([jnp.where(hit, 1.0, 0.0), jnp.zeros((rows, 64), F32)], axis=1).T[:SLOTS].astype(BF16)
               for hit in (first, second)]
    queries = [dot(spread, recv_ref[:, :1536]) for spread in spreads]
    kup_copy.wait()
    start(1)
    for side in range(2):
        for pair in range(4):
            head = side * 8 + pair * 2
            even, odd, rotary = split_pair(queries[side][:, pair * 384:(pair + 1) * 384])
            both = jnp.concatenate([jnp.concatenate([even.astype(BF16), blank], axis=1),
                                    jnp.concatenate([blank, odd.astype(BF16)], axis=1)], axis=0)
            latent = dot(both, kup_ref[:, head * 128:(head + 2) * 128], ((1,), (1,)))
            lq_ref[head:head + 2] = latent.astype(BF16).astype(F32).reshape(2, SLOTS, D_C)
            turned = pltpu.roll(rotary, 64, 1)
            qr_ref[head] = jnp.where(low_lane, rotary, turned)
            qr_ref[head + 1] = jnp.where(low_lane, turned, rotary)
    rk_copy.wait()
    start(2)

    def attend(section, width):
        @pl.loop(0, SECTION)
        def _(i):
            fetch(section, width, i).wait()

        row, lane = iota((WIDE, WIDE), 0), iota((WIDE, WIDE), 1)
        by_place = jnp.where(lane == (row & 15) * TOGETHER + (row >> 4), 1.0, 0.0).astype(BF16)
        by_head = jnp.where(row == (lane & 15) * TOGETHER + (lane >> 4), 1.0, 0.0).astype(BF16)
        row_place = iota((WIDE, 1), 0) >> 4
        starts = [pl.multiple_of(section * SECTION + group * TOGETHER, TOGETHER) for group in range(SECTION // TOGETHER)]
        queries = []
        for start in starts:
            latent = lq_ref[:, pl.ds(start, TOGETHER), :].reshape(WIDE, D_C).astype(BF16)
            rotary = qr_ref[:, pl.ds(start, TOGETHER), :].reshape(WIDE, 128).astype(BF16)
            queries.append((dot(by_place, latent).astype(BF16), dot(by_place, rotary).astype(BF16)))
        scores = []
        for start, (latent, rotary) in zip(starts, queries):
            score = []
            length = jnp.full((WIDE, 1), len_ref[start], jnp.int32)
            for i in range(TOGETHER):
                mine = slice(i * HEADS, (i + 1) * HEADS)
                score.append(dot(latent[mine], lat_ref[start + i, :width], ((1,), (1,)))
                             + dot(rotary[mine, :D_ROPE], rk_ref[order_ref[start + i], :, :width]))
                length = jnp.where(row_place == i, len_ref[start + i], length)
            score = jnp.concatenate(score, axis=0)
            scores.append(jnp.where(iota((WIDE, width), 1) < length, score * SCALE, MASKED))
        for start, score in zip(starts, scores):
            raised = jnp.exp(score - jnp.max(score, axis=1, keepdims=True))
            weights = (raised * (1.0 / jnp.sum(raised, axis=1, keepdims=True))).astype(BF16)
            total = jnp.concatenate(
                [dot(weights[i * HEADS:(i + 1) * HEADS], lat_ref[start + i, :width]).astype(BF16)
                 for i in range(TOGETHER)], axis=0)
            lo_ref[:, pl.ds(start, TOGETHER), :] = dot(by_head, total).reshape(HEADS, TOGETHER, D_C)

    @pl.loop(0, SECTIONS)
    def _(section):
        @pl.when(section == 0)
        def _():
            start(SECTIONS - 1)
            vup_copy.start()

        for width in WIDTHS:
            @pl.when(of_width(section, width))
            def _():
                attend(section, width)

    vup_copy.wait()
    outs = []
    for head in range(0, HEADS, 2):
        latent_out = lo_ref[head:head + 2].reshape(2 * SLOTS, D_C).astype(BF16)
        both = dot(latent_out, vup_ref[:, head * 128:(head + 2) * 128])
        outs += [both[:SLOTS, :128].astype(BF16), both[SLOTS:, 128:].astype(BF16)]
    outs = jnp.concatenate([jnp.concatenate(outs[:8], axis=1), jnp.concatenate(outs[8:], axis=1)], axis=0)
    first, second = place_onehot()
    spread = jnp.concatenate([jnp.where(first, 1.0, 0.0), jnp.where(second, 1.0, 0.0)], axis=1)
    out_ref[...] = dot(spread.astype(BF16), outs).astype(BF16)


def unplace_kernel(ret_ref, owner_ref, out_ref):
    owner = owner_ref[...]
    owner_col = column_of(owner)
    before = iota((ROWS, ROWS), 1) < iota((ROWS, ROWS), 0)
    rank = jnp.sum(jnp.where((owner_col == owner) & before, 1, 0), axis=1, keepdims=True)
    target = owner_col * (2 * MOST) + rank
    lane = iota((ROWS, PEERS * 2 * MOST), 1)
    for side in range(2):
        spread = jnp.where(lane == target + side * MOST, 1.0, 0.0).astype(BF16)
        out_ref[:, side * RET:(side + 1) * RET] = dot(spread, ret_ref[...]).astype(BF16)


GROUP = 4


GROUPS = HEADS // GROUP


def fetch_weights(group, sources, buffers, sems):
    return [pltpu.make_async_copy(
        src.at[:, pl.ds(pl.multiple_of(group * width, 128), width)], dst.at[group], sems.at[i, group])
        for i, (src, dst, width) in enumerate(zip(sources, buffers, (GROUP * 192, GROUP * 128, GROUP * 128)))]


def rope_tables(extra):
    turned = extra.astype(F32).T
    pos = turned[64:65] * 16.0 + turned[65:66]
    angle = pos * frequencies()
    cos, sin = jnp.cos(angle), jnp.sin(angle)
    return (jnp.concatenate([cos, cos, cos, cos], axis=0).T, jnp.concatenate([-sin, sin, -sin, sin], axis=0).T)


def rotated(rotary, cos, sin):
    lane = iota(rotary.shape, 1) & 63
    swapped = jnp.where(lane < 32, pltpu.roll(rotary, 96, 1), pltpu.roll(rotary, 32, 1))
    return (rotary * cos + swapped * sin).astype(BF16)


def own_kernel(x_ref, wq_hbm, wk_hbm, wv_hbm,
               qn_ref, qr_ref, k_ref, v_ref, wq_ref, wk_ref, wv_ref, cos_ref, sin_ref, sems):
    def fetch(group):
        return fetch_weights(group, (wq_hbm, wk_hbm, wv_hbm), (wq_ref, wk_ref, wv_ref), sems)

    for group in range(GROUPS):
        for copy in fetch(group):
            copy.start()
    cos_ref[...], sin_ref[...] = rope_tables(x_ref[:, D_Q + D_C:])

    @pl.loop(0, GROUPS)
    def _(group):
        for copy in fetch(group):
            copy.wait()
        queries = dot(x_ref[:, :D_Q], wq_ref[group])
        for pair in range(GROUP // 2):
            even, odd, rotary = split_pair(queries[:, pair * 384:(pair + 1) * 384])
            qn_ref[group, :, pair * 256:pair * 256 + 128] = even.astype(BF16)
            qn_ref[group, :, pair * 256 + 128:pair * 256 + 256] = odd.astype(BF16)
            qr_ref[group, :, pair * 128:(pair + 1) * 128] = rotated(rotary, cos_ref[...], sin_ref[...])
        latents = x_ref[:, D_Q:D_Q + D_C]
        k_ref[group] = dot(latents, wk_ref[group]).astype(BF16)
        v_ref[group] = dot(latents, wv_ref[group]).astype(BF16)


def prefill_kernel(head_ref, right_ref, far_ref, left_ref, own_hbm, wq_hbm, wk_hbm, wv_hbm,
                   own_qn_hbm, own_qr_hbm, own_k_hbm, own_v_hbm, after_ref, out_hbm,
                   own_ref, all_wq_ref, all_wk_ref, all_wv_ref, all_out_ref, chunk_sem, weight_sems, own_sems, out_sems,
                   cos_ref, sin_ref, bias_ref, pair_ref, *sets):
    me = head_ref[0]
    place = [(c - me + 3) & 3 for c in range(4)]
    half = TOKENS // 2
    sets = (sets[:4], sets[4:])
    others = (right_ref, far_ref, left_ref)
    shared_copy = pltpu.make_async_copy(own_hbm.at[:, pl.ds(D_Q + D_C, 128)], own_ref, chunk_sem)

    def fetch(group):
        return fetch_weights(group, (wq_hbm, wk_hbm, wv_hbm), (all_wq_ref, all_wk_ref, all_wv_ref), weight_sems)

    def fetch_own(group, into, parity):
        return [pltpu.make_async_copy(src.at[group], dst.at[3], own_sems.at[i, parity])
                for i, (src, dst) in enumerate(zip((own_qn_hbm, own_qr_hbm, own_k_hbm, own_v_hbm), into))]

    def send_out(group):
        return pltpu.make_async_copy(
            all_out_ref.at[group], out_hbm.at[:, pl.ds(pl.multiple_of(group * GROUP * 128, 128), GROUP * 128)],
            out_sems.at[group])

    def prepare():
        extras = [ref[:, D_Q + D_C:] for ref in others] + [own_ref[...]]
        cos_ref[...], sin_ref[...] = rope_tables(jnp.concatenate(extras[:3], axis=0))
        low_lane = iota((CHUNK, 128), 1) < 64
        for slot, extra in enumerate(extras):
            extra = extra.astype(F32)
            pos = (extra[:, 64:65] * 16.0 + extra[:, 65:66]).astype(jnp.int32)
            chunk = (slot + 1 + me) & 3
            query, key = iota((CHUNK, TOKENS), 0) + chunk * CHUNK, iota((CHUNK, TOKENS), 1)
            bias_ref[chunk] = jnp.where((key <= query) & (key >= query - pos), 0.0, MASKED)
            keep = jnp.where(low_lane, extra, 0.0)
            pair_ref[0, chunk] = keep.astype(BF16)
            pair_ref[1, chunk] = pltpu.roll(keep, 64, 1).astype(BF16)

    def project_steps(into, group):
        qn_ref, qr_ref, k_ref, v_ref = into
        wq_ref, wk_ref, wv_ref = all_wq_ref.at[group], all_wk_ref.at[group], all_wv_ref.at[group]
        rows = 3 * CHUNK
        shape = (3, CHUNK, 128)
        held = []

        def query(first, width):
            x = jnp.concatenate([ref[:, :D_Q] for ref in others], axis=0)
            held.append(dot(x, wq_ref[:, first:first + width]))

        def turn(pair):
            even, odd, rotary = split_pair(jnp.concatenate(held, axis=1)[:, pair * 384:(pair + 1) * 384])
            qn_ref[:3, :, pair * 256:pair * 256 + 128] = even.astype(BF16).reshape(shape)
            qn_ref[:3, :, pair * 256 + 128:pair * 256 + 256] = odd.astype(BF16).reshape(shape)
            qr_ref[:3, :, pair * 128:(pair + 1) * 128] = rotated(rotary, cos_ref[...], sin_ref[...]).reshape(shape)

        def latent(which):
            w_ref, to_ref = ((wk_ref, k_ref), (wv_ref, v_ref))[which - 1]
            x = jnp.concatenate([ref[:, D_Q:D_Q + D_C] for ref in others], axis=0)
            to_ref[:3] = dot(x, w_ref[...]).astype(BF16).reshape(3, CHUNK, GROUP * 128)

        return query, turn, latent

    def attend_steps(source, group):
        qn_ref, qr_ref, k_ref, v_ref = source
        out_ref = all_out_ref.at[group]
        ones = jnp.ones((CHUNK, 128), BF16)
        scores = {}

        def score(head):
            lanes = slice(head * 128, (head + 1) * 128)
            pair = slice(head // 2 * 128, (head // 2 + 1) * 128)
            query = [jnp.concatenate([qn_ref[place[c], :, lanes], qr_ref[place[c], :, pair]], axis=1) for c in range(4)]
            keys = [jnp.concatenate([k_ref[place[c], :, lanes], pair_ref[head % 2, c]], axis=1) for c in range(4)]
            bias = bias_ref[...].reshape(TOKENS, TOKENS)
            early = dot(jnp.concatenate(query, axis=0), jnp.concatenate(keys[:2], axis=0), ((1,), (1,)))
            late = dot(jnp.concatenate(query[2:], axis=0), jnp.concatenate(keys[2:], axis=0), ((1,), (1,)))
            scores[head] = early + bias[:, :half], late + bias[half:, half:]

        def weigh(head):
            lanes = slice(head * 128, (head + 1) * 128)
            early, late = scores[head]
            values = [jnp.concatenate([v_ref[place[c], :, lanes], ones], axis=1) for c in range(4)]
            top = jnp.max(early[:half], axis=1, keepdims=True)
            raised = jnp.exp2((early[:half] - top) * SCALE_LOG2).astype(BF16)
            top_late = jnp.max(jnp.maximum(early[half:], late), axis=1, keepdims=True)
            raised_late = [jnp.exp2((part - top_late) * SCALE_LOG2).astype(BF16) for part in (early[half:], late)]
            total = dot(jnp.concatenate([raised, raised_late[0]], axis=0), jnp.concatenate(values[:2], axis=0))
            total_late = total[half:] + dot(raised_late[1], jnp.concatenate(values[2:], axis=0))
            out_ref[:half, lanes] = (total[:half, :128] / total[:half, 128:]).astype(BF16)
            out_ref[half:, lanes] = (total_late[:, :128] / total_late[:, 128:]).astype(BF16)

        return score, weigh

    def step_copies(copies, act):
        for copy in copies:
            act(copy)

    start, wait = (lambda copy: copy.start()), (lambda copy: copy.wait())
    shared_copy.start()
    step_copies(fetch(0), start)
    shared_copy.wait()
    prepare()
    step_copies(fetch(0), wait)
    step_copies(fetch(1), start)
    step_copies(fetch_own(0, sets[0], 0), start)
    query, turn, latent = project_steps(sets[0], 0)
    query(0, 512)
    query(512, 256)
    turn(0)
    latent(1)
    turn(1)
    latent(2)

    @pl.loop(1, GROUPS)
    def _(step):
        step_copies(fetch(step), wait)

        @pl.when(step < GROUPS - 1)
        def _():
            step_copies(fetch(step + 1), start)

        for parity in range(2):
            @pl.when((step & 1) == parity)
            def _():
                source, into = sets[1 - parity], sets[parity]
                step_copies(fetch_own(step, into, parity), start)
                step_copies(fetch_own(step - 1, source, 1 - parity), wait)
                score, weigh = attend_steps(source, step - 1)
                query, turn, latent = project_steps(into, step)
                score(0)
                query(0, 512)
                score(1)
                weigh(0)
                query(512, 256)
                turn(0)
                score(2)
                weigh(1)
                latent(1)
                turn(1)
                score(3)
                weigh(2)
                latent(2)
                weigh(3)
        send_out(step - 1).start()

    last = GROUPS - 1
    step_copies(fetch_own(last, sets[last % 2], last % 2), wait)
    score, weigh = attend_steps(sets[last % 2], last)
    score(0)
    for head in range(GROUP):
        if head + 1 < GROUP:
            score(head + 1)
        weigh(head)
    send_out(last).start()
    for group in range(GROUPS):
        send_out(group).wait()


def whole(shape):
    return pl.BlockSpec(shape, lambda *_: (0,) * len(shape))


def params(mib):
    return pltpu.CompilerParams(vmem_limit_bytes=mib * MIB)


def smem():
    return pl.BlockSpec(memory_space=pltpu.SMEM)


def anywhere():
    return pl.BlockSpec(memory_space=pl.ANY)


def vmem():
    return pl.BlockSpec(memory_space=pltpu.VMEM)


SETS = (GROUP * 128, GROUP * 64, GROUP * 128, GROUP * 128)


WEIGHTS = [pltpu.VMEM((GROUPS, D_Q, GROUP * 192), BF16), pltpu.VMEM((GROUPS, D_C, GROUP * 128), BF16),
           pltpu.VMEM((GROUPS, D_C, GROUP * 128), BF16)]


def project_own(packed, wq, wk, wv):
    return pl.pallas_call(
        own_kernel,
        in_specs=[vmem(), anywhere(), anywhere(), anywhere()],
        out_specs=[vmem()] * 4,
        out_shape=[jax.ShapeDtypeStruct((GROUPS, CHUNK, width), BF16) for width in SETS],
        scratch_shapes=WEIGHTS + [
            pltpu.VMEM((CHUNK, 128), F32),
            pltpu.VMEM((CHUNK, 128), F32),
            pltpu.SemaphoreType.DMA((3, GROUPS)),
        ],
        compiler_params=params(60),
        name="own",
    )(packed, wq, wk, wv)


def prefill(me, right, far, left, packed, wq, wk, wv, own, after):
    return pl.pallas_call(
        prefill_kernel,
        in_specs=[smem()] + [vmem()] * 3 + [anywhere()] * 9,
        out_specs=anywhere(),
        out_shape=jax.ShapeDtypeStruct((TOKENS, HEADS * D_V), BF16),
        scratch_shapes=[pltpu.VMEM((CHUNK, 128), BF16)] + WEIGHTS + [
            pltpu.VMEM((GROUPS, TOKENS, GROUP * 128), BF16),
            pltpu.SemaphoreType.DMA,
            pltpu.SemaphoreType.DMA((3, GROUPS)),
            pltpu.SemaphoreType.DMA((4, 2)),
            pltpu.SemaphoreType.DMA((GROUPS,)),
            pltpu.VMEM((3 * CHUNK, 128), F32),
            pltpu.VMEM((3 * CHUNK, 128), F32),
            pltpu.VMEM((4, CHUNK, TOKENS), F32),
            pltpu.VMEM((2, 4, CHUNK, 128), BF16),
        ] + [pltpu.VMEM((4, CHUNK, width), BF16) for width in SETS] * 2,
        compiler_params=params(36),
        name="prefill",
    )(me, right, far, left, pltpu.with_memory_space_constraint(packed, pltpu.HBM), wq, wk, wv,
      *(pltpu.with_memory_space_constraint(part, pltpu.HBM) for part in own), after)


def on_device(x, latents, rotary_keys, positions, wq, wk, wv, queries, owner, slot, cache, cache_rope, lengths):
    me = lax.axis_index("head").astype(jnp.int32).reshape(1)
    wq, wk, wv, cache, cache_rope = (
        pltpu.with_memory_space_constraint(array, pltpu.HBM) for array in (wq, wk, wv, cache, cache_rope))
    owner_row, slot_row = owner.reshape(1, ROWS), slot.reshape(1, ROWS)
    send = pl.pallas_call(
        place_kernel,
        out_shape=jax.ShapeDtypeStruct((PEERS * 2 * MOST, SEND), BF16),
        compiler_params=params(60),
        name="place",
    )(queries, owner_row, slot_row)
    recv = lax.all_to_all(send, "req", 0, 0, tiled=True)

    row = jax.ShapeDtypeStruct((1, SLOTS), jnp.int32)
    packed, order, ordered_lengths = pl.pallas_call(
        pack_kernel,
        in_specs=[whole((CHUNK, D_Q)), whole((CHUNK, D_C)), whole((64, CHUNK)), whole((1, CHUNK)), whole((1, SLOTS)), anywhere()],
        out_specs=[whole((CHUNK, PACK)), whole((1, SLOTS)), whole((1, SLOTS))],
        out_shape=[jax.ShapeDtypeStruct((CHUNK, PACK), BF16), row, row],
        compiler_params=params(60),
        name="pack",
    )(x, latents, rotary_keys, positions.reshape(1, CHUNK), lengths.reshape(1, SLOTS), send)
    right = lax.ppermute(packed, "head", [(i, (i + 3) % 4) for i in range(4)])
    left = lax.ppermute(packed, "head", [(i, (i + 1) % 4) for i in range(4)])
    far = lax.ppermute(packed, "head", [(i, (i + 2) % 4) for i in range(4)])
    own = project_own(packed, wq, wk, wv)

    returned = pl.pallas_call(
        decode_kernel,
        in_specs=[vmem()] + [anywhere()] * 5 + [smem(), smem(), anywhere()],
        out_specs=whole((PEERS * 2 * MOST, RET)),
        out_shape=jax.ShapeDtypeStruct((PEERS * 2 * MOST, RET), BF16),
        scratch_shapes=[
            pltpu.VMEM((D_C, HEADS * D_NOPE), BF16),
            pltpu.VMEM((SLOTS, D_ROPE, CMAX), BF16),
            pltpu.VMEM((D_C, HEADS * D_V), BF16),
            pltpu.VMEM((1, SLOTS), jnp.int32),
            pltpu.VMEM((SLOTS, CMAX, D_C), BF16),
            pltpu.VMEM((HEADS, SLOTS, D_C), F32),
            pltpu.VMEM((HEADS, SLOTS, 128), F32),
            pltpu.VMEM((HEADS, SLOTS, D_C), F32),
            pltpu.SemaphoreType.DMA((4,)),
            pltpu.SemaphoreType.DMA((SECTIONS,)),
        ],
        compiler_params=params(44),
        name="decode",
    )(recv, wk, cache, cache_rope, wv, pltpu.with_memory_space_constraint(order, pltpu.HBM), order.reshape(SLOTS),
      ordered_lengths.reshape(SLOTS), own[0])

    prompt_out = prefill(me, right, far, left, packed, wq, wk, wv, own, returned)
    returned = lax.all_to_all(returned, "req", 0, 0, tiled=True)

    decode_out = pl.pallas_call(
        unplace_kernel,
        out_shape=jax.ShapeDtypeStruct((ROWS, HEADS * D_V), BF16),
        compiler_params=params(16),
        name="unplace",
    )(returned, owner_row)
    return prompt_out, decode_out


def solution(mesh):
    placed = (
        P(("req", "head"), None),
        P(("req", "head"), None),
        P(None, ("req", "head")),
        P(("req", "head")),
        P(None, "head"),
        P(None, "head"),
        P(None, "head"),
        P("req", "head"),
        P("req"),
        P("req"),
        P("req", None, None),
        P("req", None, None),
        P("req"),
    )
    return jax.shard_map(
        on_device,
        mesh=mesh,
        in_specs=placed,
        out_specs=(P("req", "head"), P("req", "head")),
        check_vma=False,
    )
```

time: 75.6 us -> 66.5 us (0.88)
  Pallas kernels: 49.2 us -> 40.5 us
  starting transfers between devices: 20.7 us -> 23.2 us
  local copies, waits for them, and re-layouts: 2.86 us -> 1.04 us
  waiting for transfers between devices: 0.93 us -> 0.01 us
    pallas_call x4 -> x3, Pallas kernels: 42.3 us -> 34.8 us  [the longest x1 14.1 us: prefill(): pl.pallas_call(prefill_kernel, in_specs=[smem()] + [vmem()] * 3 + [anywhe...]
    ppermute x1, starting transfers between devices: 0.35 us -> 2.62 us  [on_device(): far = lax.ppermute(packed, 'head', [(i, (i + 2) % 4) for i in range(4)])]
    unnamed x10 -> x6, local copies, waits for them, and re-layouts: 2.86 us -> 1.04 us
    ppermute x1, starting transfers between devices: 2.73 us -> 1.07 us  [on_device(): right = lax.ppermute(packed, 'head', [(i, (i + 3) % 4) for i in range(4)])]
    all_to_all x1, starting transfers between devices: 7.47 us -> 8.79 us  [on_device(): returned = lax.all_to_all(returned, 'req', 0, 0, tiled=True)]
    pallas_call x1, Pallas kernels: 2.18 us -> 1.14 us  [on_device(): pl.pallas_call(unplace_kernel, out_shape=jax.ShapeDtypeStruct((ROWS, HEAD...]
    all_to_all x1, waiting for transfers between devices: 0.92 us -> 0.01 us  [on_device(): recv = lax.all_to_all(send, 'req', 0, 0, tiled=True)]
  transfers between devices with their start and end apart: 5 -> 5, of which waited for: 1 -> 0; matrix products, arithmetic and copies ran while one was open for 0% -> 0% of each run, Pallas kernels for 60% -> 56%
where the time goes in v4:
time: 66.5 us; the launch traced here: 65.6 us
  Pallas kernels  40.5 us (61%)
  starting transfers between devices  23.2 us (35%)
  local copies, waits for them, and re-layouts  1.04 us (2%)
  between operations  0.75 us (1%)
    pallas_call x1, Pallas kernels, prefill(): pl.pallas_call(prefill_kernel, in_specs=[smem()] + [vmem()] * 3 + [anywhe...  14.1 us
    pallas_call x1, Pallas kernels, on_device(): pl.pallas_call(decode_kernel, in_specs=[vmem()] + [anywhere()] * 5 + [sme...  12.7 us
    all_to_all x1, starting transfers between devices, on_device(): recv = lax.all_to_all(send, 'req', 0, 0, tiled=True)  9.43 us
    all_to_all x1, starting transfers between devices, on_device(): returned = lax.all_to_all(returned, 'req', 0, 0, tiled=True)  8.79 us
    pallas_call x1, Pallas kernels, project_own(): pl.pallas_call(own_kernel, in_specs=[vmem(), anywhere(), anywhere(), anyw...  7.98 us
    ppermute x1, starting transfers between devices, on_device(): far = lax.ppermute(packed, 'head', [(i, (i + 2) % 4) for i in range(4)])  2.62 us
    pallas_call x1, Pallas kernels, on_device(): pl.pallas_call(place_kernel, out_shape=jax.ShapeDtypeStruct((PEERS * 2 *...  2.44 us
    pallas_call x1, Pallas kernels, on_device(): pl.pallas_call(pack_kernel, in_specs=[whole((CHUNK, D_Q)), whole((CHUNK,...  2.14 us
  transfers between devices with their start and end apart: 5, of which 0 were waited for; matrix products, arithmetic and copies ran while one was open for 0% of the time, Pallas kernels for 56%

profile of v4, /device:TPU:1, one launch (start us, length us, event | category | flops | bytes accessed | tf_op | source)
XLA Modules:
  0.0 65.6 jit_solution(5673185830773265741)
XLA Ops:
  0.6 2.4 %place.1.after_ref = bf16[256,1664]{1,0:T(8,128)(2,1)} custom-call(bf16[64,3072]{1,0:T(8,128)(2,1)} %q_ref.1, s32[1,64]{1,0:T(1,128)} %bitcast.13, s32[1,64]{1,0:T(1,128)} %bitcast.18), custom_call_target="tpu_custom_call" | custom-call | tf_op jit(solution)/shard_map/place/pallas_call | solution.py:515
  3.1 9.4 %all-to-all-start = ((bf16[32,8,1664]{2,1,0:T(8,128)(2,1)}), bf16[32,8,1664]{2,1,0:T(8,128)(2,1)S(1)}, u32[]{:S(2)}, u32[]{:S(2)}) async-start(bf16[32,8,1664]{2,1,0:T(8,128)(2,1)} %bitcast.16), calls=%async_computation | async-start | bytes 1703936 | tf_op jit(solution)/shard_map/all_to_all | solution.py:521
  12.5 2.1 %pack.1 = (bf16[128,2176]{1,0:T(8,128)(2,1)}, s32[1,64]{1,0:T(1,128)}, s32[1,64]{1,0:T(1,128)}) custom-call(bf16[128,1536]{1,0:T(8,128)(2,1)} %x_ref.1, bf16[128,512]{1,0:T(8,128)(2,1)} %l_ref.1, bf16[64,128]{1,0:T(8,128)(2,1)} %rk_ref.1, s32[1,128]{1,0:T(1,128)} %bitcast.19, s32[1,64]{1,0:T(1,128)} %bitcast.20, bf16[256,1664]{1,0:T(8,128)(2,1)} %place.1.after_ref), custom_call_target="tpu_custom_call" | custom-call | tf_op jit(solution)/shard_map/pack/pallas_call | solution.py:524
  14.6 0.0 copy-start.2
  14.6 1.3 %collective-permute-start.2 = (bf16[128,2176]{1,0:T(8,128)(2,1)}, bf16[128,2176]{1,0:T(8,128)(2,1)S(1)}, u32[]{:S(2)}, u32[]{:S(2)}) collective-permute-start(bf16[128,2176]{1,0:T(8,128)(2,1)} %get-tuple-element.9.x_ref.own_hbm), channel_id=1, source_target_pairs={{0,1},{1,2},{2,3},{3,0},{4,5},{5,6},{6,7},{7,4},{8,9},{9,10},{10,1... | collective-permute-start | bytes 1671176 | tf_op jit(solution)/shard_map/ppermute | solution.py:533
  15.9 2.6 %collective-permute-start.1 = (bf16[128,2176]{1,0:T(8,128)(2,1)}, bf16[128,2176]{1,0:T(8,128)(2,1)S(1)}, u32[]{:S(2)}, u32[]{:S(2)}) collective-permute-start(bf16[128,2176]{1,0:T(8,128)(2,1)} %get-tuple-element.9.x_ref.own_hbm), channel_id=1, source_target_pairs={{0,2},{1,3},{2,0},{3,1},{4,6},{5,7},{6,4},{7,5},{8,10},{9,11},{10,... | collective-permute-start | bytes 1671176 | tf_op jit(solution)/shard_map/ppermute | solution.py:534
  18.6 1.1 %collective-permute-start = (bf16[128,2176]{1,0:T(8,128)(2,1)}, bf16[128,2176]{1,0:T(8,128)(2,1)S(1)}, u32[]{:S(2)}, u32[]{:S(2)}) collective-permute-start(bf16[128,2176]{1,0:T(8,128)(2,1)} %get-tuple-element.9.x_ref.own_hbm), channel_id=1, source_target_pairs={{0,3},{1,0},{2,1},{3,2},{4,7},{5,4},{6,5},{7,6},{8,11},{9,8},{10,9... | collective-permute-start | bytes 1671176 | tf_op jit(solution)/shard_map/ppermute | solution.py:532
  19.6 8.0 %own.1 = (bf16[4,128,512]{2,1,0:T(8,128)(2,1)}, bf16[4,128,256]{2,1,0:T(8,128)(2,1)}, bf16[4,128,512]{2,1,0:T(8,128)(2,1)}, bf16[4,128,512]{2,1,0:T(8,128)(2,1)}) custom-call(bf16[128,2176]{1,0:T(8,128)(2,1)} %get-tuple-element.9.x_ref.own_hbm, bf16[1536,3072]{1,0:T(8,128)(2,1)} %wq_hbm.3, bf16[512,2048]{1,0:T(8,128)(2,1)} %wk_hbm.3, bf16[512,2048]{1,0:T(8,128)(2,1)} %wv_hbm.3), custom_call_target="tpu_custom_call" | custom-call | tf_op jit(solution)/shard_map/own/pallas_call | solution.py:472
  27.6 0.0 all-to-all-done
  27.6 0.0 copy-done.2
  27.6 0.0 copy-start
  27.7 1.0 %copy-done = bf16[4,128,512]{2,1,0:T(8,128)(2,1)S(1)} copy-done((bf16[4,128,512]{2,1,0:T(8,128)(2,1)S(1)}, bf16[4,128,512]{2,1,0:T(8,128)(2,1)}, u32[]{:S(2)}) %copy-start) | copy-done | bytes 524312
  28.7 12.7 %decode.1.after_ref = bf16[256,1024]{1,0:T(8,128)(2,1)} custom-call(bf16[256,1664]{1,0:T(8,128)(2,1)S(1)} %bitcast.11, bf16[512,2048]{1,0:T(8,128)(2,1)} %wk_hbm.3, bf16[64,256,512]{2,1,0:T(8,128)(2,1)} %lat_hbm.1, bf16[64,64,256]{2,1,0:T(8,128)(2,1)} %rk_hbm.1, bf16[512,2048]{1,0:T(8,128)(2,1)} %wv_hbm.3, s32[1,64]{1,0:T(1,128)} %get-tuple-element.14.order_hbm, ...), custom_call_target="tpu_custom_call" | custom-call | tf_op jit(solution)/shard_map/decode/pallas_call | solution.py:537
  41.4 8.8 %all-to-all-start.1 = ((bf16[32,8,1024]{2,1,0:T(8,128)(2,1)}), bf16[32,8,1024]{2,1,0:T(8,128)(2,1)S(1)}, u32[]{:S(2)}, u32[]{:S(2)}) async-start(bf16[32,8,1024]{2,1,0:T(8,128)(2,1)} %bitcast.9), calls=%async_computation.1 | async-start | bytes 1048576 | tf_op jit(solution)/shard_map/all_to_all | solution.py:560
  50.2 0.0 collective-permute-done.2.left_ref
  50.2 0.0 collective-permute-done.1.far_ref
  50.2 0.0 collective-permute-done.right_ref
  50.2 0.0 copy-start.1
  50.2 14.1 %prefill.1 = bf16[512,2048]{1,0:T(8,128)(2,1)} custom-call(s32[1]{0:T(128)} %bitcast.head_ref, bf16[128,2176]{1,0:T(8,128)(2,1)S(1)} %collective-permute-done.right_ref, bf16[128,2176]{1,0:T(8,128)(2,1)S(1)} %collective-permute-done.1.far_ref, bf16[128,2176]{1,0:T(8,128)(2,1)S(1)} %collective-permute-done.2.left_ref, ...), custom_call_target="tpu_custom_call" | custom-call | tf_op jit(solution)/shard_map/prefill/pallas_call | solution.py:488
  64.4 0.0 all-to-all-done.1
  64.4 0.0 copy-done.1
  64.4 1.1 %unplace.1 = bf16[64,2048]{1,0:T(8,128)(2,1)} custom-call(bf16[256,1024]{1,0:T(8,128)(2,1)S(1)} %bitcast.12, s32[1,64]{1,0:T(1,128)S(1)} %bitcast.14), custom_call_target="tpu_custom_call" | custom-call | tf_op jit(solution)/shard_map/unplace/pallas_call | solution.py:562
Async XLA Ops:
  3.1 24.6 %all-to-all-start = ((bf16[32,8,1664]{2,1,0:T(8,128)(2,1)}), bf16[32,8,1664]{2,1,0:T(8,128)(2,1)S(1)}, u32[]{:S(2)}, u32[]{:S(2)}) async-start(bf16[32,8,1664]{2,1,0:T(8,128)(2,1)} %bitcast.16), calls=%async_computation | async-start | bytes 1703936 | tf_op jit(solution)/shard_map/all_to_all | solution.py:521
  14.6 13.0 %copy-start.2 = (s32[1,64]{1,0:T(1,128)S(1)}, s32[1,64]{1,0:T(1,128)}, u32[]{:S(2)}) copy-start(s32[1,64]{1,0:T(1,128)} %get-tuple-element.15) | copy-start | bytes 772
  14.6 35.5 %collective-permute-start.2 = (bf16[128,2176]{1,0:T(8,128)(2,1)}, bf16[128,2176]{1,0:T(8,128)(2,1)S(1)}, u32[]{:S(2)}, u32[]{:S(2)}) collective-permute-start(bf16[128,2176]{1,0:T(8,128)(2,1)} %get-tuple-element.9.x_ref.own_hbm), channel_id=1, source_target_pairs={{0,1},{1,2},{2,3},{3,0},{4,5},{5,6},{6,7},{7,4},{8,9},{9,10},{10,1... | collective-permute-start | bytes 1671176 | tf_op jit(solution)/shard_map/ppermute | solution.py:533
  15.9 34.3 %collective-permute-start.1 = (bf16[128,2176]{1,0:T(8,128)(2,1)}, bf16[128,2176]{1,0:T(8,128)(2,1)S(1)}, u32[]{:S(2)}, u32[]{:S(2)}) collective-permute-start(bf16[128,2176]{1,0:T(8,128)(2,1)} %get-tuple-element.9.x_ref.own_hbm), channel_id=1, source_target_pairs={{0,2},{1,3},{2,0},{3,1},{4,6},{5,7},{6,4},{7,5},{8,10},{9,11},{10,... | collective-permute-start | bytes 1671176 | tf_op jit(solution)/shard_map/ppermute | solution.py:534
  18.6 31.7 %collective-permute-start = (bf16[128,2176]{1,0:T(8,128)(2,1)}, bf16[128,2176]{1,0:T(8,128)(2,1)S(1)}, u32[]{:S(2)}, u32[]{:S(2)}) collective-permute-start(bf16[128,2176]{1,0:T(8,128)(2,1)} %get-tuple-element.9.x_ref.own_hbm), channel_id=1, source_target_pairs={{0,3},{1,0},{2,1},{3,2},{4,7},{5,4},{6,5},{7,6},{8,11},{9,8},{10,9... | collective-permute-start | bytes 1671176 | tf_op jit(solution)/shard_map/ppermute | solution.py:532
  27.6 1.0 %copy-start = (bf16[4,128,512]{2,1,0:T(8,128)(2,1)S(1)}, bf16[4,128,512]{2,1,0:T(8,128)(2,1)}, u32[]{:S(2)}) copy-start(bf16[4,128,512]{2,1,0:T(8,128)(2,1)} %get-tuple-element.10.after_ref.own_qn_hbm) | copy-start | bytes 1572868
  41.4 23.0 %all-to-all-start.1 = ((bf16[32,8,1024]{2,1,0:T(8,128)(2,1)}), bf16[32,8,1024]{2,1,0:T(8,128)(2,1)S(1)}, u32[]{:S(2)}, u32[]{:S(2)}) async-start(bf16[32,8,1024]{2,1,0:T(8,128)(2,1)} %bitcast.9), calls=%async_computation.1 | async-start | bytes 1048576 | tf_op jit(solution)/shard_map/all_to_all | solution.py:560
  50.2 14.2 %copy-start.1 = (s32[64]{0:T(128)S(1)}, s32[64]{0:T(128)}, u32[]{:S(2)}) copy-start(s32[64]{0:T(128)} %param.21) | copy-start | bytes 772

commit v5 on v4

--- a/solution.py
+++ b/solution.py
@@ -50,7 +50,7 @@
     return jnp.sum(jnp.where(eye, row, 0), axis=1, keepdims=True)
 
 
-def pack_kernel(x_ref, l_ref, rk_ref, pos_ref, len_ref, after_ref, packed_ref, order_ref, sorted_ref):
+def pack_kernel(x_ref, l_ref, rk_ref, pos_ref, len_ref, after_ref, packed_ref, plan_ref):
     packed_ref[:, :D_Q] = x_ref[...]
     packed_ref[:, D_Q:D_Q + D_C] = l_ref[...]
     pos = pos_ref[...]
@@ -70,11 +70,18 @@
     this, other = iota((SLOTS, SLOTS), 0), iota((SLOTS, SLOTS), 1)
     ahead = (length < length_col) | ((length == length_col) & (other < this))
     rank = jnp.sum(jnp.where(ahead, 1, 0), axis=1, keepdims=True)
-    order_ref[...] = jnp.sum(jnp.where(rank == other, this, 0), axis=0, keepdims=True)
-    sorted_ref[...] = jnp.sum(jnp.where(rank == other, length_col, 0), axis=0, keepdims=True)
-
-
-def place_kernel(q_ref, owner_ref, slot_ref, send_ref):
+    hit = rank == other
+    plan_ref[...] = jnp.sum(
+        jnp.concatenate([jnp.where(hit, this, 0), jnp.where(hit, length_col, 0)], axis=1), axis=0, keepdims=True)
+
+
+def place_kernel(q_hbm, owner_hbm, slot_hbm, send_hbm, q_ref, owner_ref, slot_ref, send_ref, sems, send_sems):
+    copies = [pltpu.make_async_copy(src, dst, sems.at[i]) for i, (src, dst) in enumerate(
+        ((owner_hbm, owner_ref), (slot_hbm, slot_ref), (q_hbm, q_ref)))]
+    for copy in copies:
+        copy.start()
+    for copy in copies[:2]:
+        copy.wait()
     owner = owner_ref[...]
     owner_col = column_of(owner)
     same = owner_col == owner
@@ -83,12 +90,22 @@
     target = owner * (2 * MOST) + rank
     target = jnp.concatenate([target, target + MOST], axis=1)
     placing = iota((PEERS * 2 * MOST, 2 * ROWS), 0) == target
-    queries = jnp.concatenate([q_ref[:, :1536], q_ref[:, 1536:]], axis=0)
-    send_ref[:, :1536] = dot(placing.astype(BF16), queries).astype(BF16)
+    spread = placing.astype(BF16)
     slot = slot_ref[...] + 1
     slot = jnp.concatenate([slot, slot], axis=1)
     slot_col = jnp.sum(jnp.where(placing, slot, 0), axis=1, keepdims=True)
+    parts = [(0, 512), (512, 512), (1024, SEND - 1024)]
+    sends = [pltpu.make_async_copy(send_ref.at[:, pl.ds(at, width)], send_hbm.at[:, pl.ds(at, width)], send_sems.at[i])
+             for i, (at, width) in enumerate(parts)]
     send_ref[:, 1536:] = jnp.broadcast_to(slot_col.astype(F32), (PEERS * 2 * MOST, 128)).astype(BF16)
+    copies[2].wait()
+    for part, send in enumerate(sends):
+        lanes = slice(part * 512, (part + 1) * 512)
+        queries = jnp.concatenate([q_ref[:, lanes], q_ref[:, 1536 + part * 512:1536 + (part + 1) * 512]], axis=0)
+        send_ref[:, lanes] = dot(spread, queries).astype(BF16)
+        send.start()
+    for send in sends:
+        send.wait()
 
 
 def split_pair(three):
@@ -106,21 +123,21 @@
 WIDTHS = (64, 128, 192, 256)
 
 
-def decode_kernel(recv_ref, kup_hbm, lat_hbm, rk_hbm, vup_hbm, order_hbm, order_ref, len_ref, after_ref, out_ref,
-                  kup_ref, rk_ref, vup_ref, order_row_ref, lat_ref, lq_ref, qr_ref, lo_ref, sems, lat_sems):
+def decode_kernel(recv_ref, kup_hbm, lat_hbm, rk_hbm, vup_hbm, plan_hbm, after_ref, out_hbm,
+                  kup_ref, rk_ref, vup_ref, plan_row_ref, plan_ref, out_ref, lat_ref, lq_ref, qr_ref, lo_ref, sems, lat_sems, out_sem):
     rows = PEERS * 2 * MOST
-    order_copy, kup_copy, rk_copy, vup_copy = [
+    plan_copy, kup_copy, rk_copy, vup_copy, row_copy = [
         pltpu.make_async_copy(src, dst, sems.at[i]) for i, (src, dst) in enumerate(
-            ((order_hbm, order_row_ref), (kup_hbm, kup_ref), (rk_hbm, rk_ref), (vup_hbm, vup_ref)))]
+            ((plan_hbm, plan_ref), (kup_hbm, kup_ref.at[:, pl.ds(0, HEADS * D_NOPE)]), (rk_hbm, rk_ref), (vup_hbm, vup_ref.at[:, pl.ds(0, HEADS * D_V)]), (plan_hbm, plan_row_ref)))]
 
     def of_width(section, width):
-        longest = len_ref[section * SECTION + SECTION - 1]
+        longest = plan_ref[0, SLOTS + section * SECTION + SECTION - 1]
         return (longest <= width) & (longest > width - 64)
 
     def fetch(section, width, i):
         place = section * SECTION + i
         return pltpu.make_async_copy(
-            lat_hbm.at[order_ref[place], pl.ds(0, width)], lat_ref.at[place, pl.ds(0, width)], lat_sems.at[section])
+            lat_hbm.at[plan_ref[0, place], pl.ds(0, width)], lat_ref.at[place, pl.ds(0, width), pl.ds(0, D_C)], lat_sems.at[section])
 
     def start(section):
         for width in WIDTHS:
@@ -129,18 +146,20 @@
                 for i in range(SECTION):
                     fetch(section, width, i).start()
 
-    order_copy.start()
+    plan_copy.start()
+    row_copy.start()
     kup_copy.start()
+    plan_copy.wait()
     start(0)
     rk_copy.start()
 
     def place_onehot():
         slot_col = recv_ref[:, 1536:].astype(jnp.int32)
-        hit = slot_col[:, :SLOTS] == order_row_ref[...] + 1
+        hit = slot_col[:, :SLOTS] == plan_row_ref[:, :SLOTS] + 1
         half = (iota((rows, SLOTS), 0) & 7) < MOST
         return hit & half, hit & jnp.logical_not(half)
 
-    order_copy.wait()
+    row_copy.wait()
     first, second = place_onehot()
     blank = jnp.zeros((SLOTS, 128), BF16)
     low_lane = iota((SLOTS, 128), 1) < 64
@@ -164,10 +183,10 @@
     start(2)
 
     def attend(section, width):
-        @pl.loop(0, SECTION)
-        def _(i):
-            fetch(section, width, i).wait()
-
+        whole_section = pl.ds(pl.multiple_of(section * SECTION, SECTION), SECTION)
+        pltpu.make_async_copy(
+            lat_hbm.at[whole_section, pl.ds(0, width)], lat_ref.at[whole_section, pl.ds(0, width), pl.ds(0, D_C)],
+            lat_sems.at[section]).wait()
         row, lane = iota((WIDE, WIDE), 0), iota((WIDE, WIDE), 1)
         by_place = jnp.where(lane == (row & 15) * TOGETHER + (row >> 4), 1.0, 0.0).astype(BF16)
         by_head = jnp.where(row == (lane & 15) * TOGETHER + (lane >> 4), 1.0, 0.0).astype(BF16)
@@ -181,19 +200,19 @@
         scores = []
         for start, (latent, rotary) in zip(starts, queries):
             score = []
-            length = jnp.full((WIDE, 1), len_ref[start], jnp.int32)
+            length = jnp.full((WIDE, 1), plan_ref[0, SLOTS + start], jnp.int32)
             for i in range(TOGETHER):
                 mine = slice(i * HEADS, (i + 1) * HEADS)
-                score.append(dot(latent[mine], lat_ref[start + i, :width], ((1,), (1,)))
-                             + dot(rotary[mine, :D_ROPE], rk_ref[order_ref[start + i], :, :width]))
-                length = jnp.where(row_place == i, len_ref[start + i], length)
+                score.append(dot(latent[mine], lat_ref[start + i, :width, :D_C], ((1,), (1,)))
+                             + dot(rotary[mine, :D_ROPE], rk_ref[plan_ref[0, start + i], :, :width]))
+                length = jnp.where(row_place == i, plan_ref[0, SLOTS + start + i], length)
             score = jnp.concatenate(score, axis=0)
             scores.append(jnp.where(iota((WIDE, width), 1) < length, score * SCALE, MASKED))
         for start, score in zip(starts, scores):
             raised = jnp.exp(score - jnp.max(score, axis=1, keepdims=True))
             weights = (raised * (1.0 / jnp.sum(raised, axis=1, keepdims=True))).astype(BF16)
             total = jnp.concatenate(
-                [dot(weights[i * HEADS:(i + 1) * HEADS], lat_ref[start + i, :width]).astype(BF16)
+                [dot(weights[i * HEADS:(i + 1) * HEADS], lat_ref[start + i, :width, :D_C]).astype(BF16)
                  for i in range(TOGETHER)], axis=0)
             lo_ref[:, pl.ds(start, TOGETHER), :] = dot(by_head, total).reshape(HEADS, TOGETHER, D_C)
 
@@ -210,15 +229,18 @@
                 attend(section, width)
 
     vup_copy.wait()
+    first, second = place_onehot()
+    spread = jnp.concatenate([jnp.where(first, 1.0, 0.0), jnp.where(second, 1.0, 0.0)], axis=1).astype(BF16)
     outs = []
     for head in range(0, HEADS, 2):
         latent_out = lo_ref[head:head + 2].reshape(2 * SLOTS, D_C).astype(BF16)
-        both = dot(latent_out, vup_ref[:, head * 128:(head + 2) * 128])
-        outs += [both[:SLOTS, :128].astype(BF16), both[SLOTS:, 128:].astype(BF16)]
+        both = dot(latent_out, vup_ref[:, head * 128:(head + 2) * 128]).astype(BF16)
+        outs += [both[:SLOTS, :128], both[SLOTS:, 128:]]
     outs = jnp.concatenate([jnp.concatenate(outs[:8], axis=1), jnp.concatenate(outs[8:], axis=1)], axis=0)
-    first, second = place_onehot()
-    spread = jnp.concatenate([jnp.where(first, 1.0, 0.0), jnp.where(second, 1.0, 0.0)], axis=1)
-    out_ref[...] = dot(spread.astype(BF16), outs).astype(BF16)
+    out_ref[...] = dot(spread, outs).astype(BF16)
+    out_copy = pltpu.make_async_copy(out_ref, out_hbm, out_sem)
+    out_copy.start()
+    out_copy.wait()
 
 
 def unplace_kernel(ret_ref, owner_ref, out_ref):
@@ -259,12 +281,21 @@
     return (rotary * cos + swapped * sin).astype(BF16)
 
 
-def own_kernel(x_ref, wq_hbm, wk_hbm, wv_hbm,
-               qn_ref, qr_ref, k_ref, v_ref, wq_ref, wk_ref, wv_ref, cos_ref, sin_ref, sems):
+def own_kernel(packed_hbm, wq_hbm, wk_hbm, wv_hbm, qn_hbm, qr_hbm, k_hbm, v_hbm,
+               qn_ref, qr_ref, k_ref, v_ref, x_ref, wq_ref, wk_ref, wv_ref, cos_ref, sin_ref, x_sem, sems, out_sems):
     def fetch(group):
         return fetch_weights(group, (wq_hbm, wk_hbm, wv_hbm), (wq_ref, wk_ref, wv_ref), sems)
 
-    for group in range(GROUPS):
+    def send_out(group):
+        return [pltpu.make_async_copy(src.at[group], dst.at[group], out_sems.at[i, group]) for i, (src, dst) in enumerate(
+            ((qn_ref, qn_hbm), (qr_ref, qr_hbm), (k_ref, k_hbm), (v_ref, v_hbm)))]
+
+    x_copy = pltpu.make_async_copy(packed_hbm, x_ref, x_sem)
+    x_copy.start()
+    for copy in fetch(0):
+        copy.start()
+    x_copy.wait()
+    for group in range(1, GROUPS):
         for copy in fetch(group):
             copy.start()
     cos_ref[...], sin_ref[...] = rope_tables(x_ref[:, D_Q + D_C:])
@@ -282,13 +313,19 @@
         latents = x_ref[:, D_Q:D_Q + D_C]
         k_ref[group] = dot(latents, wk_ref[group]).astype(BF16)
         v_ref[group] = dot(latents, wv_ref[group]).astype(BF16)
-
-
-def prefill_kernel(head_ref, right_ref, far_ref, left_ref, own_hbm, wq_hbm, wk_hbm, wv_hbm,
+        for copy in send_out(group):
+            copy.start()
+
+    for group in range(GROUPS):
+        for copy in send_out(group):
+            copy.wait()
+
+
+def prefill_kernel(right_ref, far_ref, left_ref, own_hbm, wq_hbm, wk_hbm, wv_hbm,
                    own_qn_hbm, own_qr_hbm, own_k_hbm, own_v_hbm, after_ref, out_hbm,
                    own_ref, all_wq_ref, all_wk_ref, all_wv_ref, all_out_ref, chunk_sem, weight_sems, own_sems, out_sems,
                    cos_ref, sin_ref, bias_ref, pair_ref, *sets):
-    me = head_ref[0]
+    me = lax.axis_index("head")
     place = [(c - me + 3) & 3 for c in range(4)]
     half = TOKENS // 2
     sets = (sets[:4], sets[4:])
@@ -412,8 +449,8 @@
                 step_copies(fetch_own(step - 1, source, 1 - parity), wait)
                 score, weigh = attend_steps(source, step - 1)
                 query, turn, latent = project_steps(into, step)
+                query(0, 512)
                 score(0)
-                query(0, 512)
                 score(1)
                 weigh(0)
                 query(512, 256)
@@ -437,8 +474,11 @@
             score(head + 1)
         weigh(head)
     send_out(last).start()
-    for group in range(GROUPS):
-        send_out(group).wait()
+    step_copies([send_out(group) for group in range(GROUPS)], wait)
+
+
+def in_hbm(array):
+    return pltpu.with_memory_space_constraint(array, pltpu.HBM)
 
 
 def whole(shape):
@@ -471,23 +511,26 @@
 def project_own(packed, wq, wk, wv):
     return pl.pallas_call(
         own_kernel,
-        in_specs=[vmem(), anywhere(), anywhere(), anywhere()],
-        out_specs=[vmem()] * 4,
-        out_shape=[jax.ShapeDtypeStruct((GROUPS, CHUNK, width), BF16) for width in SETS],
-        scratch_shapes=WEIGHTS + [
+        in_specs=[anywhere()] * 4,
+        out_specs=[anywhere()] * 4,
+        out_shape=[pltpu.HBM((GROUPS, CHUNK, width), BF16) for width in SETS],
+        scratch_shapes=[pltpu.VMEM((GROUPS, CHUNK, width), BF16) for width in SETS]
+        + [pltpu.VMEM((CHUNK, PACK), BF16)] + WEIGHTS + [
             pltpu.VMEM((CHUNK, 128), F32),
             pltpu.VMEM((CHUNK, 128), F32),
+            pltpu.SemaphoreType.DMA,
             pltpu.SemaphoreType.DMA((3, GROUPS)),
+            pltpu.SemaphoreType.DMA((4, GROUPS)),
         ],
         compiler_params=params(60),
         name="own",
-    )(packed, wq, wk, wv)
-
-
-def prefill(me, right, far, left, packed, wq, wk, wv, own, after):
+    )(in_hbm(packed), wq, wk, wv)
+
+
+def prefill(right, far, left, packed, wq, wk, wv, own, after):
     return pl.pallas_call(
         prefill_kernel,
-        in_specs=[smem()] + [vmem()] * 3 + [anywhere()] * 9,
+        in_specs=[vmem()] * 3 + [anywhere()] * 9,
         out_specs=anywhere(),
         out_shape=jax.ShapeDtypeStruct((TOKENS, HEADS * D_V), BF16),
         scratch_shapes=[pltpu.VMEM((CHUNK, 128), BF16)] + WEIGHTS + [
@@ -503,60 +546,68 @@
         ] + [pltpu.VMEM((4, CHUNK, width), BF16) for width in SETS] * 2,
         compiler_params=params(36),
         name="prefill",
-    )(me, right, far, left, pltpu.with_memory_space_constraint(packed, pltpu.HBM), wq, wk, wv,
-      *(pltpu.with_memory_space_constraint(part, pltpu.HBM) for part in own), after)
+    )(right, far, left, in_hbm(packed), wq, wk, wv, *own, after)
 
 
 def on_device(x, latents, rotary_keys, positions, wq, wk, wv, queries, owner, slot, cache, cache_rope, lengths):
-    me = lax.axis_index("head").astype(jnp.int32).reshape(1)
-    wq, wk, wv, cache, cache_rope = (
-        pltpu.with_memory_space_constraint(array, pltpu.HBM) for array in (wq, wk, wv, cache, cache_rope))
+    wq, wk, wv, cache, cache_rope = (in_hbm(array) for array in (wq, wk, wv, cache, cache_rope))
     owner_row, slot_row = owner.reshape(1, ROWS), slot.reshape(1, ROWS)
     send = pl.pallas_call(
         place_kernel,
-        out_shape=jax.ShapeDtypeStruct((PEERS * 2 * MOST, SEND), BF16),
-        compiler_params=params(60),
+        in_specs=[anywhere()] * 3,
+        out_specs=anywhere(),
+        out_shape=pltpu.HBM((PEERS * 2 * MOST, SEND), BF16),
+        scratch_shapes=[
+            pltpu.VMEM((ROWS, HEADS * 192), BF16),
+            pltpu.VMEM((1, ROWS), jnp.int32),
+            pltpu.VMEM((1, ROWS), jnp.int32),
+            pltpu.VMEM((PEERS * 2 * MOST, SEND), BF16),
+            pltpu.SemaphoreType.DMA((3,)),
+            pltpu.SemaphoreType.DMA((3,)),
+        ],
+        compiler_params=params(16),
         name="place",
-    )(queries, owner_row, slot_row)
+    )(in_hbm(queries), in_hbm(owner_row), in_hbm(slot_row))
     recv = lax.all_to_all(send, "req", 0, 0, tiled=True)
 
-    row = jax.ShapeDtypeStruct((1, SLOTS), jnp.int32)
-    packed, order, ordered_lengths = pl.pallas_call(
+    packed, plan = pl.pallas_call(
         pack_kernel,
-        in_specs=[whole((CHUNK, D_Q)), whole((CHUNK, D_C)), whole((64, CHUNK)), whole((1, CHUNK)), whole((1, SLOTS)), anywhere()],
-        out_specs=[whole((CHUNK, PACK)), whole((1, SLOTS)), whole((1, SLOTS))],
-        out_shape=[jax.ShapeDtypeStruct((CHUNK, PACK), BF16), row, row],
+        in_specs=[vmem()] * 5 + [anywhere()],
+        out_specs=[vmem()] * 2,
+        out_shape=[jax.ShapeDtypeStruct((CHUNK, PACK), BF16), jax.ShapeDtypeStruct((1, 2 * SLOTS), jnp.int32)],
         compiler_params=params(60),
         name="pack",
-    )(x, latents, rotary_keys, positions.reshape(1, CHUNK), lengths.reshape(1, SLOTS), send)
+    )(x, latents, rotary_keys, positions.reshape(1, CHUNK), lengths.reshape(1, SLOTS), in_hbm(send))
     right = lax.ppermute(packed, "head", [(i, (i + 3) % 4) for i in range(4)])
     left = lax.ppermute(packed, "head", [(i, (i + 1) % 4) for i in range(4)])
     far = lax.ppermute(packed, "head", [(i, (i + 2) % 4) for i in range(4)])
-    own = project_own(packed, wq, wk, wv)
+    own = [in_hbm(part) for part in project_own(packed, wq, wk, wv)]
 
     returned = pl.pallas_call(
         decode_kernel,
-        in_specs=[vmem()] + [anywhere()] * 5 + [smem(), smem(), anywhere()],
-        out_specs=whole((PEERS * 2 * MOST, RET)),
-        out_shape=jax.ShapeDtypeStruct((PEERS * 2 * MOST, RET), BF16),
+        in_specs=[vmem()] + [anywhere()] * 6,
+        out_specs=anywhere(),
+        out_shape=pltpu.HBM((PEERS * 2 * MOST, RET), BF16),
         scratch_shapes=[
-            pltpu.VMEM((D_C, HEADS * D_NOPE), BF16),
+            pltpu.VMEM((D_C, HEADS * D_NOPE + 128), BF16),
             pltpu.VMEM((SLOTS, D_ROPE, CMAX), BF16),
-            pltpu.VMEM((D_C, HEADS * D_V), BF16),
-            pltpu.VMEM((1, SLOTS), jnp.int32),
-            pltpu.VMEM((SLOTS, CMAX, D_C), BF16),
+            pltpu.VMEM((D_C, HEADS * D_V + 128), BF16),
+            pltpu.VMEM((1, 2 * SLOTS), jnp.int32),
+            pltpu.SMEM((1, 2 * SLOTS), jnp.int32),
+            pltpu.VMEM((PEERS * 2 * MOST, RET), BF16),
+            pltpu.VMEM((SLOTS, CMAX, D_C + 128), BF16),
             pltpu.VMEM((HEADS, SLOTS, D_C), F32),
             pltpu.VMEM((HEADS, SLOTS, 128), F32),
             pltpu.VMEM((HEADS, SLOTS, D_C), F32),
-            pltpu.SemaphoreType.DMA((4,)),
+            pltpu.SemaphoreType.DMA((5,)),
             pltpu.SemaphoreType.DMA((SECTIONS,)),
+            pltpu.SemaphoreType.DMA,
         ],
         compiler_params=params(44),
         name="decode",
-    )(recv, wk, cache, cache_rope, wv, pltpu.with_memory_space_constraint(order, pltpu.HBM), order.reshape(SLOTS),
-      ordered_lengths.reshape(SLOTS), own[0])
-
-    prompt_out = prefill(me, right, far, left, packed, wq, wk, wv, own, returned)
+    )(recv, wk, cache, cache_rope, wv, in_hbm(plan), own[0])
+
+    prompt_out = prefill(right, far, left, packed, wq, wk, wv, own, in_hbm(returned))
     returned = lax.all_to_all(returned, "req", 0, 0, tiled=True)
 
     decode_out = pl.pallas_call(

time: 66.5 us -> 62.7 us (0.943)
  Pallas kernels: 40.5 us -> 36.8 us
  starting transfers between devices: 23.2 us -> 24.7 us
  local copies, waits for them, and re-layouts: 1.04 us -> 0.01 us
    pallas_call x5, Pallas kernels: 39.4 us -> 35.6 us  [the longest x1 14.1 us: prefill(): pl.pallas_call(prefill_kernel, in_specs=[vmem()] * 3 + [anywhere()] * 9,...]
    all_to_all x1, starting transfers between devices: 8.79 us -> 10.3 us  [on_device(): returned = lax.all_to_all(returned, 'req', 0, 0, tiled=True)]
    unnamed x6 -> x2, local copies, waits for them, and re-layouts: 1.04 us -> 0.01 us
  transfers between devices with their start and end apart: 5 -> 5, of which waited for: 0 -> 0; matrix products, arithmetic and copies ran while one was open for 0% -> 0% of each run, Pallas kernels for 56% -> 54%
where the time goes in v5:
time: 62.7 us; the launch traced here: 62.2 us
  Pallas kernels  36.8 us (59%)
  starting transfers between devices  24.7 us (39%)
  between operations  0.74 us (1%)
    pallas_call x1, Pallas kernels, prefill(): pl.pallas_call(prefill_kernel, in_specs=[vmem()] * 3 + [anywhere()] * 9,...  14.1 us
    all_to_all x1, starting transfers between devices, on_device(): returned = lax.all_to_all(returned, 'req', 0, 0, tiled=True)  10.3 us
    all_to_all x1, starting transfers between devices, on_device(): recv = lax.all_to_all(send, 'req', 0, 0, tiled=True)  9.45 us
    pallas_call x1, Pallas kernels, on_device(): pl.pallas_call(decode_kernel, in_specs=[vmem()] + [anywhere()] * 6, out_s...  9.23 us
    pallas_call x1, Pallas kernels, project_own(): pl.pallas_call(own_kernel, in_specs=[anywhere()] * 4, out_specs=[anywhere...  7.86 us
    ppermute x1, starting transfers between devices, on_device(): far = lax.ppermute(packed, 'head', [(i, (i + 2) % 4) for i in range(4)])  2.62 us
    pallas_call x1, Pallas kernels, on_device(): pl.pallas_call(pack_kernel, in_specs=[vmem()] * 5 + [anywhere()], out_spe...  2.2 us
    pallas_call x1, Pallas kernels, on_device(): pl.pallas_call(place_kernel, in_specs=[anywhere()] * 3, out_specs=anywher...  2.19 us
  transfers between devices with their start and end apart: 5, of which 0 were waited for; matrix products, arithmetic and copies ran while one was open for 0% of the time, Pallas kernels for 54%

profile of v5, /device:TPU:1, one launch (start us, length us, event | category | flops | bytes accessed | tf_op | source)
XLA Modules:
  0.0 62.2 jit_solution(6986379364019269691)
XLA Ops:
  0.6 2.2 %place.1.after_ref = bf16[256,1664]{1,0:T(8,128)(2,1)} custom-call(bf16[64,3072]{1,0:T(8,128)(2,1)} %q_hbm.1, s32[1,64]{1,0:T(1,128)} %bitcast.10, s32[1,64]{1,0:T(1,128)} %bitcast.14), custom_call_target="tpu_custom_call" | custom-call | tf_op jit(solution)/shard_map/place/pallas_call | solution.py:555
  2.8 9.4 %all-to-all-start = ((bf16[32,8,1664]{2,1,0:T(8,128)(2,1)}), bf16[32,8,1664]{2,1,0:T(8,128)(2,1)S(1)}, u32[]{:S(2)}, u32[]{:S(2)}) async-start(bf16[32,8,1664]{2,1,0:T(8,128)(2,1)} %bitcast.12), calls=%async_computation | async-start | bytes 1703936 | tf_op jit(solution)/shard_map/all_to_all | solution.py:571
  12.3 2.2 %pack.1 = (bf16[128,2176]{1,0:T(8,128)(2,1)}, s32[1,128]{1,0:T(1,128)}) custom-call(bf16[128,1536]{1,0:T(8,128)(2,1)} %x_ref.1, bf16[128,512]{1,0:T(8,128)(2,1)} %l_ref.1, bf16[64,128]{1,0:T(8,128)(2,1)} %rk_ref.1, s32[1,128]{1,0:T(1,128)} %bitcast.15, s32[1,64]{1,0:T(1,128)} %bitcast.16, bf16[256,1664]{1,0:T(8,128)(2,1)} %place.1.after_ref), custom_call_target="tpu_custom_call" | custom-call | tf_op jit(solution)/shard_map/pack/pallas_call | solution.py:573
  14.5 1.3 %collective-permute-start.2 = (bf16[128,2176]{1,0:T(8,128)(2,1)}, bf16[128,2176]{1,0:T(8,128)(2,1)S(1)}, u32[]{:S(2)}, u32[]{:S(2)}) collective-permute-start(bf16[128,2176]{1,0:T(8,128)(2,1)} %get-tuple-element.8.packed_hbm.own_hbm), channel_id=1, source_target_pairs={{0,1},{1,2},{2,3},{3,0},{4,5},{5,6},{6,7},{7,4},{8,9},{9,10},{10,1... | collective-permute-start | bytes 1671176 | tf_op jit(solution)/shard_map/ppermute | solution.py:582
  15.8 2.6 %collective-permute-start.1 = (bf16[128,2176]{1,0:T(8,128)(2,1)}, bf16[128,2176]{1,0:T(8,128)(2,1)S(1)}, u32[]{:S(2)}, u32[]{:S(2)}) collective-permute-start(bf16[128,2176]{1,0:T(8,128)(2,1)} %get-tuple-element.8.packed_hbm.own_hbm), channel_id=1, source_target_pairs={{0,2},{1,3},{2,0},{3,1},{4,6},{5,7},{6,4},{7,5},{8,10},{9,11},{10,... | collective-permute-start | bytes 1671176 | tf_op jit(solution)/shard_map/ppermute | solution.py:583
  18.4 1.1 %collective-permute-start = (bf16[128,2176]{1,0:T(8,128)(2,1)}, bf16[128,2176]{1,0:T(8,128)(2,1)S(1)}, u32[]{:S(2)}, u32[]{:S(2)}) collective-permute-start(bf16[128,2176]{1,0:T(8,128)(2,1)} %get-tuple-element.8.packed_hbm.own_hbm), channel_id=1, source_target_pairs={{0,3},{1,0},{2,1},{3,2},{4,7},{5,4},{6,5},{7,6},{8,11},{9,8},{10,9... | collective-permute-start | bytes 1671176 | tf_op jit(solution)/shard_map/ppermute | solution.py:581
  19.5 7.9 %own.1 = (bf16[4,128,512]{2,1,0:T(8,128)(2,1)}, bf16[4,128,256]{2,1,0:T(8,128)(2,1)}, bf16[4,128,512]{2,1,0:T(8,128)(2,1)}, bf16[4,128,512]{2,1,0:T(8,128)(2,1)}) custom-call(bf16[128,2176]{1,0:T(8,128)(2,1)} %get-tuple-element.8.packed_hbm.own_hbm, bf16[1536,3072]{1,0:T(8,128)(2,1)} %wq_hbm.3, bf16[512,2048]{1,0:T(8,128)(2,1)} %wk_hbm.3, ...), custom_call_target="tpu_custom_call" | custom-call | tf_op jit(solution)/shard_map/own/pallas_call | solution.py:512
  27.3 0.0 all-to-all-done
  27.3 9.2 %decode.1.after_ref = bf16[256,1024]{1,0:T(8,128)(2,1)} custom-call(bf16[256,1664]{1,0:T(8,128)(2,1)S(1)} %bitcast.8, bf16[512,2048]{1,0:T(8,128)(2,1)} %wk_hbm.3, bf16[64,256,512]{2,1,0:T(8,128)(2,1)} %lat_hbm.1, bf16[64,64,256]{2,1,0:T(8,128)(2,1)} %rk_hbm.1, bf16[512,2048]{1,0:T(8,128)(2,1)} %wv_hbm.3, s32[1,128]{1,0:T(1,128)} %get-tuple-element.13.plan_hbm, ...), custom_call_target="tpu_custom_call" | custom-call | tf_op jit(solution)/shard_map/decode/pallas_call | solution.py:586
  36.6 10.3 %all-to-all-start.1 = ((bf16[32,8,1024]{2,1,0:T(8,128)(2,1)}), bf16[32,8,1024]{2,1,0:T(8,128)(2,1)S(1)}, u32[]{:S(2)}, u32[]{:S(2)}) async-start(bf16[32,8,1024]{2,1,0:T(8,128)(2,1)} %bitcast.13), calls=%async_computation.1 | async-start | bytes 1048576 | tf_op jit(solution)/shard_map/all_to_all | solution.py:611
  46.9 0.0 collective-permute-done.2.left_ref
  46.9 0.0 collective-permute-done.1.far_ref
  46.9 0.0 collective-permute-done.right_ref
  46.9 0.0 copy-start
  46.9 14.1 %prefill.1 = bf16[512,2048]{1,0:T(8,128)(2,1)} custom-call(bf16[128,2176]{1,0:T(8,128)(2,1)S(1)} %collective-permute-done.right_ref, bf16[128,2176]{1,0:T(8,128)(2,1)S(1)} %collective-permute-done.1.far_ref, bf16[128,2176]{1,0:T(8,128)(2,1)S(1)} %collective-permute-done.2.left_ref, bf16[128,2176]{1,0:T(8,128)(2,1)} %get-tuple-element.8.packed_hbm.own_hbm, ...), custom_call_target="tpu_custom_call" | custom-call | tf_op jit(solution)/shard_map/prefill/pallas_call | solution.py:531
  61.1 0.0 all-to-all-done.1
  61.1 0.0 copy-done
  61.1 1.1 %unplace.1 = bf16[64,2048]{1,0:T(8,128)(2,1)} custom-call(bf16[256,1024]{1,0:T(8,128)(2,1)S(1)} %bitcast.9, s32[1,64]{1,0:T(1,128)S(1)} %bitcast.11), custom_call_target="tpu_custom_call" | custom-call | tf_op jit(solution)/shard_map/unplace/pallas_call | solution.py:613
Async XLA Ops:
  2.8 24.5 %all-to-all-start = ((bf16[32,8,1664]{2,1,0:T(8,128)(2,1)}), bf16[32,8,1664]{2,1,0:T(8,128)(2,1)S(1)}, u32[]{:S(2)}, u32[]{:S(2)}) async-start(bf16[32,8,1664]{2,1,0:T(8,128)(2,1)} %bitcast.12), calls=%async_computation | async-start | bytes 1703936 | tf_op jit(solution)/shard_map/all_to_all | solution.py:571
  14.5 32.4 %collective-permute-start.2 = (bf16[128,2176]{1,0:T(8,128)(2,1)}, bf16[128,2176]{1,0:T(8,128)(2,1)S(1)}, u32[]{:S(2)}, u32[]{:S(2)}) collective-permute-start(bf16[128,2176]{1,0:T(8,128)(2,1)} %get-tuple-element.8.packed_hbm.own_hbm), channel_id=1, source_target_pairs={{0,1},{1,2},{2,3},{3,0},{4,5},{5,6},{6,7},{7,4},{8,9},{9,10},{10,1... | collective-permute-start | bytes 1671176 | tf_op jit(solution)/shard_map/ppermute | solution.py:582
  15.8 31.1 %collective-permute-start.1 = (bf16[128,2176]{1,0:T(8,128)(2,1)}, bf16[128,2176]{1,0:T(8,128)(2,1)S(1)}, u32[]{:S(2)}, u32[]{:S(2)}) collective-permute-start(bf16[128,2176]{1,0:T(8,128)(2,1)} %get-tuple-element.8.packed_hbm.own_hbm), channel_id=1, source_target_pairs={{0,2},{1,3},{2,0},{3,1},{4,6},{5,7},{6,4},{7,5},{8,10},{9,11},{10,... | collective-permute-start | bytes 1671176 | tf_op jit(solution)/shard_map/ppermute | solution.py:583
  18.4 28.5 %collective-permute-start = (bf16[128,2176]{1,0:T(8,128)(2,1)}, bf16[128,2176]{1,0:T(8,128)(2,1)S(1)}, u32[]{:S(2)}, u32[]{:S(2)}) collective-permute-start(bf16[128,2176]{1,0:T(8,128)(2,1)} %get-tuple-element.8.packed_hbm.own_hbm), channel_id=1, source_target_pairs={{0,3},{1,0},{2,1},{3,2},{4,7},{5,4},{6,5},{7,6},{8,11},{9,8},{10,9... | collective-permute-start | bytes 1671176 | tf_op jit(solution)/shard_map/ppermute | solution.py:581
  36.6 24.5 %all-to-all-start.1 = ((bf16[32,8,1024]{2,1,0:T(8,128)(2,1)}), bf16[32,8,1024]{2,1,0:T(8,128)(2,1)S(1)}, u32[]{:S(2)}, u32[]{:S(2)}) async-start(bf16[32,8,1024]{2,1,0:T(8,128)(2,1)} %bitcast.13), calls=%async_computation.1 | async-start | bytes 1048576 | tf_op jit(solution)/shard_map/all_to_all | solution.py:611
  46.9 14.2 %copy-start = (s32[64]{0:T(128)S(1)}, s32[64]{0:T(128)}, u32[]{:S(2)}) copy-start(s32[64]{0:T(128)} %param.21) | copy-start | bytes 772

commit v6 on v5

--- a/solution.py
+++ b/solution.py
@@ -50,9 +50,35 @@
     return jnp.sum(jnp.where(eye, row, 0), axis=1, keepdims=True)
 
 
-def pack_kernel(x_ref, l_ref, rk_ref, pos_ref, len_ref, after_ref, packed_ref, plan_ref):
-    packed_ref[:, :D_Q] = x_ref[...]
-    packed_ref[:, D_Q:D_Q + D_C] = l_ref[...]
+def stage_kernel(q_hbm, owner_hbm, slot_hbm, x_hbm, l_hbm, rk_hbm, pos_hbm, len_hbm, send_hbm, packed_hbm, plan_ref,
+                 q_ref, owner_ref, slot_ref, packed_ref, rk_ref, pos_ref, len_ref, send_ref, sems, out_sems):
+    moves = [(owner_hbm, owner_ref), (slot_hbm, slot_ref), (q_hbm, q_ref), (rk_hbm, rk_ref), (pos_hbm, pos_ref),
+             (len_hbm, len_ref), (x_hbm, packed_ref.at[:, pl.ds(0, D_Q)]), (l_hbm, packed_ref.at[:, pl.ds(D_Q, D_C)])]
+    copies = [pltpu.make_async_copy(src, dst, sems.at[i]) for i, (src, dst) in enumerate(moves)]
+    send_out = pltpu.make_async_copy(send_ref, send_hbm, out_sems.at[0])
+    packed_out = pltpu.make_async_copy(packed_ref, packed_hbm, out_sems.at[1])
+    for copy in copies:
+        copy.start()
+    for copy in copies[:3]:
+        copy.wait()
+    owner = owner_ref[...]
+    owner_col = column_of(owner)
+    same = owner_col == owner
+    before = iota((ROWS, ROWS), 0) < iota((ROWS, ROWS), 1)
+    rank = jnp.sum(jnp.where(same & before, 1, 0), axis=0, keepdims=True)
+    target = owner * (2 * MOST) + rank
+    target = jnp.concatenate([target, target + MOST], axis=1)
+    placing = iota((PEERS * 2 * MOST, 2 * ROWS), 0) == target
+    queries = jnp.concatenate([q_ref[:, :1536], q_ref[:, 1536:]], axis=0)
+    send_ref[:, :1536] = dot(placing.astype(BF16), queries).astype(BF16)
+    slot = slot_ref[...] + 1
+    slot = jnp.concatenate([slot, slot], axis=1)
+    slot_col = jnp.sum(jnp.where(placing, slot, 0), axis=1, keepdims=True)
+    send_ref[:, 1536:] = jnp.broadcast_to(slot_col.astype(F32), (PEERS * 2 * MOST, 128)).astype(BF16)
+    send_out.start()
+
+    for copy in copies[3:]:
+        copy.wait()
     pos = pos_ref[...]
     angle = pos.astype(F32) * frequencies()
     cos, sin = jnp.cos(angle), jnp.sin(angle)
@@ -64,6 +90,7 @@
     tail = jnp.where(place == 0, high, jnp.where(place == 1, low, 0.0))
     block = jnp.concatenate([first * cos - second * sin, first * sin + second * cos, tail], axis=0)
     packed_ref[:, D_Q + D_C:] = block.T.astype(BF16)
+    packed_out.start()
 
     length = len_ref[...]
     length_col = column_of(length)
@@ -73,39 +100,8 @@
     hit = rank == other
     plan_ref[...] = jnp.sum(
         jnp.concatenate([jnp.where(hit, this, 0), jnp.where(hit, length_col, 0)], axis=1), axis=0, keepdims=True)
-
-
-def place_kernel(q_hbm, owner_hbm, slot_hbm, send_hbm, q_ref, owner_ref, slot_ref, send_ref, sems, send_sems):
-    copies = [pltpu.make_async_copy(src, dst, sems.at[i]) for i, (src, dst) in enumerate(
-        ((owner_hbm, owner_ref), (slot_hbm, slot_ref), (q_hbm, q_ref)))]
-    for copy in copies:
-        copy.start()
-    for copy in copies[:2]:
-        copy.wait()
-    owner = owner_ref[...]
-    owner_col = column_of(owner)
-    same = owner_col == owner
-    before = iota((ROWS, ROWS), 0) < iota((ROWS, ROWS), 1)
-    rank = jnp.sum(jnp.where(same & before, 1, 0), axis=0, keepdims=True)
-    target = owner * (2 * MOST) + rank
-    target = jnp.concatenate([target, target + MOST], axis=1)
-    placing = iota((PEERS * 2 * MOST, 2 * ROWS), 0) == target
-    spread = placing.astype(BF16)
-    slot = slot_ref[...] + 1
-    slot = jnp.concatenate([slot, slot], axis=1)
-    slot_col = jnp.sum(jnp.where(placing, slot, 0), axis=1, keepdims=True)
-    parts = [(0, 512), (512, 512), (1024, SEND - 1024)]
-    sends = [pltpu.make_async_copy(send_ref.at[:, pl.ds(at, width)], send_hbm.at[:, pl.ds(at, width)], send_sems.at[i])
-             for i, (at, width) in enumerate(parts)]
-    send_ref[:, 1536:] = jnp.broadcast_to(slot_col.astype(F32), (PEERS * 2 * MOST, 128)).astype(BF16)
-    copies[2].wait()
-    for part, send in enumerate(sends):
-        lanes = slice(part * 512, (part + 1) * 512)
-        queries = jnp.concatenate([q_ref[:, lanes], q_ref[:, 1536 + part * 512:1536 + (part + 1) * 512]], axis=0)
-        send_ref[:, lanes] = dot(spread, queries).astype(BF16)
-        send.start()
-    for send in sends:
-        send.wait()
+    send_out.wait()
+    packed_out.wait()
 
 
 def split_pair(three):
@@ -302,14 +298,16 @@
 
     @pl.loop(0, GROUPS)
     def _(group):
-        for copy in fetch(group):
-            copy.wait()
+        for_queries, for_keys, for_values = fetch(group)
+        for_queries.wait()
         queries = dot(x_ref[:, :D_Q], wq_ref[group])
         for pair in range(GROUP // 2):
             even, odd, rotary = split_pair(queries[:, pair * 384:(pair + 1) * 384])
             qn_ref[group, :, pair * 256:pair * 256 + 128] = even.astype(BF16)
             qn_ref[group, :, pair * 256 + 128:pair * 256 + 256] = odd.astype(BF16)
             qr_ref[group, :, pair * 128:(pair + 1) * 128] = rotated(rotary, cos_ref[...], sin_ref[...])
+        for_keys.wait()
+        for_values.wait()
         latents = x_ref[:, D_Q:D_Q + D_C]
         k_ref[group] = dot(latents, wk_ref[group]).astype(BF16)
         v_ref[group] = dot(latents, wv_ref[group]).astype(BF16)
@@ -552,32 +550,29 @@
 def on_device(x, latents, rotary_keys, positions, wq, wk, wv, queries, owner, slot, cache, cache_rope, lengths):
     wq, wk, wv, cache, cache_rope = (in_hbm(array) for array in (wq, wk, wv, cache, cache_rope))
     owner_row, slot_row = owner.reshape(1, ROWS), slot.reshape(1, ROWS)
-    send = pl.pallas_call(
-        place_kernel,
-        in_specs=[anywhere()] * 3,
-        out_specs=anywhere(),
-        out_shape=pltpu.HBM((PEERS * 2 * MOST, SEND), BF16),
+    send, packed, plan = pl.pallas_call(
+        stage_kernel,
+        in_specs=[anywhere()] * 8,
+        out_specs=[anywhere(), anywhere(), vmem()],
+        out_shape=[pltpu.HBM((PEERS * 2 * MOST, SEND), BF16), pltpu.HBM((CHUNK, PACK), BF16),
+                   jax.ShapeDtypeStruct((1, 2 * SLOTS), jnp.int32)],
         scratch_shapes=[
             pltpu.VMEM((ROWS, HEADS * 192), BF16),
             pltpu.VMEM((1, ROWS), jnp.int32),
             pltpu.VMEM((1, ROWS), jnp.int32),
+            pltpu.VMEM((CHUNK, PACK), BF16),
+            pltpu.VMEM((64, CHUNK), BF16),
+            pltpu.VMEM((1, CHUNK), jnp.int32),
+            pltpu.VMEM((1, SLOTS), jnp.int32),
             pltpu.VMEM((PEERS * 2 * MOST, SEND), BF16),
-            pltpu.SemaphoreType.DMA((3,)),
-            pltpu.SemaphoreType.DMA((3,)),
+            pltpu.SemaphoreType.DMA((8,)),
+            pltpu.SemaphoreType.DMA((2,)),
         ],
-        compiler_params=params(16),
-        name="place",
-    )(in_hbm(queries), in_hbm(owner_row), in_hbm(slot_row))
+        compiler_params=params(60),
+        name="stage",
+    )(*(in_hbm(array) for array in (
+        queries, owner_row, slot_row, x, latents, rotary_keys, positions.reshape(1, CHUNK), lengths.reshape(1, SLOTS))))
     recv = lax.all_to_all(send, "req", 0, 0, tiled=True)
-
-    packed, plan = pl.pallas_call(
-        pack_kernel,
-        in_specs=[vmem()] * 5 + [anywhere()],
-        out_specs=[vmem()] * 2,
-        out_shape=[jax.ShapeDtypeStruct((CHUNK, PACK), BF16), jax.ShapeDtypeStruct((1, 2 * SLOTS), jnp.int32)],
-        compiler_params=params(60),
-        name="pack",
-    )(x, latents, rotary_keys, positions.reshape(1, CHUNK), lengths.reshape(1, SLOTS), in_hbm(send))
     right = lax.ppermute(packed, "head", [(i, (i + 3) % 4) for i in range(4)])
     left = lax.ppermute(packed, "head", [(i, (i + 1) % 4) for i in range(4)])
     far = lax.ppermute(packed, "head", [(i, (i + 2) % 4) for i in range(4)])

time: 62.7 us -> 63.1 us (level)
  waiting for transfers between devices: 0.01 us -> 1.9 us
  Pallas kernels: 36.8 us -> 35.7 us
    all_to_all x1, waiting for transfers between devices: 0.01 us -> 1.89 us  [on_device(): recv = lax.all_to_all(send, 'req', 0, 0, tiled=True)]
    pallas_call x2 -> x1, Pallas kernels: 4.39 us -> 3.3 us  [on_device(): pl.pallas_call(stage_kernel, in_specs=[anywhere()] * 8, out_specs=[anywhe...]
  transfers between devices with their start and end apart: 5 -> 5, of which waited for: 0 -> 1; matrix products, arithmetic and copies ran while one was open for 0% -> 0% of each run, Pallas kernels for 54% -> 50%
where the time goes in v6:
time: 63.1 us
  Pallas kernels  35.7 us (57%)
  starting transfers between devices  24.7 us (39%)
  waiting for transfers between devices  1.9 us (3%)
  between operations  0.73 us (1%)
    pallas_call x1, Pallas kernels, prefill(): pl.pallas_call(prefill_kernel, in_specs=[vmem()] * 3 + [anywhere()] * 9,...  14.1 us
    all_to_all x1, starting transfers between devices, on_device(): returned = lax.all_to_all(returned, 'req', 0, 0, tiled=True)  10.2 us
    all_to_all x1, starting transfers between devices, on_device(): recv = lax.all_to_all(send, 'req', 0, 0, tiled=True)  9.44 us
    pallas_call x1, Pallas kernels, on_device(): pl.pallas_call(decode_kernel, in_specs=[vmem()] + [anywhere()] * 6, out_s...  9.22 us
    pallas_call x1, Pallas kernels, project_own(): pl.pallas_call(own_kernel, in_specs=[anywhere()] * 4, out_specs=[anywhere...  7.91 us
    pallas_call x1, Pallas kernels, on_device(): pl.pallas_call(stage_kernel, in_specs=[anywhere()] * 8, out_specs=[anywhe...  3.3 us
    ppermute x1, starting transfers between devices, on_device(): far = lax.ppermute(packed, 'head', [(i, (i + 2) % 4) for i in range(4)])  2.62 us
    all_to_all x1, waiting for transfers between devices, on_device(): recv = lax.all_to_all(send, 'req', 0, 0, tiled=True)  1.89 us
  transfers between devices with their start and end apart: 5, of which 1 were waited for; matrix products, arithmetic and copies ran while one was open for 0% of the time, Pallas kernels for 50%

profile of v6, /device:TPU:1, one launch (start us, length us, event | category | flops | bytes accessed | tf_op | source)
XLA Modules:
  0.0 63.1 jit_solution(7048505909075171319)
XLA Ops:
  0.6 3.3 %stage.1 = (bf16[256,1664]{1,0:T(8,128)(2,1)}, bf16[128,2176]{1,0:T(8,128)(2,1)}, s32[1,128]{1,0:T(1,128)}) custom-call(bf16[64,3072]{1,0:T(8,128)(2,1)} %q_hbm.1, s32[1,64]{1,0:T(1,128)} %bitcast.10, s32[1,64]{1,0:T(1,128)} %bitcast.14, bf16[128,1536]{1,0:T(8,128)(2,1)} %x_hbm.1, bf16[128,512]{1,0:T(8,128)(2,1)} %l_hbm.1, bf16[64,128]{1,0:T(8,128)(2,1)} %rk_hbm.2, ...), custom_call_target="tpu_custom_call" | custom-call | tf_op jit(solution)/shard_map/stage/pallas_call | solution.py:553
  3.9 9.4 %all-to-all-start = ((bf16[32,8,1664]{2,1,0:T(8,128)(2,1)}), bf16[32,8,1664]{2,1,0:T(8,128)(2,1)S(1)}, u32[]{:S(2)}, u32[]{:S(2)}) async-start(bf16[32,8,1664]{2,1,0:T(8,128)(2,1)} %bitcast.13), calls=%async_computation | async-start | bytes 1703936 | tf_op jit(solution)/shard_map/all_to_all | solution.py:575
  13.4 1.4 %collective-permute-start.2 = (bf16[128,2176]{1,0:T(8,128)(2,1)}, bf16[128,2176]{1,0:T(8,128)(2,1)S(1)}, u32[]{:S(2)}, u32[]{:S(2)}) collective-permute-start(bf16[128,2176]{1,0:T(8,128)(2,1)} %get-tuple-element.9.packed_hbm.own_hbm), channel_id=1, source_target_pairs={{0,1},{1,2},{2,3},{3,0},{4,5},{5,6},{6,7},{7,4},{8,9},{9,10},{10,1... | collective-permute-start | bytes 1671176 | tf_op jit(solution)/shard_map/ppermute | solution.py:577
  14.8 2.6 %collective-permute-start.1 = (bf16[128,2176]{1,0:T(8,128)(2,1)}, bf16[128,2176]{1,0:T(8,128)(2,1)S(1)}, u32[]{:S(2)}, u32[]{:S(2)}) collective-permute-start(bf16[128,2176]{1,0:T(8,128)(2,1)} %get-tuple-element.9.packed_hbm.own_hbm), channel_id=1, source_target_pairs={{0,2},{1,3},{2,0},{3,1},{4,6},{5,7},{6,4},{7,5},{8,10},{9,11},{10,... | collective-permute-start | bytes 1671176 | tf_op jit(solution)/shard_map/ppermute | solution.py:578
  17.4 1.1 %collective-permute-start = (bf16[128,2176]{1,0:T(8,128)(2,1)}, bf16[128,2176]{1,0:T(8,128)(2,1)S(1)}, u32[]{:S(2)}, u32[]{:S(2)}) collective-permute-start(bf16[128,2176]{1,0:T(8,128)(2,1)} %get-tuple-element.9.packed_hbm.own_hbm), channel_id=1, source_target_pairs={{0,3},{1,0},{2,1},{3,2},{4,7},{5,4},{6,5},{7,6},{8,11},{9,8},{10,9... | collective-permute-start | bytes 1671176 | tf_op jit(solution)/shard_map/ppermute | solution.py:576
  18.4 7.9 %own.1 = (bf16[4,128,512]{2,1,0:T(8,128)(2,1)}, bf16[4,128,256]{2,1,0:T(8,128)(2,1)}, bf16[4,128,512]{2,1,0:T(8,128)(2,1)}, bf16[4,128,512]{2,1,0:T(8,128)(2,1)}) custom-call(bf16[128,2176]{1,0:T(8,128)(2,1)} %get-tuple-element.9.packed_hbm.own_hbm, bf16[1536,3072]{1,0:T(8,128)(2,1)} %wq_hbm.3, bf16[512,2048]{1,0:T(8,128)(2,1)} %wk_hbm.3, ...), custom_call_target="tpu_custom_call" | custom-call | tf_op jit(solution)/shard_map/own/pallas_call | solution.py:510
  26.4 1.9 %all-to-all-done = bf16[32,8,1664]{2,1,0:T(8,128)(2,1)S(1)} async-done(((bf16[32,8,1664]{2,1,0:T(8,128)(2,1)}), bf16[32,8,1664]{2,1,0:T(8,128)(2,1)S(1)}, u32[]{:S(2)}, u32[]{:S(2)}) %all-to-all-start) | async-done | bytes 852000 | tf_op jit(solution)/shard_map/all_to_all | solution.py:575
  28.2 9.2 %decode.1.after_ref = bf16[256,1024]{1,0:T(8,128)(2,1)} custom-call(bf16[256,1664]{1,0:T(8,128)(2,1)S(1)} %bitcast.8, bf16[512,2048]{1,0:T(8,128)(2,1)} %wk_hbm.3, bf16[64,256,512]{2,1,0:T(8,128)(2,1)} %lat_hbm.1, bf16[64,64,256]{2,1,0:T(8,128)(2,1)} %rk_hbm.3, bf16[512,2048]{1,0:T(8,128)(2,1)} %wv_hbm.3, s32[1,128]{1,0:T(1,128)} %get-tuple-element.15.plan_hbm, ...), custom_call_target="tpu_custom_call" | custom-call | tf_op jit(solution)/shard_map/decode/pallas_call | solution.py:581
  37.5 10.2 %all-to-all-start.1 = ((bf16[32,8,1024]{2,1,0:T(8,128)(2,1)}), bf16[32,8,1024]{2,1,0:T(8,128)(2,1)S(1)}, u32[]{:S(2)}, u32[]{:S(2)}) async-start(bf16[32,8,1024]{2,1,0:T(8,128)(2,1)} %bitcast.12), calls=%async_computation.1 | async-start | bytes 1048576 | tf_op jit(solution)/shard_map/all_to_all | solution.py:606
  47.7 0.0 collective-permute-done.2.left_ref
  47.7 0.0 collective-permute-done.1.far_ref
  47.7 0.0 collective-permute-done.right_ref
  47.8 0.0 copy-start
  47.8 14.1 %prefill.1 = bf16[512,2048]{1,0:T(8,128)(2,1)} custom-call(bf16[128,2176]{1,0:T(8,128)(2,1)S(1)} %collective-permute-done.right_ref, bf16[128,2176]{1,0:T(8,128)(2,1)S(1)} %collective-permute-done.1.far_ref, bf16[128,2176]{1,0:T(8,128)(2,1)S(1)} %collective-permute-done.2.left_ref, bf16[128,2176]{1,0:T(8,128)(2,1)} %get-tuple-element.9.packed_hbm.own_hbm, ...), custom_call_target="tpu_custom_call" | custom-call | tf_op jit(solution)/shard_map/prefill/pallas_call | solution.py:529
  61.9 0.0 all-to-all-done.1
  61.9 0.0 copy-done
  61.9 1.1 %unplace.1 = bf16[64,2048]{1,0:T(8,128)(2,1)} custom-call(bf16[256,1024]{1,0:T(8,128)(2,1)S(1)} %bitcast.9, s32[1,64]{1,0:T(1,128)S(1)} %bitcast.11), custom_call_target="tpu_custom_call" | custom-call | tf_op jit(solution)/shard_map/unplace/pallas_call | solution.py:608
Async XLA Ops:
  3.9 24.3 %all-to-all-start = ((bf16[32,8,1664]{2,1,0:T(8,128)(2,1)}), bf16[32,8,1664]{2,1,0:T(8,128)(2,1)S(1)}, u32[]{:S(2)}, u32[]{:S(2)}) async-start(bf16[32,8,1664]{2,1,0:T(8,128)(2,1)} %bitcast.13), calls=%async_computation | async-start | bytes 1703936 | tf_op jit(solution)/shard_map/all_to_all | solution.py:575
  13.4 34.3 %collective-permute-start.2 = (bf16[128,2176]{1,0:T(8,128)(2,1)}, bf16[128,2176]{1,0:T(8,128)(2,1)S(1)}, u32[]{:S(2)}, u32[]{:S(2)}) collective-permute-start(bf16[128,2176]{1,0:T(8,128)(2,1)} %get-tuple-element.9.packed_hbm.own_hbm), channel_id=1, source_target_pairs={{0,1},{1,2},{2,3},{3,0},{4,5},{5,6},{6,7},{7,4},{8,9},{9,10},{10,1... | collective-permute-start | bytes 1671176 | tf_op jit(solution)/shard_map/ppermute | solution.py:577
  14.8 33.0 %collective-permute-start.1 = (bf16[128,2176]{1,0:T(8,128)(2,1)}, bf16[128,2176]{1,0:T(8,128)(2,1)S(1)}, u32[]{:S(2)}, u32[]{:S(2)}) collective-permute-start(bf16[128,2176]{1,0:T(8,128)(2,1)} %get-tuple-element.9.packed_hbm.own_hbm), channel_id=1, source_target_pairs={{0,2},{1,3},{2,0},{3,1},{4,6},{5,7},{6,4},{7,5},{8,10},{9,11},{10,... | collective-permute-start | bytes 1671176 | tf_op jit(solution)/shard_map/ppermute | solution.py:578
  17.4 30.4 %collective-permute-start = (bf16[128,2176]{1,0:T(8,128)(2,1)}, bf16[128,2176]{1,0:T(8,128)(2,1)S(1)}, u32[]{:S(2)}, u32[]{:S(2)}) collective-permute-start(bf16[128,2176]{1,0:T(8,128)(2,1)} %get-tuple-element.9.packed_hbm.own_hbm), channel_id=1, source_target_pairs={{0,3},{1,0},{2,1},{3,2},{4,7},{5,4},{6,5},{7,6},{8,11},{9,8},{10,9... | collective-permute-start | bytes 1671176 | tf_op jit(solution)/shard_map/ppermute | solution.py:576
  37.5 24.4 %all-to-all-start.1 = ((bf16[32,8,1024]{2,1,0:T(8,128)(2,1)}), bf16[32,8,1024]{2,1,0:T(8,128)(2,1)S(1)}, u32[]{:S(2)}, u32[]{:S(2)}) async-start(bf16[32,8,1024]{2,1,0:T(8,128)(2,1)} %bitcast.12), calls=%async_computation.1 | async-start | bytes 1048576 | tf_op jit(solution)/shard_map/all_to_all | solution.py:606
  47.8 14.2 %copy-start = (s32[64]{0:T(128)S(1)}, s32[64]{0:T(128)}, u32[]{:S(2)}) copy-start(s32[64]{0:T(128)} %param.21) | copy-start | bytes 772

commit v7 on v6

--- a/solution.py
+++ b/solution.py
@@ -52,14 +52,14 @@
 
 def stage_kernel(q_hbm, owner_hbm, slot_hbm, x_hbm, l_hbm, rk_hbm, pos_hbm, len_hbm, send_hbm, packed_hbm, plan_ref,
                  q_ref, owner_ref, slot_ref, packed_ref, rk_ref, pos_ref, len_ref, send_ref, sems, out_sems):
-    moves = [(owner_hbm, owner_ref), (slot_hbm, slot_ref), (q_hbm, q_ref), (rk_hbm, rk_ref), (pos_hbm, pos_ref),
-             (len_hbm, len_ref), (x_hbm, packed_ref.at[:, pl.ds(0, D_Q)]), (l_hbm, packed_ref.at[:, pl.ds(D_Q, D_C)])]
+    moves = [(owner_hbm, owner_ref), (slot_hbm, slot_ref), (pos_hbm, pos_ref), (rk_hbm, rk_ref), (q_hbm, q_ref),
+             (x_hbm, packed_ref.at[:, pl.ds(0, D_Q)]), (l_hbm, packed_ref.at[:, pl.ds(D_Q, D_C)]), (len_hbm, len_ref)]
     copies = [pltpu.make_async_copy(src, dst, sems.at[i]) for i, (src, dst) in enumerate(moves)]
     send_out = pltpu.make_async_copy(send_ref, send_hbm, out_sems.at[0])
     packed_out = pltpu.make_async_copy(packed_ref, packed_hbm, out_sems.at[1])
     for copy in copies:
         copy.start()
-    for copy in copies[:3]:
+    for copy in copies[:4]:
         copy.wait()
     owner = owner_ref[...]
     owner_col = column_of(owner)
@@ -69,16 +69,10 @@
     target = owner * (2 * MOST) + rank
     target = jnp.concatenate([target, target + MOST], axis=1)
     placing = iota((PEERS * 2 * MOST, 2 * ROWS), 0) == target
-    queries = jnp.concatenate([q_ref[:, :1536], q_ref[:, 1536:]], axis=0)
-    send_ref[:, :1536] = dot(placing.astype(BF16), queries).astype(BF16)
     slot = slot_ref[...] + 1
     slot = jnp.concatenate([slot, slot], axis=1)
     slot_col = jnp.sum(jnp.where(placing, slot, 0), axis=1, keepdims=True)
     send_ref[:, 1536:] = jnp.broadcast_to(slot_col.astype(F32), (PEERS * 2 * MOST, 128)).astype(BF16)
-    send_out.start()
-
-    for copy in copies[3:]:
-        copy.wait()
     pos = pos_ref[...]
     angle = pos.astype(F32) * frequencies()
     cos, sin = jnp.cos(angle), jnp.sin(angle)
@@ -90,6 +84,12 @@
     tail = jnp.where(place == 0, high, jnp.where(place == 1, low, 0.0))
     block = jnp.concatenate([first * cos - second * sin, first * sin + second * cos, tail], axis=0)
     packed_ref[:, D_Q + D_C:] = block.T.astype(BF16)
+    copies[4].wait()
+    queries = jnp.concatenate([q_ref[:, :1536], q_ref[:, 1536:]], axis=0)
+    send_ref[:, :1536] = dot(placing.astype(BF16), queries).astype(BF16)
+    send_out.start()
+    for copy in copies[5:]:
+        copy.wait()
     packed_out.start()
 
     length = len_ref[...]
@@ -116,35 +116,46 @@
 WIDE = TOGETHER * HEADS
 SECTION = 16
 SECTIONS = SLOTS // SECTION
-WIDTHS = (64, 128, 192, 256)
+WIDTHS = ((64, 64), (64, 128), (128, 128), (128, 192), (192, 192), (192, 256), (256, 256))
 
 
 def decode_kernel(recv_ref, kup_hbm, lat_hbm, rk_hbm, vup_hbm, plan_hbm, after_ref, out_hbm,
                   kup_ref, rk_ref, vup_ref, plan_row_ref, plan_ref, out_ref, lat_ref, lq_ref, qr_ref, lo_ref, sems, lat_sems, out_sem):
     rows = PEERS * 2 * MOST
-    plan_copy, kup_copy, rk_copy, vup_copy, row_copy = [
+    plan_copy, rk_copy, vup_copy, row_copy = [
         pltpu.make_async_copy(src, dst, sems.at[i]) for i, (src, dst) in enumerate(
-            ((plan_hbm, plan_ref), (kup_hbm, kup_ref.at[:, pl.ds(0, HEADS * D_NOPE)]), (rk_hbm, rk_ref), (vup_hbm, vup_ref.at[:, pl.ds(0, HEADS * D_V)]), (plan_hbm, plan_row_ref)))]
-
-    def of_width(section, width):
-        longest = plan_ref[0, SLOTS + section * SECTION + SECTION - 1]
-        return (longest <= width) & (longest > width - 64)
-
-    def fetch(section, width, i):
+            ((plan_hbm, plan_ref), (rk_hbm, rk_ref), (vup_hbm, vup_ref.at[:, pl.ds(0, HEADS * D_V)]), (plan_hbm, plan_row_ref)))]
+    kup_copies = [pltpu.make_async_copy(kup_hbm.at[:, pl.ds(side * 1024, 1024)], kup_ref.at[:, pl.ds(side * 1024, 1024)],
+                                        sems.at[4 + side]) for side in range(2)]
+
+    def of_widths(section, widths):
+        first, last = widths
+        at = SLOTS + section * SECTION
+        longest = plan_ref[0, at + SECTION - 1]
+        fits = (longest <= last) & (longest > last - 64)
+        if last > 64:
+            short = plan_ref[0, at + TOGETHER - 1] <= last - 64
+            fits = fits & (short if first < last else jnp.logical_not(short))
+        return fits
+
+    def fetch(section, widths, i):
         place = section * SECTION + i
+        rows = pl.ds(0, widths[i // TOGETHER])
         return pltpu.make_async_copy(
-            lat_hbm.at[plan_ref[0, place], pl.ds(0, width)], lat_ref.at[place, pl.ds(0, width), pl.ds(0, D_C)], lat_sems.at[section])
+            lat_hbm.at[plan_ref[0, place], rows], lat_ref.at[place, rows, pl.ds(0, D_C)],
+            lat_sems.at[section, i // TOGETHER])
 
     def start(section):
-        for width in WIDTHS:
-            @pl.when(of_width(section, width))
+        for widths in WIDTHS:
+            @pl.when(of_widths(section, widths))
             def _():
                 for i in range(SECTION):
-                    fetch(section, width, i).start()
+                    fetch(section, widths, i).start()
 
     plan_copy.start()
     row_copy.start()
-    kup_copy.start()
+    for copy in kup_copies:
+        copy.start()
     plan_copy.wait()
     start(0)
     rk_copy.start()
@@ -162,9 +173,8 @@
     spreads = [jnp.concatenate([jnp.where(hit, 1.0, 0.0), jnp.zeros((rows, 64), F32)], axis=1).T[:SLOTS].astype(BF16)
                for hit in (first, second)]
     queries = [dot(spread, recv_ref[:, :1536]) for spread in spreads]
-    kup_copy.wait()
-    start(1)
     for side in range(2):
+        kup_copies[side].wait()
         for pair in range(4):
             head = side * 8 + pair * 2
             even, odd, rotary = split_pair(queries[side][:, pair * 384:(pair + 1) * 384])
@@ -175,14 +185,17 @@
             turned = pltpu.roll(rotary, 64, 1)
             qr_ref[head] = jnp.where(low_lane, rotary, turned)
             qr_ref[head + 1] = jnp.where(low_lane, turned, rotary)
+    start(1)
     rk_copy.wait()
     start(2)
 
-    def attend(section, width):
-        whole_section = pl.ds(pl.multiple_of(section * SECTION, SECTION), SECTION)
-        pltpu.make_async_copy(
-            lat_hbm.at[whole_section, pl.ds(0, width)], lat_ref.at[whole_section, pl.ds(0, width), pl.ds(0, D_C)],
-            lat_sems.at[section]).wait()
+    def attend(section, widths):
+        for group, width in enumerate(widths):
+            places = pl.ds(pl.multiple_of(section * SECTION + group * TOGETHER, TOGETHER), TOGETHER)
+            pltpu.make_async_copy(
+                lat_hbm.at[places, pl.ds(0, width)], lat_ref.at[places, pl.ds(0, width), pl.ds(0, D_C)],
+                lat_sems.at[section, group]).wait()
+
         row, lane = iota((WIDE, WIDE), 0), iota((WIDE, WIDE), 1)
         by_place = jnp.where(lane == (row & 15) * TOGETHER + (row >> 4), 1.0, 0.0).astype(BF16)
         by_head = jnp.where(row == (lane & 15) * TOGETHER + (lane >> 4), 1.0, 0.0).astype(BF16)
@@ -194,7 +207,7 @@
             rotary = qr_ref[:, pl.ds(start, TOGETHER), :].reshape(WIDE, 128).astype(BF16)
             queries.append((dot(by_place, latent).astype(BF16), dot(by_place, rotary).astype(BF16)))
         scores = []
-        for start, (latent, rotary) in zip(starts, queries):
+        for start, width, (latent, rotary) in zip(starts, widths, queries):
             score = []
             length = jnp.full((WIDE, 1), plan_ref[0, SLOTS + start], jnp.int32)
             for i in range(TOGETHER):
@@ -204,7 +217,7 @@
                 length = jnp.where(row_place == i, plan_ref[0, SLOTS + start + i], length)
             score = jnp.concatenate(score, axis=0)
             scores.append(jnp.where(iota((WIDE, width), 1) < length, score * SCALE, MASKED))
-        for start, score in zip(starts, scores):
+        for start, width, score in zip(starts, widths, scores):
             raised = jnp.exp(score - jnp.max(score, axis=1, keepdims=True))
             weights = (raised * (1.0 / jnp.sum(raised, axis=1, keepdims=True))).astype(BF16)
             total = jnp.concatenate(
@@ -219,10 +232,10 @@
             start(SECTIONS - 1)
             vup_copy.start()
 
-        for width in WIDTHS:
-            @pl.when(of_width(section, width))
+        for widths in WIDTHS:
+            @pl.when(of_widths(section, widths))
             def _():
-                attend(section, width)
+                attend(section, widths)
 
     vup_copy.wait()
     first, second = place_onehot()
@@ -246,9 +259,10 @@
     rank = jnp.sum(jnp.where((owner_col == owner) & before, 1, 0), axis=1, keepdims=True)
     target = owner_col * (2 * MOST) + rank
     lane = iota((ROWS, PEERS * 2 * MOST), 1)
-    for side in range(2):
-        spread = jnp.where(lane == target + side * MOST, 1.0, 0.0).astype(BF16)
-        out_ref[:, side * RET:(side + 1) * RET] = dot(spread, ret_ref[...]).astype(BF16)
+    spread = jnp.concatenate([jnp.where(lane == target + side * MOST, 1.0, 0.0) for side in range(2)], axis=0)
+    both = dot(spread.astype(BF16), ret_ref[...]).astype(BF16)
+    out_ref[:, :RET] = both[:ROWS]
+    out_ref[:, RET:] = both[ROWS:]
 
 
 GROUP = 4
@@ -594,8 +608,8 @@
             pltpu.VMEM((HEADS, SLOTS, D_C), F32),
             pltpu.VMEM((HEADS, SLOTS, 128), F32),
             pltpu.VMEM((HEADS, SLOTS, D_C), F32),
-            pltpu.SemaphoreType.DMA((5,)),
-            pltpu.SemaphoreType.DMA((SECTIONS,)),
+            pltpu.SemaphoreType.DMA((6,)),
+            pltpu.SemaphoreType.DMA((SECTIONS, SECTION // TOGETHER)),
             pltpu.SemaphoreType.DMA,
         ],
         compiler_params=params(44),

time: 63.1 us -> 61.6 us (0.976)
  starting transfers between devices: 24.7 us -> 21.6 us
  Pallas kernels: 35.7 us -> 36.7 us
    all_to_all x1, starting transfers between devices: 10.2 us -> 7.12 us  [on_device(): returned = lax.all_to_all(returned, 'req', 0, 0, tiled=True)]
    pallas_call x1, Pallas kernels: 9.22 us -> 10.4 us  [on_device(): pl.pallas_call(decode_kernel, in_specs=[vmem()] + [anywhere()] * 6, out_s...]
  transfers between devices with their start and end apart: 5 -> 5, of which waited for: 1 -> 1; matrix products, arithmetic and copies ran while one was open for 0% -> 0% of each run, Pallas kernels for 50% -> 53%
where the time goes in v7:
time: 61.6 us; the launch traced here: 61 us
  Pallas kernels  36.7 us (60%)
  starting transfers between devices  21.6 us (35%)
  waiting for transfers between devices  1.89 us (3%)
  between operations  0.73 us (1%)
    pallas_call x1, Pallas kernels, prefill(): pl.pallas_call(prefill_kernel, in_specs=[vmem()] * 3 + [anywhere()] * 9,...  14.1 us
    pallas_call x1, Pallas kernels, on_device(): pl.pallas_call(decode_kernel, in_specs=[vmem()] + [anywhere()] * 6, out_s...  10.4 us
    all_to_all x1, starting transfers between devices, on_device(): recv = lax.all_to_all(send, 'req', 0, 0, tiled=True)  9.44 us
    pallas_call x1, Pallas kernels, project_own(): pl.pallas_call(own_kernel, in_specs=[anywhere()] * 4, out_specs=[anywhere...  7.91 us
    all_to_all x1, starting transfers between devices, on_device(): returned = lax.all_to_all(returned, 'req', 0, 0, tiled=True)  7.12 us
    pallas_call x1, Pallas kernels, on_device(): pl.pallas_call(stage_kernel, in_specs=[anywhere()] * 8, out_specs=[anywhe...  3.22 us
    ppermute x1, starting transfers between devices, on_device(): far = lax.ppermute(packed, 'head', [(i, (i + 2) % 4) for i in range(4)])  2.62 us
    all_to_all x1, waiting for transfers between devices, on_device(): recv = lax.all_to_all(send, 'req', 0, 0, tiled=True)  1.88 us
  transfers between devices with their start and end apart: 5, of which 1 were waited for; matrix products, arithmetic and copies ran while one was open for 0% of the time, Pallas kernels for 53%

profile of v7, /device:TPU:1, one launch (start us, length us, event | category | flops | bytes accessed | tf_op | source)
XLA Modules:
  0.0 61.0 jit_solution(10203326123087721524)
XLA Ops:
  0.6 3.2 %stage.1 = (bf16[256,1664]{1,0:T(8,128)(2,1)}, bf16[128,2176]{1,0:T(8,128)(2,1)}, s32[1,128]{1,0:T(1,128)}) custom-call(bf16[64,3072]{1,0:T(8,128)(2,1)} %q_hbm.1, s32[1,64]{1,0:T(1,128)} %bitcast.10, s32[1,64]{1,0:T(1,128)} %bitcast.14, bf16[128,1536]{1,0:T(8,128)(2,1)} %x_hbm.1, bf16[128,512]{1,0:T(8,128)(2,1)} %l_hbm.1, bf16[64,128]{1,0:T(8,128)(2,1)} %rk_hbm.2, ...), custom_call_target="tpu_custom_call" | custom-call | tf_op jit(solution)/shard_map/stage/pallas_call | solution.py:567
  3.9 9.4 %all-to-all-start = ((bf16[32,8,1664]{2,1,0:T(8,128)(2,1)}), bf16[32,8,1664]{2,1,0:T(8,128)(2,1)S(1)}, u32[]{:S(2)}, u32[]{:S(2)}) async-start(bf16[32,8,1664]{2,1,0:T(8,128)(2,1)} %bitcast.13), calls=%async_computation | async-start | bytes 1703936 | tf_op jit(solution)/shard_map/all_to_all | solution.py:589
  13.3 1.4 %collective-permute-start.2 = (bf16[128,2176]{1,0:T(8,128)(2,1)}, bf16[128,2176]{1,0:T(8,128)(2,1)S(1)}, u32[]{:S(2)}, u32[]{:S(2)}) collective-permute-start(bf16[128,2176]{1,0:T(8,128)(2,1)} %get-tuple-element.9.packed_hbm.own_hbm), channel_id=1, source_target_pairs={{0,1},{1,2},{2,3},{3,0},{4,5},{5,6},{6,7},{7,4},{8,9},{9,10},{10,1... | collective-permute-start | bytes 1671176 | tf_op jit(solution)/shard_map/ppermute | solution.py:591
  14.7 2.6 %collective-permute-start.1 = (bf16[128,2176]{1,0:T(8,128)(2,1)}, bf16[128,2176]{1,0:T(8,128)(2,1)S(1)}, u32[]{:S(2)}, u32[]{:S(2)}) collective-permute-start(bf16[128,2176]{1,0:T(8,128)(2,1)} %get-tuple-element.9.packed_hbm.own_hbm), channel_id=1, source_target_pairs={{0,2},{1,3},{2,0},{3,1},{4,6},{5,7},{6,4},{7,5},{8,10},{9,11},{10,... | collective-permute-start | bytes 1671176 | tf_op jit(solution)/shard_map/ppermute | solution.py:592
  17.3 1.1 %collective-permute-start = (bf16[128,2176]{1,0:T(8,128)(2,1)}, bf16[128,2176]{1,0:T(8,128)(2,1)S(1)}, u32[]{:S(2)}, u32[]{:S(2)}) collective-permute-start(bf16[128,2176]{1,0:T(8,128)(2,1)} %get-tuple-element.9.packed_hbm.own_hbm), channel_id=1, source_target_pairs={{0,3},{1,0},{2,1},{3,2},{4,7},{5,4},{6,5},{7,6},{8,11},{9,8},{10,9... | collective-permute-start | bytes 1671176 | tf_op jit(solution)/shard_map/ppermute | solution.py:590
  18.4 7.9 %own.1 = (bf16[4,128,512]{2,1,0:T(8,128)(2,1)}, bf16[4,128,256]{2,1,0:T(8,128)(2,1)}, bf16[4,128,512]{2,1,0:T(8,128)(2,1)}, bf16[4,128,512]{2,1,0:T(8,128)(2,1)}) custom-call(bf16[128,2176]{1,0:T(8,128)(2,1)} %get-tuple-element.9.packed_hbm.own_hbm, bf16[1536,3072]{1,0:T(8,128)(2,1)} %wq_hbm.3, bf16[512,2048]{1,0:T(8,128)(2,1)} %wk_hbm.3, ...), custom_call_target="tpu_custom_call" | custom-call | tf_op jit(solution)/shard_map/own/pallas_call | solution.py:524
  26.3 1.9 %all-to-all-done = bf16[32,8,1664]{2,1,0:T(8,128)(2,1)S(1)} async-done(((bf16[32,8,1664]{2,1,0:T(8,128)(2,1)}), bf16[32,8,1664]{2,1,0:T(8,128)(2,1)S(1)}, u32[]{:S(2)}, u32[]{:S(2)}) %all-to-all-start) | async-done | bytes 852000 | tf_op jit(solution)/shard_map/all_to_all | solution.py:589
  28.2 10.4 %decode.1.after_ref = bf16[256,1024]{1,0:T(8,128)(2,1)} custom-call(bf16[256,1664]{1,0:T(8,128)(2,1)S(1)} %bitcast.8, bf16[512,2048]{1,0:T(8,128)(2,1)} %wk_hbm.3, bf16[64,256,512]{2,1,0:T(8,128)(2,1)} %lat_hbm.1, bf16[64,64,256]{2,1,0:T(8,128)(2,1)} %rk_hbm.3, bf16[512,2048]{1,0:T(8,128)(2,1)} %wv_hbm.3, s32[1,128]{1,0:T(1,128)} %get-tuple-element.15.plan_hbm, ...), custom_call_target="tpu_custom_call" | custom-call | tf_op jit(solution)/shard_map/decode/pallas_call | solution.py:595
  38.6 7.1 %all-to-all-start.1 = ((bf16[32,8,1024]{2,1,0:T(8,128)(2,1)}), bf16[32,8,1024]{2,1,0:T(8,128)(2,1)S(1)}, u32[]{:S(2)}, u32[]{:S(2)}) async-start(bf16[32,8,1024]{2,1,0:T(8,128)(2,1)} %bitcast.12), calls=%async_computation.1 | async-start | bytes 1048576 | tf_op jit(solution)/shard_map/all_to_all | solution.py:620
  45.7 0.0 collective-permute-done.2.left_ref
  45.7 0.0 collective-permute-done.1.far_ref
  45.7 0.0 collective-permute-done.right_ref
  45.7 0.0 copy-start
  45.7 14.1 %prefill.1 = bf16[512,2048]{1,0:T(8,128)(2,1)} custom-call(bf16[128,2176]{1,0:T(8,128)(2,1)S(1)} %collective-permute-done.right_ref, bf16[128,2176]{1,0:T(8,128)(2,1)S(1)} %collective-permute-done.1.far_ref, bf16[128,2176]{1,0:T(8,128)(2,1)S(1)} %collective-permute-done.2.left_ref, bf16[128,2176]{1,0:T(8,128)(2,1)} %get-tuple-element.9.packed_hbm.own_hbm, ...), custom_call_target="tpu_custom_call" | custom-call | tf_op jit(solution)/shard_map/prefill/pallas_call | solution.py:543
  59.9 0.0 all-to-all-done.1
  59.9 0.0 copy-done
  59.9 1.1 %unplace.1 = bf16[64,2048]{1,0:T(8,128)(2,1)} custom-call(bf16[256,1024]{1,0:T(8,128)(2,1)S(1)} %bitcast.9, s32[1,64]{1,0:T(1,128)S(1)} %bitcast.11), custom_call_target="tpu_custom_call" | custom-call | tf_op jit(solution)/shard_map/unplace/pallas_call | solution.py:622
Async XLA Ops:
  3.9 24.3 %all-to-all-start = ((bf16[32,8,1664]{2,1,0:T(8,128)(2,1)}), bf16[32,8,1664]{2,1,0:T(8,128)(2,1)S(1)}, u32[]{:S(2)}, u32[]{:S(2)}) async-start(bf16[32,8,1664]{2,1,0:T(8,128)(2,1)} %bitcast.13), calls=%async_computation | async-start | bytes 1703936 | tf_op jit(solution)/shard_map/all_to_all | solution.py:589
  13.3 32.4 %collective-permute-start.2 = (bf16[128,2176]{1,0:T(8,128)(2,1)}, bf16[128,2176]{1,0:T(8,128)(2,1)S(1)}, u32[]{:S(2)}, u32[]{:S(2)}) collective-permute-start(bf16[128,2176]{1,0:T(8,128)(2,1)} %get-tuple-element.9.packed_hbm.own_hbm), channel_id=1, source_target_pairs={{0,1},{1,2},{2,3},{3,0},{4,5},{5,6},{6,7},{7,4},{8,9},{9,10},{10,1... | collective-permute-start | bytes 1671176 | tf_op jit(solution)/shard_map/ppermute | solution.py:591
  14.7 31.0 %collective-permute-start.1 = (bf16[128,2176]{1,0:T(8,128)(2,1)}, bf16[128,2176]{1,0:T(8,128)(2,1)S(1)}, u32[]{:S(2)}, u32[]{:S(2)}) collective-permute-start(bf16[128,2176]{1,0:T(8,128)(2,1)} %get-tuple-element.9.packed_hbm.own_hbm), channel_id=1, source_target_pairs={{0,2},{1,3},{2,0},{3,1},{4,6},{5,7},{6,4},{7,5},{8,10},{9,11},{10,... | collective-permute-start | bytes 1671176 | tf_op jit(solution)/shard_map/ppermute | solution.py:592
  17.3 28.4 %collective-permute-start = (bf16[128,2176]{1,0:T(8,128)(2,1)}, bf16[128,2176]{1,0:T(8,128)(2,1)S(1)}, u32[]{:S(2)}, u32[]{:S(2)}) collective-permute-start(bf16[128,2176]{1,0:T(8,128)(2,1)} %get-tuple-element.9.packed_hbm.own_hbm), channel_id=1, source_target_pairs={{0,3},{1,0},{2,1},{3,2},{4,7},{5,4},{6,5},{7,6},{8,11},{9,8},{10,9... | collective-permute-start | bytes 1671176 | tf_op jit(solution)/shard_map/ppermute | solution.py:590
  38.6 21.3 %all-to-all-start.1 = ((bf16[32,8,1024]{2,1,0:T(8,128)(2,1)}), bf16[32,8,1024]{2,1,0:T(8,128)(2,1)S(1)}, u32[]{:S(2)}, u32[]{:S(2)}) async-start(bf16[32,8,1024]{2,1,0:T(8,128)(2,1)} %bitcast.12), calls=%async_computation.1 | async-start | bytes 1048576 | tf_op jit(solution)/shard_map/all_to_all | solution.py:620
  45.7 14.2 %copy-start = (s32[64]{0:T(128)S(1)}, s32[64]{0:T(128)}, u32[]{:S(2)}) copy-start(s32[64]{0:T(128)} %param.21) | copy-start | bytes 772
